TPU v7x, 32 devices: a whole 2x2x4 slice. The times are simulated.
32 devices in a mesh: dp: 8 (over y, x, core), tensor: 4 (over z).
Axes of the slice: x: 2, y: 2, z: 4, core: 2. Of those that a mesh axis runs over, the one named last changes fastest.
Arguments:
- inputs: bfloat16 [16, 544, 1536], P('dp', 'tensor'), may hold values from -6 to 6
- context: bfloat16 [16, 130, 768], P('dp'), may hold values from -6 to 6
- lengths: int32 [16], P('dp'), may hold values from 257 to 513, as said below
- cotangent: bfloat16 [16, 544, 1536], P('dp', 'tensor'), may hold values from -6 to 6
- self_qkv: float32 [3, 1536, 1536], P(None, 'dp', 'tensor'), may hold values from -0.15625 to 0.15625
- self_out: float32 [1536, 1536], P('tensor', 'dp'), may hold values from -1 to 1
- cross_query: float32 [1536, 1536], P('dp', 'tensor'), may hold values from -0.15625 to 0.15625
- cross_context: float32 [2, 768, 1536], P(None, 'dp', 'tensor'), may hold values from -0.21875 to 0.21875
- cross_out: float32 [1536, 1536], P('tensor', 'dp'), may hold values from -1 to 1
- gate_up: float32 [2, 1536, 6144], P(None, 'dp', 'tensor'), may hold values from -0.15625 to 0.15625
- down_proj: float32 [6144, 1536], P('tensor', 'dp'), may hold values from -0.078125 to 0.078125
- norm_gains: float32 [3, 1536], replicated, may hold values from 0.5 to 1.5
Outputs:
- output: bfloat16 [16, 544, 1536], P('dp', 'tensor')
- grad_inputs: float32 [16, 544, 1536], P('dp', 'tensor')
- grad_context: float32 [16, 130, 768], P('dp')
- grad_self_qkv: float32 [3, 1536, 1536], P(None, 'dp', 'tensor')
- grad_self_out: float32 [1536, 1536], P('tensor', 'dp')
- grad_cross_query: float32 [1536, 1536], P('dp', 'tensor')
- grad_cross_context: float32 [2, 768, 1536], P(None, 'dp', 'tensor')
- grad_cross_out: float32 [1536, 1536], P('tensor', 'dp')
- grad_gate_up: float32 [2, 1536, 6144], P(None, 'dp', 'tensor')
- grad_down_proj: float32 [6144, 1536], P('tensor', 'dp')
- grad_norm_gains: float32 [3, 1536], P(None, 'dp')
Inputs may be any that keep to these rules, and one draw needn't show every extreme that they name: `lengths`: each sequence has more than half of 513 valid positions, and some sequence has exactly 513.
All inputs are finite; a program needn't handle non-finite values.
Results may differ from a plain program's by a relative error of at most 0.025.
Values may be sent and summed in bfloat16 or wider, within the bound.
A program may use at most 256 MiB of HBM per device.

v0:
```python
import jax
import jax.numpy as jnp
from jax import lax
from jax.sharding import PartitionSpec as P

HD = 64


EPSILON = 1e-05
NEGATIVE = -1000000000.0


def norm_rows(stream, gain):
    centred = stream - jnp.mean(stream, axis=-1, keepdims=True)
    inverse = lax.rsqrt(jnp.mean(centred * centred, axis=-1, keepdims=True) + EPSILON)
    scaled = centred * inverse
    return (scaled * gain, scaled, inverse)


def norm_back(grad_out, scaled, inverse, gain):
    grad_scaled = grad_out * gain
    centre_part = jnp.mean(grad_scaled, axis=-1, keepdims=True)
    slope_part = jnp.mean(grad_scaled * scaled, axis=-1, keepdims=True)
    grad_in = inverse * (grad_scaled - centre_part - scaled * slope_part)
    return (grad_in, grad_out * scaled)


def split_heads(flat):
    return flat.reshape(flat.shape[0], flat.shape[1] // HD, HD)


def masked_scores(queries, keys_in, key_valid):
    scores = jnp.einsum(
        "qhd,khd->hqk", queries, keys_in, preferred_element_type=jnp.float32
    ) * HD ** (-0.5)
    return jnp.where(key_valid[None, None, :], scores, NEGATIVE)


def attend_forward(item):
    query_rows, key_rows, value_rows, key_valid = item
    scores = masked_scores(split_heads(query_rows), split_heads(key_rows), key_valid)
    peak_score = jnp.max(scores, axis=-1, keepdims=True)
    exponent = jnp.exp(scores - peak_score)
    denominator = jnp.sum(exponent, axis=-1, keepdims=True)
    probs = (exponent / denominator).astype(jnp.bfloat16)
    mixed = jnp.einsum(
        "hqk,khd->qhd", probs, split_heads(value_rows), preferred_element_type=jnp.float32
    )
    return (
        mixed.reshape(query_rows.shape).astype(jnp.bfloat16),
        (peak_score + jnp.log(denominator))[..., 0],
    )


def attend_backward(item):
    query_rows, key_rows, value_rows, logsum, grad_mixed, key_valid = item
    queries = split_heads(query_rows)
    keys_in = split_heads(key_rows)
    values = split_heads(value_rows)
    grads = split_heads(grad_mixed)
    probs = jnp.exp(masked_scores(queries, keys_in, key_valid) - logsum[..., None])
    grad_probs = jnp.einsum("qhd,khd->hqk", grads, values, preferred_element_type=jnp.float32)
    inner_sum = jnp.sum(probs * grad_probs, axis=-1, keepdims=True)
    grad_scores = (probs * (grad_probs - inner_sum)).astype(jnp.bfloat16)
    grad_values = jnp.einsum(
        "hqk,qhd->khd", probs.astype(jnp.bfloat16), grads, preferred_element_type=jnp.float32
    )
    grad_queries = jnp.einsum(
        "hqk,khd->qhd", grad_scores, keys_in, preferred_element_type=jnp.float32
    ) * HD ** (-0.5)
    grad_keys = jnp.einsum(
        "hqk,qhd->khd", grad_scores, queries, preferred_element_type=jnp.float32
    ) * HD ** (-0.5)
    return (
        grad_queries.reshape(query_rows.shape).astype(jnp.bfloat16),
        grad_keys.reshape(key_rows.shape).astype(jnp.bfloat16),
        grad_values.reshape(value_rows.shape).astype(jnp.bfloat16),
    )


def rows_whole(local_rows):
    return lax.all_gather(local_rows, "tensor", axis=1, tiled=True)


def rows_share(partial_value):
    return lax.psum_scatter(partial_value, "tensor", scatter_dimension=1, tiled=True)


def grad_whole(local_rows):
    return lax.all_gather(local_rows, "tensor", axis=1, tiled=True)


def grad_share(partial_value):
    return lax.psum_scatter(
        partial_value.astype(jnp.bfloat16), "tensor", scatter_dimension=1, tiled=True
    ).astype(jnp.float32)


def shards(
    inputs,
    context,
    lengths,
    cotangent,
    self_qkv,
    self_out,
    cross_query,
    cross_context,
    cross_out,
    gate_up,
    down_proj,
    norm_gains,
):
    seq_count, row_count, model_width = inputs.shape
    padded = row_count * lax.axis_size("tensor")
    tokens = seq_count * padded
    local_pos = lax.axis_index("tensor") * row_count + jnp.arange(row_count, dtype=jnp.int32)
    key_valid = jnp.arange(padded, dtype=jnp.int32)[None, :] < lengths[:, None]
    context_valid = jnp.ones((seq_count, context.shape[1]), dtype=jnp.bool_)
    row_keep = (local_pos[None, :] < lengths[:, None]).astype(jnp.float32)[:, :, None]
    (
        full_self_qkv,
        full_self_out,
        full_cross_query,
        full_cross_context,
        full_cross_out,
        full_gate_up,
        full_down,
    ) = (
        lax.all_gather(self_qkv.astype(jnp.bfloat16), "dp", axis=1, tiled=True),
        lax.all_gather(self_out.astype(jnp.bfloat16), "dp", axis=1, tiled=True),
        lax.all_gather(cross_query.astype(jnp.bfloat16), "dp", axis=0, tiled=True),
        lax.all_gather(cross_context.astype(jnp.bfloat16), "dp", axis=1, tiled=True),
        lax.all_gather(cross_out.astype(jnp.bfloat16), "dp", axis=1, tiled=True),
        lax.all_gather(gate_up.astype(jnp.bfloat16), "dp", axis=1, tiled=True),
        lax.all_gather(down_proj.astype(jnp.bfloat16), "dp", axis=1, tiled=True),
    )
    stream = inputs.astype(jnp.float32)
    normed, scaled_one, inverse_one = norm_rows(stream, norm_gains[0])
    whole_one = rows_whole(normed.astype(jnp.bfloat16)).reshape(tokens, model_width)
    qkv_rows = jnp.einsum(
        "td,cde->cte", whole_one, full_self_qkv, preferred_element_type=jnp.float32
    )
    qkv_rows = qkv_rows.astype(jnp.bfloat16).reshape(3, seq_count, padded, -1)
    mixed_one, logsum_one = lax.map(
        attend_forward, (qkv_rows[0], qkv_rows[1], qkv_rows[2], key_valid)
    )
    branch = jnp.dot(
        mixed_one.reshape(tokens, -1), full_self_out, preferred_element_type=jnp.float32
    )
    stream = stream + row_keep * rows_share(branch.reshape(seq_count, padded, model_width))
    normed, scaled_two, inverse_two = norm_rows(stream, norm_gains[1])
    whole_two = rows_whole(normed.astype(jnp.bfloat16)).reshape(tokens, model_width)
    cross_rows = jnp.dot(whole_two, full_cross_query, preferred_element_type=jnp.float32)
    cross_rows = cross_rows.astype(jnp.bfloat16).reshape(seq_count, padded, -1)
    context_rows = jnp.einsum(
        "scd,kde->ksce", context, full_cross_context, preferred_element_type=jnp.float32
    ).astype(jnp.bfloat16)
    mixed_two, logsum_two = lax.map(
        attend_forward, (cross_rows, context_rows[0], context_rows[1], context_valid)
    )
    branch = jnp.dot(
        mixed_two.reshape(tokens, -1), full_cross_out, preferred_element_type=jnp.float32
    )
    stream = stream + row_keep * rows_share(branch.reshape(seq_count, padded, model_width))
    normed, scaled_three, inverse_three = norm_rows(stream, norm_gains[2])
    whole_three = rows_whole(normed.astype(jnp.bfloat16)).reshape(tokens, model_width)
    gate_rows = jnp.einsum(
        "td,kdf->ktf", whole_three, full_gate_up, preferred_element_type=jnp.float32
    )
    sigmoid_gate = jax.nn.sigmoid(gate_rows[0])
    hidden = (gate_rows[0] * sigmoid_gate * gate_rows[1]).astype(jnp.bfloat16)
    branch = jnp.dot(hidden, full_down, preferred_element_type=jnp.float32)
    stream = stream + row_keep * rows_share(branch.reshape(seq_count, padded, model_width))
    output = (row_keep * stream).astype(jnp.bfloat16)
    (
        full_self_qkv,
        full_self_out,
        full_cross_query,
        full_cross_context,
        full_cross_out,
        full_gate_up,
        full_down,
    ) = (
        lax.all_gather(self_qkv.astype(jnp.bfloat16), "dp", axis=1, tiled=True),
        lax.all_gather(self_out.astype(jnp.bfloat16), "dp", axis=1, tiled=True),
        lax.all_gather(cross_query.astype(jnp.bfloat16), "dp", axis=0, tiled=True),
        lax.all_gather(cross_context.astype(jnp.bfloat16), "dp", axis=1, tiled=True),
        lax.all_gather(cross_out.astype(jnp.bfloat16), "dp", axis=1, tiled=True),
        lax.all_gather(gate_up.astype(jnp.bfloat16), "dp", axis=1, tiled=True),
        lax.all_gather(down_proj.astype(jnp.bfloat16), "dp", axis=1, tiled=True),
    )
    grad_stream = row_keep * cotangent.astype(jnp.float32)
    grad_branch = grad_whole((row_keep * grad_stream).astype(jnp.bfloat16)).reshape(
        tokens, model_width
    )
    grad_down = jnp.einsum("tf,td->fd", hidden, grad_branch, preferred_element_type=jnp.float32)
    grad_hidden = jnp.einsum(
        "td,fd->tf", grad_branch, full_down, preferred_element_type=jnp.float32
    )
    grad_gate = (
        grad_hidden * gate_rows[1] * sigmoid_gate * (1.0 + gate_rows[0] * (1.0 - sigmoid_gate))
    )
    grad_upper = grad_hidden * gate_rows[0] * sigmoid_gate
    grad_expand = jnp.stack([grad_gate, grad_upper]).astype(jnp.bfloat16)
    grad_gates = jnp.einsum(
        "td,ktf->kdf", whole_three, grad_expand, preferred_element_type=jnp.float32
    )
    partial_value = jnp.einsum(
        "ktf,kdf->td", grad_expand, full_gate_up, preferred_element_type=jnp.float32
    )
    grad_norm, gain_rows = norm_back(
        grad_share(partial_value.reshape(seq_count, padded, model_width)),
        scaled_three,
        inverse_three,
        norm_gains[2],
    )
    gain_three = jnp.sum(gain_rows, axis=(0, 1))
    grad_stream = grad_stream + grad_norm
    grad_branch = grad_whole((row_keep * grad_stream).astype(jnp.bfloat16)).reshape(
        tokens, model_width
    )
    grad_merge = jnp.einsum(
        "te,td->ed", mixed_two.reshape(tokens, -1), grad_branch, preferred_element_type=jnp.float32
    )
    grad_mixed = jnp.einsum(
        "td,ed->te", grad_branch, full_cross_out, preferred_element_type=jnp.float32
    )
    grad_mixed = grad_mixed.astype(jnp.bfloat16).reshape(seq_count, padded, -1)
    grad_query, grad_key, grad_value = lax.map(
        attend_backward,
        (cross_rows, context_rows[0], context_rows[1], logsum_two, grad_mixed, context_valid),
    )
    grad_cross = jnp.einsum(
        "td,te->de", whole_two, grad_query.reshape(tokens, -1), preferred_element_type=jnp.float32
    )
    grad_pairs = jnp.stack([grad_key, grad_value])
    grad_context_proj = jnp.einsum(
        "scd,ksce->kde", context, grad_pairs, preferred_element_type=jnp.float32
    )
    context_part = jnp.einsum(
        "ksce,kde->scd", grad_pairs, full_cross_context, preferred_element_type=jnp.float32
    )
    partial_value = jnp.einsum(
        "te,de->td",
        grad_query.reshape(tokens, -1),
        full_cross_query,
        preferred_element_type=jnp.float32,
    )
    grad_norm, gain_rows = norm_back(
        grad_share(partial_value.reshape(seq_count, padded, model_width)),
        scaled_two,
        inverse_two,
        norm_gains[1],
    )
    gain_two = jnp.sum(gain_rows, axis=(0, 1))
    grad_stream = grad_stream + grad_norm
    grad_branch = grad_whole((row_keep * grad_stream).astype(jnp.bfloat16)).reshape(
        tokens, model_width
    )
    grad_after = jnp.einsum(
        "te,td->ed", mixed_one.reshape(tokens, -1), grad_branch, preferred_element_type=jnp.float32
    )
    grad_mixed = jnp.einsum(
        "td,ed->te", grad_branch, full_self_out, preferred_element_type=jnp.float32
    )
    grad_mixed = grad_mixed.astype(jnp.bfloat16).reshape(seq_count, padded, -1)
    grad_query, grad_key, grad_value = lax.map(
        attend_backward, (qkv_rows[0], qkv_rows[1], qkv_rows[2], logsum_one, grad_mixed, key_valid)
    )
    grad_triple = jnp.stack([grad_query, grad_key, grad_value]).reshape(3, tokens, -1)
    grad_self = jnp.einsum(
        "td,cte->cde", whole_one, grad_triple, preferred_element_type=jnp.float32
    )
    partial_value = jnp.einsum(
        "cte,cde->td", grad_triple, full_self_qkv, preferred_element_type=jnp.float32
    )
    grad_norm, gain_rows = norm_back(
        grad_share(partial_value.reshape(seq_count, padded, model_width)),
        scaled_one,
        inverse_one,
        norm_gains[0],
    )
    gain_one = jnp.sum(gain_rows, axis=(0, 1))
    grad_inputs = grad_stream + grad_norm
    gain_partial = jnp.stack([gain_one, gain_two, gain_three])
    gain_total, grad_context = (
        lax.psum(gain_partial.astype(jnp.bfloat16), "tensor").astype(jnp.float32),
        lax.psum(context_part.astype(jnp.bfloat16), "tensor").astype(jnp.float32),
    )
    result_grads = (
        lax.psum_scatter(
            grad_self.astype(jnp.bfloat16), "dp", scatter_dimension=1, tiled=True
        ).astype(jnp.float32),
        lax.psum_scatter(
            grad_after.astype(jnp.bfloat16), "dp", scatter_dimension=1, tiled=True
        ).astype(jnp.float32),
        lax.psum_scatter(
            grad_cross.astype(jnp.bfloat16), "dp", scatter_dimension=0, tiled=True
        ).astype(jnp.float32),
        lax.psum_scatter(
            grad_context_proj.astype(jnp.bfloat16), "dp", scatter_dimension=1, tiled=True
        ).astype(jnp.float32),
        lax.psum_scatter(
            grad_merge.astype(jnp.bfloat16), "dp", scatter_dimension=1, tiled=True
        ).astype(jnp.float32),
        lax.psum_scatter(
            grad_gates.astype(jnp.bfloat16), "dp", scatter_dimension=1, tiled=True
        ).astype(jnp.float32),
        lax.psum_scatter(
            grad_down.astype(jnp.bfloat16), "dp", scatter_dimension=1, tiled=True
        ).astype(jnp.float32),
        lax.psum_scatter(
            gain_total.astype(jnp.bfloat16), "dp", scatter_dimension=1, tiled=True
        ).astype(jnp.float32),
    )
    return (
        output,
        grad_inputs,
        grad_context,
        result_grads[0],
        result_grads[1],
        result_grads[2],
        result_grads[3],
        result_grads[4],
        result_grads[5],
        result_grads[6],
        result_grads[7],
    )


def solution(mesh):
    placed = (
        P("dp", "tensor", None),
        P("dp", None, None),
        P("dp"),
        P("dp", "tensor", None),
        P(None, "dp", "tensor"),
        P("tensor", "dp"),
        P("dp", "tensor"),
        P(None, "dp", "tensor"),
        P("tensor", "dp"),
        P(None, "dp", "tensor"),
        P("tensor", "dp"),
        P(),
    )
    return jax.shard_map(
        shards,
        mesh=mesh,
        in_specs=placed,
        out_specs=(
            P("dp", "tensor", None),
            P("dp", "tensor", None),
            P("dp", None, None),
            P(None, "dp", "tensor"),
            P("tensor", "dp"),
            P("dp", "tensor"),
            P(None, "dp", "tensor"),
            P("tensor", "dp"),
            P(None, "dp", "tensor"),
            P("tensor", "dp"),
            P(None, "dp"),
        ),
        check_vma=False,
    )
```

profile of v0, /device:TPU:0, one launch (start us, length us, event | category | flops | bytes accessed | tf_op | source)
XLA Modules:
  0.0 1786.4 jit_solution(8967615113991448713)
XLA Ops:
  15.4 67.8 %all-gather.14.cloned.1.call-done = bf16[2,544,1536]{2,1,0:T(8,128)(2,1)} async-done(((bf16[2,136,1536]{2,1,0:T(8,128)(2,1)}), bf16[2,544,1536]{2,1,0:T(8,128)(2,1)}) %all-gather.14.cloned.1.call-update) | async-done | bytes 3342352 | tf_op jit(solution)/shard_map/all_gather | solution.py:82
  83.1 35.1 %all-gather.16.cloned.1.call-done = bf16[3,1536,384]{2,1,0:T(8,128)(2,1)} async-done(((bf16[3,192,384]{2,1,0:T(8,128)(2,1)}), bf16[3,1536,384]{2,1,0:T(8,128)(2,1)}) %all-gather.16.cloned.1.call-update) | async-done | bytes 3538960 | tf_op jit(solution)/shard_map/all_gather | solution.py:129
  118.3 7.5 fusion.37
  130.8 15.3 while.52
  146.2 7.4 fusion.88
  156.3 114.6 %reduce-scatter.23.cloned.1.call-done = f32[2,136,1536]{2,1,0:T(8,128)} async-done(((f32[2,544,1536]{2,1,0:T(8,128)}), f32[2,136,1536]{2,1,0:T(8,128)}) %reduce-scatter.23.cloned.1.call-update) | async-done | bytes 1671184 | tf_op jit(solution)/shard_map/reduce_scatter | solution.py:86
  275.2 22.7 %all-gather.20.cloned.1.call-done = bf16[2,768,384]{2,1,0:T(8,128)(2,1)} async-done(((bf16[2,96,384]{2,1,0:T(8,128)(2,1)}), bf16[2,768,384]{2,1,0:T(8,128)(2,1)}) %all-gather.20.cloned.1.call-update) | async-done | bytes 1179664 | tf_op jit(solution)/shard_map/all_gather | solution.py:132
  300.8 23.5 %all-gather.24.cloned.1.call-done = bf16[1536,384]{1,0:T(8,128)(2,1)} async-done(((bf16[192,384]{1,0:T(8,128)(2,1)}), bf16[1536,384]{1,0:T(8,128)(2,1)}) %all-gather.24.cloned.1.call-update) | async-done | bytes 1179664 | tf_op jit(solution)/shard_map/all_gather | solution.py:131
  324.3 68.9 %all-gather.22.cloned.1.call-done = bf16[2,544,1536]{2,1,0:T(8,128)(2,1)} async-done(((bf16[2,136,1536]{2,1,0:T(8,128)(2,1)}), bf16[2,544,1536]{2,1,0:T(8,128)(2,1)}) %all-gather.22.cloned.1.call-update) | async-done | bytes 3342352 | tf_op jit(solution)/shard_map/all_gather | solution.py:82
  393.2 5.1 convolution_convert_fusion.8
  400.9 8.5 while.53
  409.4 9.0 all-gather.26.cloned.1.call-done
  418.4 6.4 fusion.85
  424.8 2.8 convert_element_type.338
  427.7 114.4 %reduce-scatter.25.cloned.1.call-done = f32[2,136,1536]{2,1,0:T(8,128)} async-done(((f32[2,544,1536]{2,1,0:T(8,128)}), f32[2,136,1536]{2,1,0:T(8,128)}) %reduce-scatter.25.cloned.1.call-update) | async-done | bytes 1671184 | tf_op jit(solution)/shard_map/reduce_scatter | solution.py:86
  542.0 3.0 fusion.103
  549.8 53.9 %all-gather.30.cloned.1.call-done = bf16[2,1536,1536]{2,1,0:T(8,128)(2,1)} async-done(((bf16[2,192,1536]{2,1,0:T(8,128)(2,1)}), bf16[2,1536,1536]{2,1,0:T(8,128)(2,1)}) %all-gather.30.cloned.1.call-update) | async-done | bytes 9437200 | tf_op jit(solution)/shard_map/all_gather | solution.py:134
  603.7 68.9 %all-gather.28.cloned.1.call-done = bf16[2,544,1536]{2,1,0:T(8,128)(2,1)} async-done(((bf16[2,136,1536]{2,1,0:T(8,128)(2,1)}), bf16[2,544,1536]{2,1,0:T(8,128)(2,1)}) %all-gather.28.cloned.1.call-update) | async-done | bytes 3342352 | tf_op jit(solution)/shard_map/all_gather | solution.py:82
  672.6 17.1 convolution_bitcast_fusion
  689.7 22.9 %all-gather.32.cloned.1.call-done = bf16[1536,1536]{0,1:T(8,128)(2,1)} async-done(((bf16[1536,192]{0,1:T(8,128)(2,1)}), bf16[1536,1536]{0,1:T(8,128)(2,1)}) %all-gather.32.cloned.1.call-update) | async-done | bytes 4718608 | tf_op jit(solution)/shard_map/all_gather | solution.py:135
  712.5 68.9 %all-gather.34.cloned.1.call-done = bf16[2,544,1536]{2,1,0:T(8,128)(2,1)} async-done(((bf16[2,136,1536]{2,1,0:T(8,128)(2,1)}), bf16[2,544,1536]{2,1,0:T(8,128)(2,1)}) %all-gather.34.cloned.1.call-update) | async-done | bytes 3342352 | tf_op jit(solution)/shard_map/all_gather | solution.py:90
  781.4 12.6 fusion.41
  794.1 15.6 fusion.23
  809.7 3.4 copy.156
  815.7 62.1 %reduce-scatter.37.cloned.1.call-done = bf16[136,3072]{1,0:T(8,128)(2,1)} async-done(((bf16[544,3072]{1,0:T(8,128)(2,1)}), bf16[136,3072]{1,0:T(8,128)(2,1)}) %reduce-scatter.37.cloned.1.call-update) | async-done | bytes 835600
  877.8 3.4 reshape.420
  881.2 2.8 fusion.72
  885.7 66.9 %all-gather.36.cloned.1.call-done = bf16[2,544,1536]{2,1,0:T(8,128)(2,1)} async-done(((bf16[2,136,1536]{2,1,0:T(8,128)(2,1)}), bf16[2,544,1536]{2,1,0:T(8,128)(2,1)}) %all-gather.36.cloned.1.call-update) | async-done | bytes 3342352 | tf_op jit(solution)/shard_map/all_gather | solution.py:90
  952.7 5.1 convolution_convert_fusion.7
  958.8 17.0 while.54
  975.8 3.6 convolution_convert_fusion.5
  979.4 3.4 copy.158
  985.5 10.9 fusion.105
  996.5 11.9 fusion.33
  1008.4 39.1 %reduce-scatter.39.cloned.1.call-done = bf16[136,3072]{1,0:T(8,128)(2,1)} async-done(((bf16[544,3072]{1,0:T(8,128)(2,1)}), bf16[136,3072]{1,0:T(8,128)(2,1)}) %reduce-scatter.39.cloned.1.call-update) | async-done | bytes 835600
  1047.6 3.4 reshape.422
  1053.6 113.5 %reduce-scatter.27.cloned.1.call-done = f32[2,136,1536]{2,1,0:T(8,128)} async-done(((f32[2,544,1536]{2,1,0:T(8,128)}), f32[2,136,1536]{2,1,0:T(8,128)}) %reduce-scatter.27.cloned.1.call-update) | async-done | bytes 1671184 | tf_op jit(solution)/shard_map/reduce_scatter | solution.py:86
  1167.0 4.5 multiply_convert_fusion.6
  1171.6 12.3 convolution_convert_fusion.3
  1186.7 5.3 fusion.43
  1192.4 5.2 fusion.44
  1197.6 17.9 %fusion.22 = bf16[2,1536,1536]{1,2,0:T(8,128)(2,1)} fusion(bf16[1088,1536,1]{1,0,2:T(8,128)(2,1)} %bitcast.431, bf16[1,1088,1536]{2,1,0:T(8,128)(2,1)} %copy-done.62, bf16[1,1088,1536]{2,1,0:T(8,128)(2,1)} %copy-done.61), kind=kOutput, calls=%fused_computation.67 | convolution fusion | flops 10275717120 | bytes 19464192 | tf_op jit(solution)/shard_map/td,ktf->kdf/dot_general | solution.py:205
  1215.6 24.1 %copy.134 = bf16[2,1536,1536]{2,0,1:T(2,128)(2,1)} copy(bf16[2,1536,1536]{1,2,0:T(8,128)(2,1)} %fusion.22) | data formatting | bytes 18874368 | tf_op jit(solution)/shard_map/convert_element_type | solution.py:307
  1240.5 2.8 copy.132
  1244.6 5.3 fusion.42
  1250.4 5.2 convolution_convert_fusion.6
  1255.6 46.6 %while.55 = (s32[]{:T(128)}, bf16[2,544,384]{2,1,0:T(8,128)(2,1)}, bf16[2,544,384]{2,1,0:T(8,128)(2,1)}, bf16[2,544,384]{2,1,0:T(8,128)(2,1)}, bf16[2,544,384]{1...) while((s32[]{:T(128)}, bf16[2,544,384]{2,1,0:T(8,128)(2,1)}, ...), condition=%wide.region_28.29_spmd, body=%wide.region_26.28_spmd.sunk | while | flops 1164069632 | bytes 123551856 | solution.py:267
  1260.5 3.5 fusion.230
  1265.4 6.3 multiply_reduce_fusion.10
  1283.8 3.5 fusion.230
  1288.6 6.3 multiply_reduce_fusion.10
  1302.2 7.6 fusion.36
  1309.8 5.7 copy.162
  1315.5 4.9 copy.181
  1324.1 4.8 bitcast_convert_fusion.1
  1328.9 3.4 copy.160
  1341.9 32.8 %reduce-scatter.31.cloned.1.call-done = bf16[192,384]{1,0:T(8,128)(2,1)} async-done(((bf16[1536,384]{1,0:T(8,128)(2,1)}), bf16[192,384]{1,0:T(8,128)(2,1)}) %reduce-scatter.31.cloned.1.call-update) | async-done | bytes 147472 | tf_op jit(solution)/shard_map/reduce_scatter | solution.py:297
  1376.4 38.7 %reduce-scatter.33.cloned.1.call-done = bf16[384,192]{0,1:T(8,128)(2,1)} async-done(((bf16[384,1536]{0,1:T(8,128)(2,1)}), bf16[384,192]{0,1:T(8,128)(2,1)}) %reduce-scatter.33.cloned.1.call-update) | async-done | bytes 147472 | tf_op jit(solution)/shard_map/reduce_scatter | solution.py:303
  1416.7 153.2 %all-reduce.8.cloned.1.call-done = (bf16[2,768,384]{2,0,1:T(2,128)(2,1)}, bf16[2,1536,1536]{2,0,1:T(2,128)(2,1)}) async-done(((bf16[2,768,384]{2,0,1:T(2,128)(2,1)}, bf16[2,1536,1536]{2,0,1:T(2,128)(2,1)}), (bf16[2,768,384]{2,0,1:T(2,128)(2,1)}, bf16[2,1536,1536]{2,0,1:T(2,128)(2,1)})) %all-reduce.8.cloned.1.call-update) | async-done | bytes 10616848
  1575.6 34.6 %reduce-scatter.29.cloned.1.call-done = bf16[384,192]{0,1:T(8,128)(2,1)} async-done(((bf16[384,1536]{0,1:T(8,128)(2,1)}), bf16[384,192]{0,1:T(8,128)(2,1)}) %reduce-scatter.29.cloned.1.call-update) | async-done | bytes 147472 | tf_op jit(solution)/shard_map/reduce_scatter | solution.py:294
  1611.9 49.9 %reduce-scatter.43.cloned.1.call-done = bf16[192,1152]{1,0:T(8,128)(2,1)} async-done(((bf16[1536,1152]{1,0:T(8,128)(2,1)}), bf16[192,1152]{1,0:T(8,128)(2,1)}) %reduce-scatter.43.cloned.1.call-update) | async-done | bytes 442384
  1666.9 60.4 %reduce-scatter.41.cloned.1.call-done = bf16[136,3072]{1,0:T(8,128)(2,1)} async-done(((bf16[544,3072]{1,0:T(8,128)(2,1)}), bf16[136,3072]{1,0:T(8,128)(2,1)}) %reduce-scatter.41.cloned.1.call-update) | async-done | bytes 835600
  1733.8 32.3 %reduce-scatter.45.cloned.1.call-done = bf16[192,3]{1,0:T(8,128)(2,1)} async-done(((bf16[1536,3]{1,0:T(8,128)(2,1)}), bf16[192,3]{1,0:T(8,128)(2,1)}) %reduce-scatter.45.cloned.1.call-update) | async-done | bytes 1168
  1767.0 11.7 psum.16
  (373 shorter events, 148.6 us)
Async XLA Ops:
  7.2 6.5 copy-start.24
  7.2 76.0 %all-gather.14.cloned.1.call-start = ((), (), s32[]{:S(2)}) async-start(), calls=%async_computation.12 | async-start | bytes 4177920 | tf_op jit(solution)/shard_map/all_gather | solution.py:82
  8.7 5.8 copy-start.40
  8.7 5.9 copy-start.32
  10.3 115.5 %copy-start.44 = (f32[2,136]{1,0:T(2,128)}, f32[2,136]{1,0:T(2,128)S(1)}, u32[]{:S(2)}) copy-start(f32[2,136]{1,0:T(2,128)S(1)} %add_rsqrt_fusion.2) | copy-start | bytes 3268
  11.2 114.6 %copy-start.36 = (f32[1536]{0:T(1024)}, f32[1536]{0:T(1024)S(1)}, u32[]{:S(2)}) copy-start(f32[1536]{0:T(1024)S(1)} %get-tuple-element.334) | copy-start | bytes 18436
  11.2 261.9 %copy-start.38 = (f32[1536]{0:T(1024)}, f32[1536]{0:T(1024)S(1)}, u32[]{:S(2)}) copy-start(f32[1536]{0:T(1024)S(1)} %get-tuple-element.335) | copy-start | bytes 18436
  13.6 104.7 %all-gather.16.cloned.1.call-start = ((), (), s32[]{:S(2)}) async-start(), calls=%async_computation.13 | async-start | bytes 3981312 | tf_op jit(solution)/shard_map/all_gather | solution.py:129
  14.5 131.7 %all-gather.18.cloned.1.call-start = ((), (), s32[]{:S(2)}) async-start(), calls=%async_computation.14 | async-start | bytes 1327104 | tf_op jit(solution)/shard_map/all_gather | solution.py:130
  15.2 255.7 %reduce-scatter.23.cloned.1.call-start = ((), (), s32[]{:S(2)}) async-start(), calls=%async_computation.15 | async-start | bytes 8355840 | tf_op jit(solution)/shard_map/reduce_scatter | solution.py:86
  146.1 7.5 copy-start.4
  146.1 7.5 copy-start.7
  146.1 7.5 copy-start.8
  146.1 7.5 copy-start.28
  146.1 7.5 copy-start.30
  153.6 117.3 %copy-start.9 = (bf16[2,136,1536]{2,1,0:T(8,128)(2,1)S(1)}, bf16[2,136,1536]{2,1,0:T(8,128)(2,1)}, u32[]{:S(2)}) copy-start(bf16[2,136,1536]{2,1,0:T(8,128)(2,1)} %param.20) | copy-start | bytes 2506756
  153.7 144.2 %all-gather.20.cloned.1.call-start = ((), (), s32[]{:S(2)}) async-start(), calls=%async_computation.16 | async-start | bytes 1327104 | tf_op jit(solution)/shard_map/all_gather | solution.py:132
  155.3 169.0 %all-gather.24.cloned.1.call-start = ((), (), s32[]{:S(2)}) async-start(), calls=%async_computation.18 | async-start | bytes 1327104 | tf_op jit(solution)/shard_map/all_gather | solution.py:131
  156.0 237.1 %all-gather.22.cloned.1.call-start = ((), (), s32[]{:S(2)}) async-start(), calls=%async_computation.17 | async-start | bytes 4177920 | tf_op jit(solution)/shard_map/all_gather | solution.py:82
  272.8 25.1 %copy-start.53 = (bf16[2,130,768]{2,0,1:T(2,128)(2,1)S(1)}, bf16[2,130,768]{2,0,1:T(2,128)(2,1)}, u32[]{:S(2)}) copy-start(bf16[2,130,768]{2,0,1:T(2,128)(2,1)} %param.21) | copy-start | bytes 1198084
  273.1 26.5 %copy-start.46 = (f32[2,136]{1,0:T(2,128)}, f32[2,136]{1,0:T(2,128)S(1)}, u32[]{:S(2)}) copy-start(f32[2,136]{1,0:T(2,128)S(1)} %add_rsqrt_fusion.1) | copy-start | bytes 3268
  274.3 144.0 %all-gather.26.cloned.1.call-start = ((), (), s32[]{:S(2)}) async-start(), calls=%async_computation.19 | async-start | bytes 1327104 | tf_op jit(solution)/shard_map/all_gather | solution.py:133
  275.1 266.9 %reduce-scatter.25.cloned.1.call-start = ((), (), s32[]{:S(2)}) async-start(), calls=%async_computation.20 | async-start | bytes 8355840 | tf_op jit(solution)/shard_map/reduce_scatter | solution.py:86
  409.4 15.4 copy-start.6
  409.4 15.4 copy-start.11
  424.7 179.0 %all-gather.30.cloned.1.call-start = ((), (), s32[]{:S(2)}) async-start(), calls=%async_computation.22 | async-start | bytes 10616832 | tf_op jit(solution)/shard_map/all_gather | solution.py:134
  427.6 245.0 %all-gather.28.cloned.1.call-start = ((), (), s32[]{:S(2)}) async-start(), calls=%async_computation.21 | async-start | bytes 4177920 | tf_op jit(solution)/shard_map/all_gather | solution.py:82
  545.0 338.9 %copy-start.2 = (f32[2,136,1536]{2,1,0:T(8,128)}, f32[2,136,1536]{2,1,0:T(8,128)S(1)}, u32[]{:S(2)}) copy-start(f32[2,136,1536]{2,1,0:T(8,128)S(1)} %get-tuple-element.405) | copy-start | bytes 5013508
  546.6 165.9 %all-gather.32.cloned.1.call-start = ((), (), s32[]{:S(2)}) async-start(), calls=%async_computation.23 | async-start | bytes 5308416 | tf_op jit(solution)/shard_map/all_gather | solution.py:135
  548.8 232.6 %all-gather.34.cloned.1.call-start = ((), (), s32[]{:S(2)}) async-start(), calls=%async_computation.25 | async-start | bytes 4177920 | tf_op jit(solution)/shard_map/all_gather | solution.py:90
  549.6 328.2 %reduce-scatter.37.cloned.1.call-start = ((), (), s32[]{:S(2)}) async-start(), calls=%async_computation.33 | async-start | bytes 4177920
  794.0 15.7 copy-start.61
  794.1 15.7 copy-start.62
  815.7 137.0 %all-gather.36.cloned.1.call-start = ((), (), s32[]{:S(2)}) async-start(), calls=%async_computation.26 | async-start | bytes 4177920 | tf_op jit(solution)/shard_map/all_gather | solution.py:90
  885.7 161.9 %reduce-scatter.39.cloned.1.call-start = ((), (), s32[]{:S(2)}) async-start(), calls=%async_computation.34 | async-start | bytes 4177920
  952.7 6.2 copy-start.12
  985.5 181.6 %reduce-scatter.27.cloned.1.call-start = ((), (), s32[]{:S(2)}) async-start(), calls=%async_computation.24 | async-start | bytes 8355840 | tf_op jit(solution)/shard_map/reduce_scatter | solution.py:86
  1008.3 42.6 %copy-start.39 = (f32[1536]{0:T(1024)S(1)}, f32[1536]{0:T(1024)}, u32[]{:S(2)}) copy-start(f32[1536]{0:T(1024)} %copy-done.38) | copy-start | bytes 18436
  1008.3 42.6 %copy-start.43 = (f32[2,136]{1,0:T(2,128)S(1)}, f32[2,136]{1,0:T(2,128)}, u32[]{:S(2)}) copy-start(f32[2,136]{1,0:T(2,128)} %copy-done.42) | copy-start | bytes 3268
  1008.3 42.6 %copy-start.47 = (f32[2,136]{1,0:T(2,128)S(1)}, f32[2,136]{1,0:T(2,128)}, u32[]{:S(2)}) copy-start(f32[2,136]{1,0:T(2,128)} %copy-done.46) | copy-start | bytes 3268
  1008.4 158.7 %copy-start.3 = (f32[2,136,1536]{2,1,0:T(8,128)S(1)}, f32[2,136,1536]{2,1,0:T(8,128)}, u32[]{:S(2)}) copy-start(f32[2,136,1536]{2,1,0:T(8,128)} %copy-done.2) | copy-start | bytes 5013508
  1008.4 235.1 %all-gather.38.cloned.1.call-start = ((), (), s32[]{:S(2)}) async-start(), calls=%async_computation.27 | async-start | bytes 4177920 | tf_op jit(solution)/shard_map/all_gather | solution.py:90
  1171.6 165.9 %reduce-scatter.35.cloned.1.call-start = ((), (), s32[]{:S(2)}) async-start(), calls=%async_computation.32 | async-start | bytes 5308416 | tf_op jit(solution)/shard_map/reduce_scatter | solution.py:309
  1184.0 155.7 %all-reduce.6.cloned.1.call-start = ((), (), s32[]{:S(2)}) async-start(), calls=%async_computation.28 | async-start | bytes 835584 | tf_op jit(solution)/shard_map/psum | solution.py:288
  1186.6 5.7 copy-start.21
  1186.7 188.1 %reduce-scatter.31.cloned.1.call-start = ((), (), s32[]{:S(2)}) async-start(), calls=%async_computation.30 | async-start | bytes 1327104 | tf_op jit(solution)/shard_map/reduce_scatter | solution.py:297
  1192.1 223.0 %reduce-scatter.33.cloned.1.call-start = ((), (), s32[]{:S(2)}) async-start(), calls=%async_computation.31 | async-start | bytes 1327104 | tf_op jit(solution)/shard_map/reduce_scatter | solution.py:303
  1197.6 372.3 %all-reduce.8.cloned.1.call-start = ((), (), s32[]{:S(2)}) async-start(), calls=%async_computation.38 | async-start | bytes 21233664
  1215.6 24.1 %copy-start.54 = (bf16[2,130,768]{2,0,1:T(2,128)(2,1)S(1)}, bf16[2,130,768]{2,0,1:T(2,128)(2,1)}, u32[]{:S(2)}) copy-start(bf16[2,130,768]{2,0,1:T(2,128)(2,1)} %param.21) | copy-start | bytes 1198084
  1215.6 24.1 %copy-start.59 = (bf16[2,130,384]{2,1,0:T(8,128)(2,1)S(1)}, bf16[2,130,384]{2,1,0:T(8,128)(2,1)}, u32[]{:S(2)}) copy-start(bf16[2,130,384]{2,1,0:T(8,128)(2,1)} %get-tuple-element.193) | copy-start | bytes 599044
  1243.4 366.8 %reduce-scatter.29.cloned.1.call-start = ((), (), s32[]{:S(2)}) async-start(), calls=%async_computation.29 | async-start | bytes 1327104 | tf_op jit(solution)/shard_map/reduce_scatter | solution.py:294
  1243.5 6.9 copy-start.22
  1249.9 411.9 %reduce-scatter.43.cloned.1.call-start = ((), (), s32[]{:S(2)}) async-start(), calls=%async_computation.36 | async-start | bytes 3981312
  1250.4 5.2 copy-start.5
  1250.4 5.2 copy-start.29
  1265.4 6.3 copy-start.1
  1288.6 6.3 copy-start.1
  1320.4 406.9 %reduce-scatter.41.cloned.1.call-start = ((), (), s32[]{:S(2)}) async-start(), calls=%async_computation.35 | async-start | bytes 4177920
  1334.9 431.2 %reduce-scatter.45.cloned.1.call-start = ((), (), s32[]{:S(2)}) async-start(), calls=%async_computation.37 | async-start | bytes 442368
  1611.9 118.1 %copy-start.10 = (bf16[2,136,1536]{2,1,0:T(8,128)(2,1)S(1)}, bf16[2,136,1536]{2,1,0:T(8,128)(2,1)}, u32[]{:S(2)}) copy-start(bf16[2,136,1536]{2,1,0:T(8,128)(2,1)} %param.20) | copy-start | bytes 2506756
  1611.9 118.1 %copy-start.37 = (f32[1536]{0:T(1024)S(1)}, f32[1536]{0:T(1024)}, u32[]{:S(2)}) copy-start(f32[1536]{0:T(1024)} %copy-done.36) | copy-start | bytes 18436
  1611.9 118.1 %copy-start.41 = (f32[2,136]{1,0:T(2,128)S(1)}, f32[2,136]{1,0:T(2,128)}, u32[]{:S(2)}) copy-start(f32[2,136]{1,0:T(2,128)} %copy-done.40) | copy-start | bytes 3268
  1611.9 118.1 %copy-start.45 = (f32[2,136]{1,0:T(2,128)S(1)}, f32[2,136]{1,0:T(2,128)}, u32[]{:S(2)}) copy-start(f32[2,136]{1,0:T(2,128)} %copy-done.44) | copy-start | bytes 3268
  1664.5 67.5 %copy-start.15 = (f32[2,136,1536]{2,1,0:T(8,128)S(1)}, f32[2,136,1536]{2,1,0:T(8,128)}, u32[]{:S(2)}) copy-start(f32[2,136,1536]{2,1,0:T(8,128)} %get-tuple-element.403) | copy-start | bytes 5013508
  (34 other events, 63.0 us)
Sparse Core Ops, SparseCore 0:
  13.7 69.3 all-gather.13
  85.6 32.6 all-gather.15
  120.7 24.0 all-gather.17
  153.8 117.0 reduce-scatter.22
  273.2 24.5 all-gather.19
  300.2 24.0 all-gather.23
  326.4 66.6 all-gather.21
  395.6 22.7 all-gather.25
  424.9 117.1 reduce-scatter.24
  544.4 59.3 all-gather.29
  605.9 66.6 all-gather.27
  674.9 37.5 all-gather.31
  714.7 66.6 all-gather.33
  815.8 61.9 reduce-scatter.36
  885.8 66.8 all-gather.35
  985.6 61.9 reduce-scatter.38
  1049.7 117.2 reduce-scatter.26
  1171.7 67.2 all-gather.37
  1242.4 52.5 reduce-scatter.34
  1297.4 36.8 all-reduce.5
  1338.1 36.5 reduce-scatter.30
  1378.3 36.7 reduce-scatter.32
  1418.7 151.1 all-reduce.7
  1573.3 36.8 reduce-scatter.28
  1613.7 48.0 reduce-scatter.42
  1664.0 63.2 reduce-scatter.40
  1732.1 33.9 reduce-scatter.44
where the time goes:
time: 1800 us; the launch traced here: 1790 us
  waiting for transfers between devices  1360 us (76%)
  matrix products  203 us (11%)
  local copies, waits for them, and re-layouts  138 us (8%)
  other arithmetic  58.2 us (3%)
    unnamed x33, waiting for transfers between devices  398 us
    reduce_scatter x3, waiting for transfers between devices, rows_share(): lax.psum_scatter(partial_value, 'tensor', scatter_dimension=1, tiled=True)  342 us
    all_gather x3, waiting for transfers between devices, rows_whole(): return lax.all_gather(local_rows, 'tensor', axis=1, tiled=True)  206 us
    all_gather x3, waiting for transfers between devices, grad_whole(): return lax.all_gather(local_rows, 'tensor', axis=1, tiled=True)  136 us
    unnamed x130, local copies, waits for them, and re-layouts  57.1 us
    all_gather x1, waiting for transfers between devices, shards(): lax.all_gather(gate_up.astype(jnp.bfloat16), 'dp', axis=1, tiled=True)  53.9 us
    reduce_scatter x1, waiting for transfers between devices, shards(): lax.psum_scatter(grad_merge.astype(jnp.bfloat16), 'dp', scatter_dimension...  38.7 us
  transfers between devices with their start and end apart: 27, of which 23 were waited for; matrix products, arithmetic and copies ran while one was open for 16% of the time, Pallas kernels for 0%

commit v1 on v0

--- a/solution.py
+++ b/solution.py
@@ -1,6 +1,10 @@
+import functools
+
 import jax
 import jax.numpy as jnp
 from jax import lax
+from jax.experimental import pallas as pl
+from jax.experimental.pallas import tpu as pltpu
 from jax.sharding import PartitionSpec as P
 
 HD = 64
@@ -328,7 +332,633 @@
     )
 
 
+CORE, XBIT, YBIT = 1, 2, 4
+BF = jnp.bfloat16
+F32 = jnp.float32
+
+
+def swap(value, bit):
+    count = lax.axis_size("dp")
+    return lax.ppermute(value, "dp", [(i, i ^ bit) for i in range(count)])
+
+
+def take(value, index, axis):
+    return lax.dynamic_index_in_dim(value, index, axis, keepdims=False)
+
+
+def ordered(place, mine, theirs, axis):
+    low = jnp.where(place == 0, mine, theirs)
+    high = jnp.where(place == 0, theirs, mine)
+    return jnp.stack([low, high], axis)
+
+
+def added(mine, theirs):
+    return mine.astype(F32) + theirs.astype(F32)
+
+
+def z_routes(turn):
+    pairs = []
+    for plane in range(4):
+        for core in range(2):
+            for z in range(4):
+                picked = (z + turn) % 2
+                source = (plane * 2 + core) * 4 + z
+                target = (plane * 2 + z // 2) * 4 + 2 * core + picked
+                pairs.append((source, target))
+    return pairs
+
+
+def rows_in(value, z):
+    first = lax.ppermute(take(value, z % 2, 0), ("dp", "tensor"), z_routes(0))
+    second = lax.ppermute(take(value, 1 - z % 2, 0), ("dp", "tensor"), z_routes(1))
+    return ordered(z % 2, first, second, 0).reshape(-1, value.shape[-1])
+
+
+def rows_out(half, z):
+    blocks = half.reshape(2, -1, half.shape[-1])
+    back = [[(b, a) for a, b in z_routes(turn)] for turn in range(2)]
+    first = lax.ppermute(take(blocks, z % 2, 0), ("dp", "tensor"), back[0])
+    second = lax.ppermute(take(blocks, 1 - z % 2, 0), ("dp", "tensor"), back[1])
+    return ordered(z % 2, first, second, 0)
+
+
+def plane_rows(half):
+    cut = half.shape[0] // 2
+    upper, lower = half[:cut], half[cut:]
+    upper_x = swap(upper, XBIT)
+    lower_y = swap(lower, YBIT)
+    upper_two = swap(jnp.stack([upper, upper_x]), YBIT)
+    lower_two = swap(jnp.stack([lower, lower_y]), XBIT)
+    return jnp.concatenate(
+        [upper, lower, upper_x, lower_two[0], upper_two[0], lower_y, upper_two[1], lower_two[1]]
+    )
+
+
+def plane_sums(partial_value):
+    blocks = partial_value.astype(BF).reshape(4, 2, -1, partial_value.shape[-1])
+    upper, lower = blocks[:, 0], blocks[:, 1]
+    got = swap(jnp.stack([upper[1], upper[3]]), XBIT)
+    upper_near, upper_far = added(upper[0], got[0]), added(upper[2], got[1])
+    got = swap(jnp.stack([lower[2], lower[3]]), YBIT)
+    lower_near, lower_far = added(lower[0], got[0]), added(lower[1], got[1])
+    upper_sum = added(upper_near, swap(upper_far.astype(BF), YBIT))
+    lower_sum = added(lower_near, swap(lower_far.astype(BF), XBIT))
+    return jnp.concatenate([upper_sum, lower_sum])
+
+
+def narrow_share(grads, place):
+    core, xbit, ybit, z = place
+    count, depth, width = grads.shape[0], grads.shape[1] // 8, grads.shape[2] // 2
+    grid = grads.astype(BF).reshape(count, 2, 2, 2 * depth, 2 * width)
+    left, right = grid[..., :width], grid[..., width:]
+    left = added(take(left, xbit, 2), swap(take(left, 1 - xbit, 2), XBIT)).astype(BF)
+    right = added(take(right, ybit, 1), swap(take(right, 1 - ybit, 1), YBIT)).astype(BF)
+    left = added(take(left, ybit, 1), swap(take(left, 1 - ybit, 1), YBIT)).astype(BF)
+    right = added(take(right, xbit, 1), swap(take(right, 1 - xbit, 1), XBIT)).astype(BF)
+    both = jnp.stack([left, right]).reshape(2, count, 2, depth, width)
+    mine = take(both, core, 2)
+    theirs = swap(take(both, 1 - core, 2), CORE)
+    parts = ordered(core, mine, theirs, 0).reshape(4, count, depth, width)
+    return lax.psum_scatter(parts, "tensor", scatter_dimension=0, tiled=False)
+
+
+def wide_share(grads, place):
+    core, xbit, ybit, z = place
+    count, depth, width = grads.shape[0], grads.shape[1] // 8, grads.shape[2]
+    grid = grads.astype(BF).reshape(count, 2, 2, 2, depth, 4, width // 4)
+    grid = added(take(grid, core, 3), swap(take(grid, 1 - core, 3), CORE)).astype(BF)
+    grid = jnp.moveaxis(grid, 4, 0)
+    grid = lax.psum_scatter(grid, "tensor", scatter_dimension=0, tiled=False)
+    grid = ordered(ybit, take(grid, ybit, 1), swap(take(grid, 1 - ybit, 1), YBIT), 3)
+    grid = ordered(xbit, take(grid, xbit, 1), swap(take(grid, 1 - xbit, 1), XBIT), 3)
+    return grid.reshape(count, depth, width)
+
+
+MESH = pl.DeviceIdType.MESH
+
+
+def spot():
+    dp, z = lax.axis_index("dp"), lax.axis_index("tensor")
+    return dp, dp // 2, dp % 2, z
+
+
+def greet(devices):
+    barrier = pltpu.get_barrier_semaphore()
+    for dp, z in devices:
+        pl.semaphore_signal(
+            barrier, inc=1, device_id={"dp": dp, "tensor": z}, device_id_type=MESH
+        )
+    pl.semaphore_wait(barrier, len(devices))
+
+
+def flip(dp, bit):
+    bits = {1: dp % 2, 2: dp // 2 % 2, 4: dp // 4 % 2}
+    return dp + bit * (1 - 2 * bits[bit])
+
+
+def plane_mates(dp, z):
+    return [(flip(dp, 2), z), (flip(dp, 4), z), (flip(flip(dp, 2), 4), z)]
+
+
+def column_mates(dp, z):
+    mates = [(flip(dp, 1), z)]
+    for step in range(1, 4):
+        far = lax.rem(z + step, 4)
+        mates += [(dp, far), (flip(dp, 1), far)]
+    return mates
+
+
+def push(source, target, send, recv, device):
+    dp, z = device
+    return pltpu.make_async_remote_copy(
+        src_ref=source,
+        dst_ref=target,
+        send_sem=send,
+        recv_sem=recv,
+        device_id={"dp": dp, "tensor": z},
+        device_id_type=MESH,
+    )
+
+
+def first_kernel(
+    rows_ref, wide_ref, seq_ref, block_ref, send_a, recv_a, send_b, recv_b, send_c, recv_c, local
+):
+    dp, plane, core, z = spot()
+    sibling = (flip(dp, 1), z)
+    greet(plane_mates(dp, z) + column_mates(dp, z))
+    home = z // 2 == core
+    for s in range(2):
+        stays = jnp.logical_and(home, z % 2 == s)
+
+        @pl.when(jnp.logical_not(stays))
+        def _(s=s):
+            target = (plane * 2 + z // 2, 2 * core + s)
+            push(rows_ref.at[s], seq_ref.at[z], send_a.at[s], recv_a.at[z % 2], target).start()
+
+        @pl.when(stays)
+        def _(s=s):
+            pltpu.make_async_copy(rows_ref.at[s], seq_ref.at[z], local.at[0]).start()
+
+    wide = []
+    for slot, mate in enumerate(plane_mates(dp, z)):
+        copy = push(
+            wide_ref.at[:, mate[0] // 2],
+            block_ref.at[:, plane],
+            send_b.at[slot],
+            recv_b.at[slot],
+            mate,
+        )
+        copy.start()
+        wide.append(copy)
+    own = pltpu.make_async_copy(wide_ref.at[:, plane], block_ref.at[:, plane], local.at[1])
+    own.start()
+    for j in range(2):
+        block = 2 * core + j
+        stays = jnp.logical_and(home, block == z)
+
+        @pl.when(stays)
+        def _(block=block):
+            pltpu.make_async_copy(rows_ref.at[0], seq_ref.at[block], local.at[0]).wait()
+
+        @pl.when(jnp.logical_not(stays))
+        def _(block=block, j=j):
+            push(rows_ref.at[0], seq_ref.at[block], send_a.at[0], recv_a.at[j], sibling).wait_recv()
+
+        push(seq_ref.at[block], seq_ref.at[block], send_c.at[j], recv_c.at[j], sibling).start()
+    for j in range(2):
+        mine, other = 2 * core + j, 2 * (1 - core) + j
+        push(seq_ref.at[mine], seq_ref.at[mine], send_c.at[j], recv_c.at[j], sibling).wait_send()
+        push(seq_ref.at[other], seq_ref.at[other], send_c.at[j], recv_c.at[j], sibling).wait_recv()
+    for s in range(2):
+        stays = jnp.logical_and(home, z % 2 == s)
+
+        @pl.when(jnp.logical_not(stays))
+        def _(s=s):
+            push(rows_ref.at[s], seq_ref.at[z], send_a.at[s], recv_a.at[0], sibling).wait_send()
+
+    for copy in wide:
+        copy.wait()
+    own.wait()
+
+
+def any_specs(count):
+    return [pl.BlockSpec(memory_space=pl.ANY)] * count
+
+
+def near_specs(count):
+    return [pl.BlockSpec(memory_space=pltpu.VMEM)] * count
+
+
+ROOM = 56 << 20
+
+
+def dma(*shape):
+    return pltpu.SemaphoreType.DMA(shape)
+
+
+def first_moves(rows, wide):
+    _, height, width = rows.shape
+    return pl.pallas_call(
+        first_kernel,
+        out_shape=[
+            jax.ShapeDtypeStruct((4, height, width), BF),
+            jax.ShapeDtypeStruct(wide.shape, BF),
+        ],
+        in_specs=near_specs(2),
+        out_specs=any_specs(2),
+        scratch_shapes=[dma(2), dma(2), dma(3), dma(3), dma(2), dma(2), dma(2)],
+        compiler_params=pltpu.CompilerParams(
+            collective_id=1, has_side_effects=True, vmem_limit_bytes=ROOM
+        ),
+        name="first_moves",
+    )(rows, wide)
+
+
+def narrow_kernel(shard_ref, whole_ref, send_s, recv_s, send_z, recv_z, send_p, recv_p, local, *, groups):
+    dp, plane, core, z = spot()
+    width = shard_ref.shape[2]
+    sibling = (flip(dp, 1), z)
+    xmate, ymate, far = plane_mates(dp, z)
+    lines = [(dp, lax.rem(z + step, 4)) for step in range(1, 4)]
+    greet([sibling, xmate, ymate] + lines)
+    home = z // 2 == core
+    above, below = (dp, z + 1), (dp, z - 1)
+
+    def columns(which):
+        return pl.ds(pl.multiple_of(which * width, width), width)
+
+    for g, (low, count) in enumerate(groups):
+        piece = shard_ref.at[pl.ds(low, count)]
+
+        @pl.when(home)
+        def _(g=g, low=low, count=count, piece=piece):
+            spot_ref = whole_ref.at[pl.ds(low, count), plane, core, :, columns(z % 2)]
+            pltpu.make_async_copy(piece, spot_ref, local.at[g]).start()
+
+        @pl.when(jnp.logical_not(home))
+        def _(g=g, low=low, count=count, piece=piece):
+            spot_ref = whole_ref.at[pl.ds(low, count), plane, core, :, columns(z % 2)]
+            push(piece, spot_ref, send_s.at[g], recv_s.at[g], sibling).start()
+
+    near = jnp.where(core == 0, jnp.where(z >= 1, 1, 0), jnp.where(z <= 2, 0, 1))
+
+    def area(g, which, chip):
+        low, count = groups[g]
+        return whole_ref.at[pl.ds(low, count), chip, :, :, columns(which)]
+
+    def order(turn):
+        return near if turn == 0 else 1 - near
+
+    def on_z(g, turn, act):
+        which = order(turn)
+        source_z = 2 * core + which
+        spot_ref = area(g, which, plane)
+        for way, (wanted, target) in enumerate(
+            [
+                (jnp.logical_and(z >= source_z, z < 3), above),
+                (jnp.logical_and(z <= source_z, z > 0), below),
+            ]
+        ):
+
+            @pl.when(wanted)
+            def _(way=way, target=target):
+                act(push(spot_ref, spot_ref, send_z.at[g, which, way], recv_z.at[g, which], target))
+
+    def arrive(g, turn):
+        which = order(turn)
+        source_z = 2 * core + which
+        low, count = groups[g]
+
+        @pl.when(z == source_z)
+        def _():
+            mine = whole_ref.at[pl.ds(low, count), plane, core, :, columns(which)]
+            other = whole_ref.at[pl.ds(low, count), plane, 1 - core, :, columns(which)]
+            pltpu.make_async_copy(shard_ref.at[pl.ds(low, count)], mine, local.at[g]).wait()
+            push(mine, other, send_s.at[g], recv_s.at[g], sibling).wait_recv()
+
+        @pl.when(z != source_z)
+        def _():
+            spot_ref = area(g, which, plane)
+            push(spot_ref, spot_ref, send_z.at[g, which, 0], recv_z.at[g, which], sibling).wait_recv()
+
+    def hop(g, turn, chip, slot, mate):
+        spot_ref = area(g, order(turn), chip)
+        return push(spot_ref, spot_ref, send_p.at[g, turn, slot], recv_p.at[g, turn, slot], mate)
+
+    mates = (xmate, ymate)
+
+    def spread(g, turn):
+        arrive(g, turn)
+        on_z(g, turn, lambda copy: copy.start())
+        hop(g, turn, plane, turn, mates[turn]).start()
+        hop(g, turn, plane, 1 - turn, mates[1 - turn]).start()
+
+    def relay(g, turn):
+        chip = mates[turn][0] // 2
+        hop(g, turn, chip, turn, mates[turn]).wait_recv()
+        hop(g, turn, chip, 2, mates[1 - turn]).start()
+
+    count = len(groups)
+    spread(0, 0)
+    spread(0, 1)
+    for g in range(count):
+        relay(g, 0)
+        if g + 1 < count:
+            spread(g + 1, 0)
+        relay(g, 1)
+        if g + 1 < count:
+            spread(g + 1, 1)
+    for g in range(count):
+        for turn in range(2):
+            hop(g, turn, mates[1 - turn][0] // 2, 1 - turn, mates[1 - turn]).wait_recv()
+            hop(g, turn, far[0] // 2, 2, mates[1 - turn]).wait_recv()
+            for slot in range(3):
+                hop(g, turn, plane, slot, xmate).wait_send()
+            on_z(g, turn, lambda copy: copy.wait_send())
+        low, size = groups[g]
+
+        @pl.when(jnp.logical_not(home))
+        def _(g=g, low=low, size=size):
+            piece = shard_ref.at[pl.ds(low, size)]
+            push(piece, piece, send_s.at[g], recv_s.at[g], sibling).wait_send()
+
+
+def narrow_moves(shard, groups):
+    count, depth, width = shard.shape
+    parts = len(groups)
+    whole = pl.pallas_call(
+        functools.partial(narrow_kernel, groups=groups),
+        out_shape=jax.ShapeDtypeStruct((count, 4, 2, depth, 2 * width), BF),
+        in_specs=near_specs(1),
+        out_specs=pl.BlockSpec(memory_space=pl.ANY),
+        scratch_shapes=[
+            dma(parts),
+            dma(parts),
+            dma(parts, 2, 2),
+            dma(parts, 2),
+            dma(parts, 2, 3),
+            dma(parts, 2, 3),
+            dma(parts),
+        ],
+        compiler_params=pltpu.CompilerParams(
+            collective_id=2, has_side_effects=True, vmem_limit_bytes=ROOM
+        ),
+        name="narrow_moves",
+    )(shard)
+    return whole.reshape(count, 8 * depth, 2 * width)
+
+
+def second_kernel(
+    rows_ref, quarter_ref, all_ref, wide_ref, send_r, recv_r, send_w, recv_w, local, held, held_sem
+):
+    dp, plane, core, z = spot()
+    sibling = (flip(dp, 1), z)
+    xmate, ymate, far = plane_mates(dp, z)
+    greet([sibling, xmate, ymate])
+    width = quarter_ref.shape[4]
+
+    def rows(source, chip, part, slot, mate):
+        return push(source, all_ref.at[chip, part], send_r.at[slot], recv_r.at[slot], mate)
+
+    own = [
+        rows(rows_ref.at[0], 1, 0, 0, xmate),
+        rows(rows_ref.at[1], 2, 1, 1, ymate),
+        rows(rows_ref.at[0], 2, 0, 2, ymate),
+        rows(rows_ref.at[1], 1, 1, 3, xmate),
+    ]
+    for copy in own:
+        copy.start()
+    wide, loads = [], []
+    for block in range(4):
+        columns = pl.ds(block * width, width)
+        target = wide_ref.at[:, :, core, :, columns]
+        loads.append(pltpu.make_async_copy(quarter_ref.at[block], held.at[block], held_sem.at[block]))
+        wide.append(pltpu.make_async_copy(held.at[block], target, local.at[block]))
+        wide.append(push(held.at[block], target, send_w.at[block], recv_w.at[block], sibling))
+    for copy in loads:
+        copy.start()
+    keep = pltpu.make_async_copy(rows_ref, all_ref.at[0], local.at[4])
+    keep.start()
+    for block in range(4):
+        loads[block].wait()
+        wide[2 * block].start()
+        wide[2 * block + 1].start()
+    own[0].wait_recv()
+    upper = rows(all_ref.at[1, 0], 3, 0, 4, ymate)
+    upper.start()
+    own[1].wait_recv()
+    lower = rows(all_ref.at[2, 1], 3, 1, 5, xmate)
+    lower.start()
+    own[2].wait_recv()
+    own[3].wait_recv()
+    for copy in own:
+        copy.wait_send()
+    upper.wait()
+    lower.wait()
+    keep.wait()
+    for block in range(4):
+        columns = pl.ds(block * width, width)
+        wide[2 * block].wait()
+        wide[2 * block + 1].wait_send()
+        theirs = wide_ref.at[:, :, 1 - core, :, columns]
+        push(theirs, theirs, send_w.at[block], recv_w.at[block], sibling).wait_recv()
+
+
+def second_moves(rows, quarter):
+    blocks, count, chips, depth, width = quarter.shape
+    return pl.pallas_call(
+        second_kernel,
+        out_shape=[
+            jax.ShapeDtypeStruct((4, *rows.shape), BF),
+            jax.ShapeDtypeStruct((count, chips, 2, depth, blocks * width), BF),
+        ],
+        in_specs=near_specs(1) + any_specs(1),
+        out_specs=any_specs(2),
+        scratch_shapes=[
+            dma(6),
+            dma(6),
+            dma(4),
+            dma(4),
+            dma(5),
+            pltpu.VMEM(quarter.shape, BF),
+            dma(4),
+        ],
+        compiler_params=pltpu.CompilerParams(
+            collective_id=3, has_side_effects=True, vmem_limit_bytes=ROOM
+        ),
+        name="second_moves",
+    )(rows, quarter)
+
+
+def chip_shards(
+    inputs,
+    context,
+    lengths,
+    cotangent,
+    self_qkv,
+    self_out,
+    cross_query,
+    cross_context,
+    cross_out,
+    gate_up,
+    down_proj,
+    norm_gains,
+):
+    dp, z = lax.axis_index("dp"), lax.axis_index("tensor")
+    core, xbit, ybit = dp & 1, (dp >> 1) & 1, (dp >> 2) & 1
+    place = (core, xbit, ybit, z)
+    model_width = inputs.shape[-1]
+    padded = inputs.shape[1] * 4
+    half_rows = padded // 2
+
+    def sibling_owned(value):
+        mine = take(value, z % 2, 0)
+        return jnp.where(core == z // 2, mine, swap(mine, CORE))
+
+    def own_half(value):
+        return take(value.reshape(2, half_rows, -1), core, 0)
+
+    def both_halves(mine, theirs):
+        return ordered(core, mine, theirs, 0).reshape(padded, -1)
+
+    pair_sum = lambda value: value + swap(value.astype(BF), CORE).astype(F32)
+
+    cc_depth = cross_context.shape[1]
+    narrow = jnp.concatenate(
+        [
+            self_qkv,
+            self_out.T[None],
+            cross_query[None],
+            cross_context.reshape(1, 2 * cc_depth, -1),
+            cross_out.T[None],
+        ]
+    ).astype(BF)
+    depth, units = gate_up.shape[1], gate_up.shape[2]
+    wide = jnp.concatenate([gate_up, down_proj.T[None]]).astype(BF)
+    wide = jnp.moveaxis(wide.reshape(3, depth, 4, units // 4), 2, 1)
+    sequence, wide = first_moves(inputs, wide)
+    quarter = lax.all_gather(wide, "tensor", axis=0)
+    stream = sequence.reshape(padded, model_width).astype(F32)
+    length = sibling_owned(lengths[:, None])[0]
+    cond = sibling_owned(context)
+    narrow_all = narrow_moves(narrow, ((0, 3), (3, 4)))
+    qkv_whole, so_whole, cq_whole, co_whole = narrow_all[:3], narrow_all[3], narrow_all[4], narrow_all[6]
+    cc_whole = narrow_all[5].reshape(8, 2, cc_depth, -1)
+    cc_whole = jnp.moveaxis(cc_whole, 1, 0).reshape(2, 8 * cc_depth, -1)
+    cot_half = rows_in(cotangent, z)
+    cot = both_halves(cot_half, swap(cot_half, CORE)).astype(F32)
+
+    positions = jnp.arange(padded, dtype=jnp.int32)
+    key_valid = positions < length
+    row_keep = key_valid.astype(F32)[:, None]
+    keep_half = own_half(row_keep)
+    context_valid = jnp.ones((cond.shape[0],), dtype=jnp.bool_)
+
+    normed_one, scaled_one, inverse_one = norm_rows(stream, norm_gains[0])
+    normed_one = normed_one.astype(BF)
+    qkv = jnp.einsum("td,kde->kte", normed_one, qkv_whole, preferred_element_type=F32).astype(BF)
+    mixed_one, logsum_one = attend_forward((qkv[0], qkv[1], qkv[2], key_valid))
+    branch = jnp.einsum("te,de->td", mixed_one, so_whole, preferred_element_type=F32)
+    stream = stream + row_keep * pair_sum(branch)
+    normed_two, scaled_two, inverse_two = norm_rows(stream, norm_gains[1])
+    normed_two = normed_two.astype(BF)
+    cross_rows = jnp.einsum("td,de->te", normed_two, cq_whole, preferred_element_type=F32).astype(BF)
+    cond_rows = jnp.einsum("sd,kde->kse", cond, cc_whole, preferred_element_type=F32).astype(BF)
+    mixed_two, logsum_two = attend_forward((cross_rows, cond_rows[0], cond_rows[1], context_valid))
+    branch = jnp.einsum("te,de->td", mixed_two, co_whole, preferred_element_type=F32)
+    stream = stream + row_keep * pair_sum(branch)
+    stream_half = own_half(stream)
+    normed_three, scaled_three, inverse_three = norm_rows(stream_half, norm_gains[2])
+    rows_three, wide_all = second_moves(
+        normed_three.astype(BF).reshape(2, -1, model_width), quarter
+    )
+    rows_three = rows_three.reshape(-1, model_width)
+    wide_all = wide_all.reshape(3, model_width, units)
+    gu_whole, down_whole = wide_all[:2], wide_all[2]
+    gate_rows = jnp.einsum("td,kde->kte", rows_three, gu_whole, preferred_element_type=F32)
+    sigmoid_gate = jax.nn.sigmoid(gate_rows[0])
+    hidden = (gate_rows[0] * sigmoid_gate * gate_rows[1]).astype(BF)
+
+    grad_stream = row_keep * cot
+    grad_branch = plane_rows((keep_half * own_half(grad_stream)).astype(BF))
+    grad_hidden = jnp.einsum("td,df->tf", grad_branch, down_whole, preferred_element_type=F32)
+    grad_gate = (
+        grad_hidden * gate_rows[1] * sigmoid_gate * (1.0 + gate_rows[0] * (1.0 - sigmoid_gate))
+    )
+    grad_upper = grad_hidden * gate_rows[0] * sigmoid_gate
+    grad_expand = jnp.stack([grad_gate, grad_upper]).astype(BF)
+    partial_value = jnp.einsum("ktf,kdf->td", grad_expand, gu_whole, preferred_element_type=F32)
+    grad_norm, gain_rows = norm_back(
+        plane_sums(partial_value), scaled_three, inverse_three, norm_gains[2]
+    )
+    gain_three = jnp.sum(gain_rows, axis=0)
+    branch = jnp.einsum("tf,df->td", hidden, down_whole, preferred_element_type=F32)
+    stream_half = stream_half + keep_half * plane_sums(branch)
+    output = rows_out((keep_half * stream_half).astype(BF), z)
+    grad_down = jnp.einsum("td,tf->df", grad_branch, hidden, preferred_element_type=F32)
+    grad_gates = jnp.einsum("td,ktf->kdf", rows_three, grad_expand, preferred_element_type=F32)
+    grad_gates = wide_share(grad_gates, place)
+    grad_down = wide_share(grad_down[None], place)[0]
+
+    grad_stream = grad_stream + both_halves(grad_norm, swap(grad_norm.astype(BF), CORE).astype(F32))
+    grad_branch = (row_keep * grad_stream).astype(BF)
+    grad_mixed = jnp.einsum("td,de->te", grad_branch, co_whole, preferred_element_type=F32).astype(BF)
+    grad_query, grad_key, grad_value = attend_backward(
+        (cross_rows, cond_rows[0], cond_rows[1], logsum_two, grad_mixed, context_valid)
+    )
+    partial_value = jnp.einsum("te,de->td", grad_query, cq_whole, preferred_element_type=F32)
+    grad_norm, gain_rows = norm_back(
+        pair_sum(partial_value), scaled_two, inverse_two, norm_gains[1]
+    )
+    gain_two = 0.5 * jnp.sum(gain_rows, axis=0)
+    grad_merge = jnp.einsum("td,te->de", grad_branch, mixed_two, preferred_element_type=F32)
+    grad_cross = jnp.einsum("td,te->de", normed_two, grad_query, preferred_element_type=F32)
+    grad_pairs = jnp.stack([grad_key, grad_value])
+    grad_cc = jnp.einsum("sd,kse->kde", cond, grad_pairs, preferred_element_type=F32)
+    grad_cc = jnp.moveaxis(grad_cc.reshape(2, 8, cc_depth, -1), 0, 1).reshape(model_width, -1)
+    crossed = narrow_share(
+        jnp.stack([grad_merge.astype(BF), grad_cross.astype(BF), grad_cc.astype(BF)]), place
+    )
+    context_part = jnp.einsum("kse,kde->sd", grad_pairs, cc_whole, preferred_element_type=F32)
+    context_all = lax.all_gather(pair_sum(context_part).astype(BF), "tensor", axis=0)
+    grad_context = take(context_all.reshape(2, 2, *context_part.shape), core, 0).astype(F32)
+
+    grad_stream = grad_stream + grad_norm
+    grad_branch = (row_keep * grad_stream).astype(BF)
+    grad_mixed = jnp.einsum("td,de->te", grad_branch, so_whole, preferred_element_type=F32).astype(BF)
+    grad_after = jnp.einsum("td,te->de", grad_branch, mixed_one, preferred_element_type=F32)
+    after = narrow_share(grad_after.astype(BF)[None], place)[0]
+    grad_triple = jnp.stack(
+        attend_backward((qkv[0], qkv[1], qkv[2], logsum_one, grad_mixed, key_valid))
+    )
+    grad_self = jnp.einsum("td,kte->kde", normed_one, grad_triple, preferred_element_type=F32)
+    selfed = narrow_share(grad_self, place)
+    partial_value = jnp.einsum("kte,kde->td", grad_triple, qkv_whole, preferred_element_type=F32)
+    grad_norm, gain_rows = norm_back(
+        pair_sum(partial_value), scaled_one, inverse_one, norm_gains[0]
+    )
+    gain_one = 0.5 * jnp.sum(gain_rows, axis=0)
+    grad_inputs = rows_out(own_half(grad_stream + grad_norm).astype(BF), z).astype(F32)
+    gains = lax.psum(jnp.stack([gain_one, gain_two, gain_three]), ("dp", "tensor"))
+    gains = lax.dynamic_slice_in_dim(gains, dp * (model_width // 8), model_width // 8, 1)
+    return (
+        output,
+        grad_inputs,
+        grad_context,
+        selfed.astype(F32),
+        after.T.astype(F32),
+        crossed[1].astype(F32),
+        crossed[2].reshape(2, cc_depth, -1).astype(F32),
+        crossed[0].T.astype(F32),
+        grad_gates.astype(F32),
+        grad_down.T.astype(F32),
+        gains,
+    )
+
+
 def solution(mesh):
+    sizes = (mesh.shape["dp"], mesh.shape["tensor"])
+    body = chip_shards if sizes == (8, 4) else shards
     placed = (
         P("dp", "tensor", None),
         P("dp", None, None),
@@ -344,7 +974,7 @@
         P(),
     )
     return jax.shard_map(
-        shards,
+        body,
         mesh=mesh,
         in_specs=placed,
         out_specs=(

time: 1800 us -> 1100 us (0.61)
  waiting for transfers between devices: 1360 us -> 85.2 us
  Pallas kernels: 0 us -> 237 us
  starting transfers between devices: 2.33 us -> 107 us
  local copies, waits for them, and re-layouts: 138 us -> 236 us
  blocking collectives: 11.7 us -> 98.6 us
  other arithmetic: 58.2 us -> 121 us
  matrix products: 203 us -> 184 us
    all_gather x13 -> x1, waiting for transfers between devices: 508 us -> 0.01 us  [chip_shards(): quarter = lax.all_gather(wide, 'tensor', axis=0)]
    reduce_scatter x7 -> x4, waiting for transfers between devices: 449 us -> 0.01 us  [the longest x3 0.01 us: narrow_share(): return lax.psum_scatter(parts, 'tensor', scatter_dimension=0, tiled=False)]
    unnamed x33 -> x7, waiting for transfers between devices: 398 us -> 0.1 us
    pallas_call x0 -> x3, Pallas kernels: none -> 237 us  [the longest x1 177 us: narrow_moves(): pl.pallas_call(functools.partial(narrow_kernel, groups=groups), out_shape...]
    ppermute x0 -> x48, starting transfers between devices: none -> 107 us  [the longest x42 93.8 us: swap(): return lax.ppermute(value, 'dp', [(i, i ^ bit) for i in range(count)])]
    ppermute x0 -> x48, waiting for transfers between devices: none -> 85.1 us  [the longest x42 84.8 us: swap(): return lax.ppermute(value, 'dp', [(i, i ^ bit) for i in range(count)])]
    psum x1, blocking collectives: 11.7 us -> 64.4 us  [chip_shards(): lax.psum(jnp.stack([gain_one, gain_two, gain_three]), ('dp', 'tensor'))]
    reshape x0 -> x3, local copies, waits for them, and re-layouts: none -> 40.5 us  [the longest x2 25.5 us: wide_share(): grid = grads.astype(BF).reshape(count, 2, 2, 2, depth, 4, width // 4)]
  transfers between devices with their start and end apart: 27 -> 54, of which waited for: 23 -> 13; matrix products, arithmetic and copies ran while one was open for 16% -> 39% of each run, Pallas kernels for 0% -> 19%
where the time goes in v1:
time: 1100 us; the launch traced here: 1090 us
  Pallas kernels  237 us (22%)
  local copies, waits for them, and re-layouts  236 us (21%)
  matrix products  184 us (17%)
  other arithmetic  121 us (11%)
  starting transfers between devices  107 us (10%)
  blocking collectives  98.6 us (9%)
  waiting for transfers between devices  85.2 us (8%)
  between operations  18.5 us (2%)
    pallas_call x1, Pallas kernels, narrow_moves(): pl.pallas_call(functools.partial(narrow_kernel, groups=groups), out_shape...  177 us
    ppermute x42, starting transfers between devices, swap(): return lax.ppermute(value, 'dp', [(i, i ^ bit) for i in range(count)])  93.8 us
    ppermute x42, waiting for transfers between devices, swap(): return lax.ppermute(value, 'dp', [(i, i ^ bit) for i in range(count)])  84.8 us
    psum x1, blocking collectives, chip_shards(): lax.psum(jnp.stack([gain_one, gain_two, gain_three]), ('dp', 'tensor'))  64.4 us
    unnamed x254, local copies, waits for them, and re-layouts  56.2 us
    dynamic_slice x9, local copies, waits for them, and re-layouts, take(): return lax.dynamic_index_in_dim(value, index, axis, keepdims=False)  38 us
    all_gather x1, blocking collectives, chip_shards(): lax.all_gather(pair_sum(context_part).astype(BF), 'tensor', axis=0)  34.2 us
    pallas_call x1, Pallas kernels, second_moves(): pl.pallas_call(second_kernel, out_shape=[jax.ShapeDtypeStruct((4, *rows.s...  31.2 us
  transfers between devices with their start and end apart: 54, of which 13 were waited for; matrix products, arithmetic and copies ran while one was open for 39% of the time, Pallas kernels for 19%

profile of v1, /device:TPU:0, one launch (start us, length us, event | category | flops | bytes accessed | tf_op | source)
XLA Modules:
  0.0 1087.5 jit_solution(18281490046781262757)
XLA Ops:
  11.9 4.9 collective-permute-start.10
  16.8 3.0 collective-permute-start.11
  24.9 28.6 %first_moves.1 = (bf16[4,136,1536]{2,1,0:T(8,128)(2,1)}, bf16[3,4,192,384]{3,2,1,0:T(8,128)(2,1)}) custom-call(bf16[2,136,1536]{2,1,0:T(8,128)(2,1)} %rows_ref.1, bf16[3,4,192,384]{3,2,1,0:T(8,128)(2,1)} %maximum_bitcast_fusion.wide_ref), custom_call_target="tpu_custom_call" | custom-call | tf_op jit(solution)/shard_map/first_moves/pallas_call | solution.py:561
  58.3 177.0 %narrow_moves.1 = bf16[7,4,2,192,768]{4,3,2,1,0:T(8,128)(2,1)} custom-call(bf16[7,192,384]{2,1,0:T(8,128)(2,1)} %copy-done.57), custom_call_target="tpu_custom_call" | custom-call | tf_op jit(solution)/shard_map/narrow_moves/pallas_call | solution.py:689
  235.3 6.5 slice.247
  241.9 6.9 fusion.122
  251.3 7.3 convert_bitcast_fusion.1
  266.4 3.2 copy.251
  271.0 5.0 fusion.118
  276.0 4.1 fusion
  281.8 4.4 fusion.52
  288.0 52.7 %collective-permute-start.12 = (bf16[272,1536]{1,0:T(8,128)(2,1)S(1)}, bf16[272,1536]{1,0:T(8,128)(2,1)}, u32[]{:S(2)}, u32[]{:S(2)}) collective-permute-start(bf16[272,1536]{1,0:T(8,128)(2,1)S(1)} %bitcast.685), channel_id=1, source_target_pairs={{0,4},{4,0},{8,12},{12,8},{16,20},{20,16},{24,28},{28,24},{1,5},{5... | collective-permute-start | bytes 2506760 | tf_op jit(solution)/shard_map/ppermute | solution.py:342
  340.7 4.1 fusion.128
  357.4 3.1 maximum_convert_fusion
  360.5 4.0 collective-permute-done.13
  371.7 4.0 multiply_add_fusion.2
  403.2 31.2 %second_moves.1 = (bf16[4,2,136,1536]{3,2,1,0:T(8,128)(2,1)}, bf16[3,4,2,192,1536]{4,3,2,1,0:T(8,128)(2,1)}) custom-call(bf16[2,136,1536]{2,1,0:T(8,128)(2,1)} %multiply_convert_fusion.13.rows_ref, bf16[4,3,4,192,384]{4,3,2,1,0:T(8,128)(2,1)} %bitcast.668), custom_call_target="tpu_custom_call" | custom-call | tf_op jit(solution)/shard_map/second_moves/pallas_call | solution.py:769
  434.5 4.8 slice.265
  439.3 8.1 slice.261
  447.5 17.1 %convolution_bitcast_fusion = f32[2,1088,1536]{2,1,0:T(8,128)} fusion(bf16[1088,1536,1]{1,0,2:T(8,128)(2,1)} %bitcast.730, bf16[2,1536,1536]{2,1,0:T(8,128)(2,1)} %bitcast.644), kind=kOutput, calls=%fused_computation.7 | convolution fusion | flops 10267656192 | bytes 26148864 | tf_op jit(solution)/shard_map/td,kde->kte/dot_general | solution.py:878
  464.6 10.0 convolution_convert_fusion.2
  474.6 13.0 %fusion.31 = (bf16[1,1088,1536]{2,1,0:T(8,128)(2,1)}, bf16[1,1088,1536]{2,1,0:T(8,128)(2,1)}) fusion(f32[2,1088,1536]{2,1,0:T(8,128)} %convolution_bitcast_fusion, bf16[1088,1536]{1,0:T(8,128)(2,1)} %fusion.87, bf16[1536,1536]{1,0:T(8,128)(2,1)S(1)} %bitcast.676), kind=kOutput, calls=%fused_computation.87 | convolution fusion | flops 5155553280 | bytes 28114944 | tf_op jit(solution)/shard_map/td,df->tf/dot_general | solution.py:884
  487.6 12.3 %convolution_convert_fusion.1 = bf16[1536,1536]{1,0:T(8,128)(2,1)} fusion(bf16[1088,1536]{1,0:T(8,128)(2,1)} %fusion.87, f32[2,1088,1536]{2,1,0:T(8,128)} %convolution_bitcast_fusion), kind=kOutput, calls=%fused_computation.18 | convolution fusion | flops 5146214400 | bytes 21430272 | tf_op jit(solution)/shard_map/td,tf->df/dot_general | solution.py:898
  500.0 13.6 %fusion.8 = bf16[1088,1536]{1,0:T(8,128)(2,1)} fusion(bf16[2,1536,1536]{2,1,0:T(8,128)(2,1)S(1)} %bitcast.647, bf16[1,1088,1536]{2,1,0:T(8,128)(2,1)} %get-tuple-element.39, bf16[1,1088,1536]{2,1,0:T(8,128)(2,1)S(1)} %copy-done.113), kind=kOutput, calls=%fused_computation.17 | convolution fusion | flops 10272669696 | bytes 19464192 | tf_op jit(solution)/shard_map/ktf,kdf->td/dot_general | solution.py:890
  513.6 17.4 %fusion.3 = bf16[2,1536,1536]{1,2,0:T(8,128)(2,1)} fusion(bf16[1088,1536,1]{1,0,2:T(8,128)(2,1)S(1)} %bitcast.731, bf16[1,1088,1536]{2,1,0:T(8,128)(2,1)} %get-tuple-element.39, bf16[1,1088,1536]{2,1,0:T(8,128)(2,1)S(1)} %copy-done.113), kind=kOutput, calls=%fused_computation.12 | convolution fusion | flops 10275717120 | bytes 19464192 | tf_op jit(solution)/shard_map/td,ktf->kdf/dot_general | solution.py:899
  535.1 12.7 %copy.273 = bf16[2,1536,1536]{2,1,0:T(8,128)(2,1)} copy(bf16[2,1536,1536]{1,2,0:T(8,128)(2,1)} %fusion.3) | data formatting | bytes 18874368 | tf_op jit(solution)/shard_map/convert_element_type | solution.py:428
  547.8 16.4 %reshape.724 = bf16[2,2,2,2,192,4,384]{6,5,4,3,2,1,0:T(4,128)(2,1)} reshape(bf16[2,1536,1536]{2,1,0:T(8,128)(2,1)} %copy.273) | data formatting | bytes 18874368 | tf_op jit(solution)/shard_map/reshape | solution.py:428
  564.2 9.0 reshape.725
  582.5 10.8 constant_dynamic-slice_fusion.4
  593.3 5.6 copy.322
  603.8 9.3 collective-permute-done.5
  616.0 5.1 collective-permute-done.18
  627.0 6.3 collective-permute-done.20
  639.2 3.6 fusion.33
  651.4 3.3 fusion.58
  662.3 4.1 fusion.130
  668.9 7.1 collective-permute-start.22
  693.8 3.7 convolution_convert_fusion.5
  698.2 12.4 %multiply_reduce_fusion = (f32[12,544]{1,0:T(8,128)S(1)}, f32[12,544,544]{1,2,0:T(8,128)}) fusion(f32[12,544]{1,0:T(8,128)S(1)} %copy-done.77, f32[12,544,544]{1,2,0:T(8,128)} %copy-done.2, pred[544]{0:T(1024)(128)(4,1)S(1)} %copy-done.104, bf16[544,12,64]{0,2,1:T(8,128)(2,1)S(1)} %bitcast.680, bf16[544,12,64]{0,2,1:T(8,128)(2,1)S(1)} %bitcast.678), kind=kOutput, calls=%fused_computation.1 | convolution fusion | flops 472307328 | bytes 30133792 | tf_op jit(solution)/shard_map/qhd,khd->hqk/dot_general | solution.py:66
  712.0 12.5 %multiply_convert_fusion = bf16[12,544,544]{1,2,0:T(8,128)(2,1)S(1)} fusion(f32[12,544,544]{1,2,0:T(8,128)} %get-tuple-element.129, f32[12,544]{1,0:T(8,128)S(1)} %get-tuple-element.128, f32[12,544]{1,0:T(8,128)S(1)} %copy-done.77, f32[12,544,544]{1,2,0:T(8,128)} %copy-done.2, pred[544]{0:T(1024)(128)(4,1)S(1)} %copy-done.104), kind=kLoop, calls=%fused_computation | loop fusion | flops 21307392 | bytes 35565088 | tf_op jit(solution)/shard_map/convert_element_type | solution.py:68
  728.9 10.8 fusion.54
  739.8 6.0 fusion.20
  755.2 10.2 bitcast_convert_fusion
  778.4 17.7 %collective-permute-done.33 = bf16[1,384,384]{2,1,0:T(8,128)(2,1)S(1)} collective-permute-done((bf16[1,384,384]{2,1,0:T(8,128)(2,1)S(1)}, bf16[1,384,384]{2,1,0:T(8,128)(2,1)S(1)}, u32[]{:S(2)}, u32[]{:S(2)}) %collective-permute-start.33) | collective-permute-done | bytes 294944 | tf_op jit(solution)/shard_map/ppermute | solution.py:342
  803.2 4.5 multiply_reduce_fusion.4
  807.8 8.4 convert_bitcast_fusion
  816.1 15.0 %reshape.720 = bf16[3,2,2,384,768]{3,2,1,4,0:T(2,128)(2,1)} reshape(bf16[3,1536,768]{1,2,0:T(8,128)(2,1)} %convert_bitcast_fusion) | data formatting | bytes 14155776 | tf_op jit(solution)/shard_map/reshape | solution.py:412
  831.2 7.1 fusion.124
  838.3 4.2 constant_dynamic-slice_fusion.6
  842.6 6.9 copy.300
  850.5 13.4 %constant_dynamic-slice_fusion.8 = (bf16[3,2,1,384,384]{3,2,1,4,0:T(2,128)(2,1)}, bf16[3,2,1,384,384]{3,2,1,4,0:T(2,128)(2,1)}) fusion(bf16[3,2,2,384,384]{3,2,1,4,0:T(2,128)(2,1)} %get-tuple-element.49, s32[]{:T(128)S(6)} %select_n.303, s32[]{:T(128)S(6)} %select_n.304), kind=kLoop, calls=%fused_computation.342 | loop fusion | bytes 7077896 | tf_op jit(solution)/shard_map/jit(dynamic_index_in_dim)/dynamic_slice | solution.py:346
  863.9 11.4 %copy.297 = bf16[3,2,1,384,384]{4,3,1,0,2:T(8,128)(2,1)} copy(bf16[3,2,1,384,384]{3,2,1,4,0:T(2,128)(2,1)} %get-tuple-element.57) | data formatting | bytes 3538944
  877.3 34.2 %all-gather.2 = bf16[4,130,768]{2,1,0:T(8,128)(2,1)S(1)} all-gather(bf16[1,130,768]{2,1,0:T(8,128)(2,1)S(1)} %fusion.102), channel_id=3, replica_groups=mesh['dp'=8,'tensor'=4] {'tensor'}, dimensions={0}, use_global_device_ids=true | all-gather | bytes 998400 | tf_op jit(solution)/shard_map/all_gather | solution.py:923
  912.8 6.5 copy.299
  919.3 11.3 %copy.296 = bf16[3,2,1,384,384]{4,3,1,0,2:T(8,128)(2,1)} copy(bf16[3,2,1,384,384]{3,2,1,4,0:T(2,128)(2,1)} %get-tuple-element.56) | data formatting | bytes 3538944
  940.6 15.6 %collective-permute-done.30 = bf16[3,384,384]{2,1,0:T(8,128)(2,1)S(1)} collective-permute-done((bf16[3,384,384]{2,1,0:T(8,128)(2,1)S(1)}, bf16[3,384,384]{2,1,0:T(8,128)(2,1)S(1)}, u32[]{:S(2)}, u32[]{:S(2)}) %collective-permute-start.30) | collective-permute-done | bytes 884768 | tf_op jit(solution)/shard_map/ppermute | solution.py:342
  956.4 2.9 collective-permute-done.28
  959.8 2.9 multiply_add_fusion
  963.6 3.7 collective-permute-start.25
  969.0 64.4 %psum.7 = f32[3,1536]{1,0:T(4,128)S(1)} all-reduce(f32[3,1536]{1,0:T(4,128)S(1)} %pad_maximum_fusion.24), channel_id=1, replica_groups=mesh['dp'=8,'tensor'=4] {'dp','tensor'}, use_global_device_ids=true, to_apply=%region_26.27 | all-reduce | flops 4608 | bytes 36864 | tf_op jit(solution)/shard_map/psum | solution.py:942
  1041.7 5.0 collective-permute-done.46
  1049.9 8.1 collective-permute-done.43
  1065.7 7.7 collective-permute-done.44
  1075.5 2.9 reshape.761
  (532 shorter events, 219.7 us)
Async XLA Ops:
  7.2 396.0 %all-gather.5.cloned.1.call-start = ((), (), s32[]{:S(2)}) async-start(), calls=%async_computation.8 | async-start | bytes 8847360 | tf_op jit(solution)/shard_map/all_gather | solution.py:840
  8.5 261.1 %collective-permute-start = (s32[1]{0:T(128)}, s32[1]{0:T(128)}, u32[]{:S(2)}, u32[]{:S(2)}) collective-permute-start(s32[1]{0:T(128)} %squeeze.212), channel_id=1, source_target_pairs={{0,4},{4,0},{8,12},{12,8},{16,20},{20,16},{24,28},{28,24},{1,5},{5... | collective-permute-start | bytes 20 | tf_op jit(solution)/shard_map/ppermute | solution.py:342
  9.5 337.2 %copy-start.58 = (bf16[1,130,768]{2,1,0:T(8,128)(2,1)}, bf16[1,130,768]{2,1,0:T(8,128)(2,1)S(1)}, u32[]{:S(2)}) copy-start(bf16[1,130,768]{2,1,0:T(8,128)(2,1)S(1)} %copy.326) | copy-start | bytes 599044
  9.5 337.2 %collective-permute-start.2 = (bf16[130,768]{1,0:T(8,128)(2,1)S(1)}, bf16[130,768]{1,0:T(8,128)(2,1)}, u32[]{:S(2)}, u32[]{:S(2)}) collective-permute-start(bf16[130,768]{1,0:T(8,128)(2,1)S(1)} %bitcast.710), channel_id=1, source_target_pairs={{0,4},{4,0},{8,12},{12,8},{16,20},{20,16},{24,28},{28,24},{1,5},{5... | collective-permute-start | bytes 599048 | tf_op jit(solution)/shard_map/ppermute | solution.py:342
  11.9 274.4 %collective-permute-start.10 = (bf16[136,1536]{1,0:T(8,128)(2,1)}, bf16[136,1536]{1,0:T(8,128)(2,1)}, u32[]{:S(2)}, u32[]{:S(2)}) collective-permute-start(bf16[136,1536]{1,0:T(8,128)(2,1)} %get-tuple-element.105), channel_id=1, source_target_pairs={{0,0},{1,1},{2,4},{3,5},{4,2},{5,3},{6,6},{7,7},{8,8},{9,9},{10,12... | collective-permute-start | bytes 1253384 | tf_op jit(solution)/shard_map/ppermute | solution.py:372
  16.8 269.5 %collective-permute-start.11 = (bf16[136,1536]{1,0:T(8,128)(2,1)}, bf16[136,1536]{1,0:T(8,128)(2,1)}, u32[]{:S(2)}, u32[]{:S(2)}) collective-permute-start(bf16[136,1536]{1,0:T(8,128)(2,1)} %get-tuple-element.106), channel_id=1, source_target_pairs={{0,1},{1,0},{2,5},{3,4},{4,3},{5,2},{6,7},{7,6},{8,9},{9,8},{10,13... | collective-permute-start | bytes 1253384 | tf_op jit(solution)/shard_map/ppermute | solution.py:373
  53.6 981.9 %reduce-scatter.14.cloned.1.call-start = ((), (), s32[]{:S(2)}) async-start(), calls=%async_computation.7 | async-start | bytes 2949120 | tf_op jit(solution)/shard_map/reduce_scatter | solution.py:431
  250.1 130.6 %copy-start.86 = (f32[1536]{0:T(1024)}, f32[1536]{0:T(1024)S(1)}, u32[]{:S(2)}) copy-start(f32[1536]{0:T(1024)S(1)} %get-tuple-element.30) | copy-start | bytes 18436
  250.1 152.0 %copy-start.82 = (f32[1536]{0:T(1024)}, f32[1536]{0:T(1024)S(1)}, u32[]{:S(2)}) copy-start(f32[1536]{0:T(1024)S(1)} %get-tuple-element.28) | copy-start | bytes 18436
  286.2 58.5 %copy-start.108 = (bf16[12,64,544]{2,1,0:T(8,128)(2,1)}, bf16[12,64,544]{2,1,0:T(8,128)(2,1)S(1)}, u32[]{:S(2)}) copy-start(bf16[12,64,544]{2,1,0:T(8,128)(2,1)S(1)} %fusion.52) | copy-start | bytes 2506756
  286.3 54.4 %copy-start.49 = (bf16[1,4,2,192,768]{4,3,2,1,0:T(8,128)(2,1)S(1)}, bf16[1,4,2,192,768]{4,3,2,1,0:T(8,128)(2,1)}, u32[]{:S(2)}) copy-start(bf16[1,4,2,192,768]{4,3,2,1,0:T(8,128)(2,1)} %get-tuple-element.43) | copy-start | bytes 7077892
  288.0 56.8 %copy-start.44 = (bf16[2,136,1536]{2,1,0:T(8,128)(2,1)}, bf16[2,136,1536]{2,1,0:T(8,128)(2,1)S(1)}, u32[]{:S(2)}) copy-start(bf16[2,136,1536]{2,1,0:T(8,128)(2,1)S(1)} %pad_maximum_fusion.15) | copy-start | bytes 2506756
  288.0 60.9 %collective-permute-start.12 = (bf16[272,1536]{1,0:T(8,128)(2,1)S(1)}, bf16[272,1536]{1,0:T(8,128)(2,1)}, u32[]{:S(2)}, u32[]{:S(2)}) collective-permute-start(bf16[272,1536]{1,0:T(8,128)(2,1)S(1)} %bitcast.685), channel_id=1, source_target_pairs={{0,4},{4,0},{8,12},{12,8},{16,20},{20,16},{24,28},{28,24},{1,5},{5... | collective-permute-start | bytes 2506760 | tf_op jit(solution)/shard_map/ppermute | solution.py:342
  345.5 26.2 %collective-permute-start.1 = (bf16[544,1536]{1,0:T(8,128)(2,1)}, bf16[544,1536]{1,0:T(8,128)(2,1)}, u32[]{:S(2)}, u32[]{:S(2)}) collective-permute-start(bf16[544,1536]{1,0:T(8,128)(2,1)} %get-tuple-element.118), channel_id=1, source_target_pairs={{0,4},{4,0},{8,12},{12,8},{16,20},{20,16},{24,28},{28,24},{1,5},{5... | collective-permute-start | bytes 5013512 | tf_op jit(solution)/shard_map/ppermute | solution.py:342
  346.0 54.8 %copy-start.88 = (f32[544]{0:T(1024)}, f32[544]{0:T(1024)S(1)}, u32[]{:S(2)}) copy-start(f32[544]{0:T(1024)S(1)} %fusion.107) | copy-start | bytes 6532
  352.6 11.9 %collective-permute-start.13 = (bf16[136,1536]{1,0:T(8,128)(2,1)}, bf16[136,1536]{1,0:T(8,128)(2,1)}, u32[]{:S(2)}, u32[]{:S(2)}) collective-permute-start(bf16[136,1536]{1,0:T(8,128)(2,1)} %get-tuple-element.102), channel_id=1, source_target_pairs={{0,8},{4,12},{8,0},{12,4},{16,24},{20,28},{24,16},{28,20},{1,9},{5... | collective-permute-start | bytes 1253384 | tf_op jit(solution)/shard_map/ppermute | solution.py:342
  356.4 11.6 %collective-permute-start.14 = (bf16[136,1536]{1,0:T(8,128)(2,1)}, bf16[136,1536]{1,0:T(8,128)(2,1)S(1)}, u32[]{:S(2)}, u32[]{:S(2)}) collective-permute-start(bf16[136,1536]{1,0:T(8,128)(2,1)} %get-tuple-element.101), channel_id=1, source_target_pairs={{0,16},{4,20},{8,24},{12,28},{16,0},{20,4},{24,8},{28,12},{1,17},{... | collective-permute-start | bytes 1253384 | tf_op jit(solution)/shard_map/ppermute | solution.py:342
  366.5 28.0 %collective-permute-start.16 = (bf16[2,136,1536]{2,1,0:T(8,128)(2,1)}, bf16[2,136,1536]{2,1,0:T(8,128)(2,1)}, u32[]{:S(2)}, u32[]{:S(2)}) collective-permute-start(bf16[2,136,1536]{2,1,0:T(8,128)(2,1)} %pad_maximum_fusion.17), channel_id=1, source_target_pairs={{0,16},{4,20},{8,24},{12,28},{16,0},{20,4},{24,8},{28,12},{1,17},{... | collective-permute-start | bytes 2506760 | tf_op jit(solution)/shard_map/ppermute | solution.py:342
  369.0 23.4 %collective-permute-start.15 = (bf16[2,136,1536]{2,1,0:T(8,128)(2,1)}, bf16[2,136,1536]{2,1,0:T(8,128)(2,1)}, u32[]{:S(2)}, u32[]{:S(2)}) collective-permute-start(bf16[2,136,1536]{2,1,0:T(8,128)(2,1)} %pad_maximum_fusion.16), channel_id=1, source_target_pairs={{0,8},{4,12},{8,0},{12,4},{16,24},{20,28},{24,16},{28,20},{1,9},{5... | collective-permute-start | bytes 2506760 | tf_op jit(solution)/shard_map/ppermute | solution.py:342
  391.7 9.1 collective-permute-start.3
  401.5 33.0 %copy-start.11 = (f32[1,272,1536]{2,1,0:T(8,128)}, f32[1,272,1536]{2,1,0:T(8,128)S(1)}, u32[]{:S(2)}) copy-start(f32[1,272,1536]{2,1,0:T(8,128)S(1)} %get-tuple-element.37) | copy-start | bytes 5013508
  401.5 33.0 %copy-start.92 = (f32[272]{0:T(512)}, f32[272]{0:T(512)S(1)}, u32[]{:S(2)}) copy-start(f32[272]{0:T(512)S(1)} %broadcast_multiply_fusion.11) | copy-start | bytes 3268
  401.9 32.6 %copy-start.98 = (f32[272]{0:T(512)}, f32[272]{0:T(512)S(1)}, u32[]{:S(2)}) copy-start(f32[272]{0:T(512)S(1)} %add_rsqrt_fusion.2) | copy-start | bytes 3268
  532.1 71.0 %collective-permute-start.6 = (bf16[2,136,1536]{2,1,0:T(8,128)(2,1)}, bf16[2,136,1536]{2,1,0:T(8,128)(2,1)}, u32[]{:S(2)}, u32[]{:S(2)}) collective-permute-start(bf16[2,136,1536]{2,1,0:T(8,128)(2,1)} %pad_maximum_fusion.13), channel_id=1, source_target_pairs={{0,16},{4,20},{8,24},{12,28},{16,0},{20,4},{24,8},{28,12},{1,17},{... | collective-permute-start | bytes 2506760 | tf_op jit(solution)/shard_map/ppermute | solution.py:342
  534.5 64.4 %collective-permute-start.4 = (bf16[2,136,1536]{2,1,0:T(8,128)(2,1)}, bf16[2,136,1536]{2,1,0:T(8,128)(2,1)}, u32[]{:S(2)}, u32[]{:S(2)}) collective-permute-start(bf16[2,136,1536]{2,1,0:T(8,128)(2,1)} %pad_maximum_fusion.12), channel_id=1, source_target_pairs={{0,8},{4,12},{8,0},{12,4},{16,24},{20,28},{24,16},{28,20},{1,9},{5... | collective-permute-start | bytes 2506760 | tf_op jit(solution)/shard_map/ppermute | solution.py:342
  576.0 40.0 %collective-permute-start.19 = (bf16[2,136,1536]{2,1,0:T(8,128)(2,1)}, bf16[2,136,1536]{2,1,0:T(8,128)(2,1)}, u32[]{:S(2)}, u32[]{:S(2)}) collective-permute-start(bf16[2,136,1536]{2,1,0:T(8,128)(2,1)} %pad_maximum_fusion.19), channel_id=1, source_target_pairs={{0,16},{4,20},{8,24},{12,28},{16,0},{20,4},{24,8},{28,12},{1,17},{... | collective-permute-start | bytes 2506760 | tf_op jit(solution)/shard_map/ppermute | solution.py:342
  578.4 22.1 %collective-permute-start.17 = (bf16[2,136,1536]{2,1,0:T(8,128)(2,1)}, bf16[2,136,1536]{2,1,0:T(8,128)(2,1)}, u32[]{:S(2)}, u32[]{:S(2)}) collective-permute-start(bf16[2,136,1536]{2,1,0:T(8,128)(2,1)} %pad_maximum_fusion.18), channel_id=1, source_target_pairs={{0,8},{4,12},{8,0},{12,4},{16,24},{20,28},{24,16},{28,20},{1,9},{5... | collective-permute-start | bytes 2506760 | tf_op jit(solution)/shard_map/ppermute | solution.py:342
  582.4 56.7 %collective-permute-start.45 = (bf16[1,2,2,192,4,384]{5,3,2,1,0,4:T(8,128)(2,1)}, bf16[1,2,2,192,4,384]{5,3,2,1,0,4:T(8,128)(2,1)}, u32[]{:S(2)}, u32[]{:S(2)}) collective-permute-start(bf16[1,2,2,192,4,384]{5,3,2,1,0,4:T(8,128)(2,1)} %bitcast.628), channel_id=1, source_target_pairs={{0,4},{4,0},{8,12},{12,8},{16,20},{20,16},{24,28},{28,24},{1,5},{5... | collective-permute-start | bytes 7077896 | tf_op jit(solution)/shard_map/ppermute | solution.py:342
  598.9 140.8 %collective-permute-start.42 = (bf16[2,2,2,192,4,384]{5,3,4,2,1,0:T(8,128)(2,1)}, bf16[2,2,2,192,4,384]{5,3,4,2,1,0:T(8,128)(2,1)}, u32[]{:S(2)}, u32[]{:S(2)}) collective-permute-start(bf16[2,2,2,192,4,384]{5,3,4,2,1,0:T(8,128)(2,1)} %bitcast.627), channel_id=1, source_target_pairs={{0,4},{4,0},{8,12},{12,8},{16,20},{20,16},{24,28},{28,24},{1,5},{5... | collective-permute-start | bytes 14155784 | tf_op jit(solution)/shard_map/ppermute | solution.py:342
  600.5 12.6 %collective-permute-start.5 = (bf16[136,1536]{1,0:T(8,128)(2,1)S(1)}, bf16[136,1536]{1,0:T(8,128)(2,1)S(1)}, u32[]{:S(2)}, u32[]{:S(2)}) collective-permute-start(bf16[136,1536]{1,0:T(8,128)(2,1)S(1)} %fusion.79), channel_id=1, source_target_pairs={{0,16},{4,20},{8,24},{12,28},{16,0},{20,4},{24,8},{28,12},{1,17},{... | collective-permute-start | bytes 1253384 | tf_op jit(solution)/shard_map/ppermute | solution.py:342
  603.2 18.0 %collective-permute-start.18 = (bf16[136,1536]{1,0:T(8,128)(2,1)S(1)}, bf16[136,1536]{1,0:T(8,128)(2,1)S(1)}, u32[]{:S(2)}, u32[]{:S(2)}) collective-permute-start(bf16[136,1536]{1,0:T(8,128)(2,1)S(1)} %fusion.75), channel_id=1, source_target_pairs={{0,16},{4,20},{8,24},{12,28},{16,0},{20,4},{24,8},{28,12},{1,17},{... | collective-permute-start | bytes 1253384 | tf_op jit(solution)/shard_map/ppermute | solution.py:342
  614.5 9.8 collective-permute-start.7
  622.5 10.8 collective-permute-start.20
  626.2 11.7 %collective-permute-start.8 = (bf16[136,1536]{1,0:T(8,128)(2,1)S(1)}, bf16[136,1536]{1,0:T(8,128)(2,1)S(1)}, u32[]{:S(2)}, u32[]{:S(2)}) collective-permute-start(bf16[136,1536]{1,0:T(8,128)(2,1)S(1)} %get-tuple-element.109), channel_id=1, source_target_pairs={{0,0},{1,1},{4,2},{5,3},{2,4},{3,5},{6,6},{7,7},{8,8},{9,9},{12,10... | collective-permute-start | bytes 1253384 | tf_op jit(solution)/shard_map/ppermute | solution.py:380
  626.9 11.3 %collective-permute-start.9 = (bf16[136,1536]{1,0:T(8,128)(2,1)S(1)}, bf16[136,1536]{1,0:T(8,128)(2,1)S(1)}, u32[]{:S(2)}, u32[]{:S(2)}) collective-permute-start(bf16[136,1536]{1,0:T(8,128)(2,1)S(1)} %get-tuple-element.110), channel_id=1, source_target_pairs={{1,0},{0,1},{5,2},{4,3},{3,4},{2,5},{7,6},{6,7},{9,8},{8,9},{13,10... | collective-permute-start | bytes 1253384 | tf_op jit(solution)/shard_map/ppermute | solution.py:381
  637.9 5.0 collective-permute-start.21
  642.8 396.0 %all-reduce.3.cloned.1.call-start = ((), (), s32[]{:S(2)}) async-start(), calls=%async_computation.9 | async-start | bytes 9437184
  668.9 17.8 %collective-permute-start.22 = (bf16[544,1536]{1,0:T(8,128)(2,1)}, bf16[544,1536]{1,0:T(8,128)(2,1)S(1)}, u32[]{:S(2)}, u32[]{:S(2)}) collective-permute-start(bf16[544,1536]{1,0:T(8,128)(2,1)} %get-tuple-element.126), channel_id=1, source_target_pairs={{0,4},{4,0},{8,12},{12,8},{16,20},{20,16},{24,28},{28,24},{1,5},{5... | collective-permute-start | bytes 5013512 | tf_op jit(solution)/shard_map/ppermute | solution.py:342
  681.9 83.5 %collective-permute-start.37 = (bf16[3,2,384,384]{3,2,1,0:T(8,128)(2,1)}, bf16[3,2,384,384]{3,2,1,0:T(8,128)(2,1)}, u32[]{:S(2)}, u32[]{:S(2)}) collective-permute-start(bf16[3,2,384,384]{3,2,1,0:T(8,128)(2,1)} %dynamic-slice_bitcast_fusion.1), channel_id=1, source_target_pairs={{0,8},{4,12},{8,0},{12,4},{16,24},{20,28},{24,16},{28,20},{1,9},{5... | collective-permute-start | bytes 5308424 | tf_op jit(solution)/shard_map/ppermute | solution.py:342
  685.6 83.0 %collective-permute-start.39 = (bf16[3,2,384,384]{3,2,1,0:T(8,128)(2,1)}, bf16[3,2,384,384]{3,2,1,0:T(8,128)(2,1)}, u32[]{:S(2)}, u32[]{:S(2)}) collective-permute-start(bf16[3,2,384,384]{3,2,1,0:T(8,128)(2,1)} %dynamic-slice_bitcast_fusion), channel_id=1, source_target_pairs={{0,16},{4,20},{8,24},{12,28},{16,0},{20,4},{24,8},{28,12},{1,17},{... | collective-permute-start | bytes 5308424 | tf_op jit(solution)/shard_map/ppermute | solution.py:342
  745.8 294.3 %reduce-scatter.10.cloned.1.call-start = ((), (), s32[]{:S(2)}) async-start(), calls=%async_computation.5 | async-start | bytes 737280 | tf_op jit(solution)/shard_map/reduce_scatter | solution.py:422
  750.1 21.9 %collective-permute-start.32 = (bf16[1,2,384,384]{3,2,1,0:T(8,128)(2,1)}, bf16[1,2,384,384]{3,2,1,0:T(8,128)(2,1)}, u32[]{:S(2)}, u32[]{:S(2)}) collective-permute-start(bf16[1,2,384,384]{3,2,1,0:T(8,128)(2,1)} %dynamic-slice_bitcast_fusion.9), channel_id=1, source_target_pairs={{0,8},{4,12},{8,0},{12,4},{16,24},{20,28},{24,16},{28,20},{1,9},{5... | collective-permute-start | bytes 1769480 | tf_op jit(solution)/shard_map/ppermute | solution.py:342
  752.0 22.1 %collective-permute-start.34 = (bf16[1,2,384,384]{3,2,1,0:T(8,128)(2,1)}, bf16[1,2,384,384]{3,2,1,0:T(8,128)(2,1)}, u32[]{:S(2)}, u32[]{:S(2)}) collective-permute-start(bf16[1,2,384,384]{3,2,1,0:T(8,128)(2,1)} %dynamic-slice_bitcast_fusion.8), channel_id=1, source_target_pairs={{0,16},{4,20},{8,24},{12,28},{16,0},{20,4},{24,8},{28,12},{1,17},{... | collective-permute-start | bytes 1769480 | tf_op jit(solution)/shard_map/ppermute | solution.py:342
  765.4 37.8 %collective-permute-start.23 = (bf16[544,1536]{1,0:T(8,128)(2,1)}, bf16[544,1536]{1,0:T(8,128)(2,1)}, u32[]{:S(2)}, u32[]{:S(2)}) collective-permute-start(bf16[544,1536]{1,0:T(8,128)(2,1)} %get-tuple-element.130), channel_id=1, source_target_pairs={{0,4},{4,0},{8,12},{12,8},{16,20},{20,16},{24,28},{28,24},{1,5},{5... | collective-permute-start | bytes 5013512 | tf_op jit(solution)/shard_map/ppermute | solution.py:342
  767.7 31.4 %collective-permute-start.38 = (bf16[3,384,384]{2,1,0:T(8,128)(2,1)S(1)}, bf16[3,384,384]{2,1,0:T(8,128)(2,1)S(1)}, u32[]{:S(2)}, u32[]{:S(2)}) collective-permute-start(bf16[3,384,384]{2,1,0:T(8,128)(2,1)S(1)} %dynamic-slice_bitcast_fusion.3), channel_id=1, source_target_pairs={{0,16},{4,20},{8,24},{12,28},{16,0},{20,4},{24,8},{28,12},{1,17},{... | collective-permute-start | bytes 2654216 | tf_op jit(solution)/shard_map/ppermute | solution.py:342
  770.7 28.8 %collective-permute-start.40 = (bf16[3,384,384]{2,1,0:T(8,128)(2,1)S(1)}, bf16[3,384,384]{2,1,0:T(8,128)(2,1)S(1)}, u32[]{:S(2)}, u32[]{:S(2)}) collective-permute-start(bf16[3,384,384]{2,1,0:T(8,128)(2,1)S(1)} %dynamic-slice_bitcast_fusion.2), channel_id=1, source_target_pairs={{0,8},{4,12},{8,0},{12,4},{16,24},{20,28},{24,16},{28,20},{1,9},{5... | collective-permute-start | bytes 2654216 | tf_op jit(solution)/shard_map/ppermute | solution.py:342
  773.2 22.8 %collective-permute-start.33 = (bf16[1,384,384]{2,1,0:T(8,128)(2,1)S(1)}, bf16[1,384,384]{2,1,0:T(8,128)(2,1)S(1)}, u32[]{:S(2)}, u32[]{:S(2)}) collective-permute-start(bf16[1,384,384]{2,1,0:T(8,128)(2,1)S(1)} %dynamic-slice_bitcast_fusion.18), channel_id=1, source_target_pairs={{0,16},{4,20},{8,24},{12,28},{16,0},{20,4},{24,8},{28,12},{1,17},{... | collective-permute-start | bytes 884744 | tf_op jit(solution)/shard_map/ppermute | solution.py:342
  775.4 23.5 %collective-permute-start.35 = (bf16[1,384,384]{2,1,0:T(8,128)(2,1)S(1)}, bf16[1,384,384]{2,1,0:T(8,128)(2,1)S(1)}, u32[]{:S(2)}, u32[]{:S(2)}) collective-permute-start(bf16[1,384,384]{2,1,0:T(8,128)(2,1)S(1)} %dynamic-slice_bitcast_fusion.17), channel_id=1, source_target_pairs={{0,8},{4,12},{8,0},{12,4},{16,24},{20,28},{24,16},{28,20},{1,9},{5... | collective-permute-start | bytes 884744 | tf_op jit(solution)/shard_map/ppermute | solution.py:342
  796.1 80.3 %collective-permute-start.26 = (bf16[130,768]{1,0:T(8,128)(2,1)}, bf16[130,768]{1,0:T(8,128)(2,1)}, u32[]{:S(2)}, u32[]{:S(2)}) collective-permute-start(bf16[130,768]{1,0:T(8,128)(2,1)} %get-tuple-element.132), channel_id=1, source_target_pairs={{0,4},{4,0},{8,12},{12,8},{16,20},{20,16},{24,28},{28,24},{1,5},{5... | collective-permute-start | bytes 599048 | tf_op jit(solution)/shard_map/ppermute | solution.py:342
  799.1 3.0 collective-permute-start.36
  801.6 129.0 %collective-permute-start.41 = (bf16[2,3,192,384]{3,2,1,0:T(8,128)(2,1)}, bf16[2,3,192,384]{3,2,1,0:T(8,128)(2,1)}, u32[]{:S(2)}, u32[]{:S(2)}) collective-permute-start(bf16[2,3,192,384]{3,2,1,0:T(8,128)(2,1)} %fusion.66), channel_id=1, source_target_pairs={{0,4},{4,0},{8,12},{12,8},{16,20},{20,16},{24,28},{28,24},{1,5},{5... | collective-permute-start | bytes 2654216 | tf_op jit(solution)/shard_map/ppermute | solution.py:342
  803.1 260.0 %reduce-scatter.12.cloned.1.call-start = ((), (), s32[]{:S(2)}) async-start(), calls=%async_computation.6 | async-start | bytes 2211840 | tf_op jit(solution)/shard_map/reduce_scatter | solution.py:422
  849.5 84.3 %collective-permute-start.29 = (bf16[3,2,384,384]{3,2,0,1:T(8,128)(2,1)}, bf16[3,2,384,384]{3,2,0,1:T(8,128)(2,1)}, u32[]{:S(2)}, u32[]{:S(2)}) collective-permute-start(bf16[3,2,384,384]{3,2,0,1:T(8,128)(2,1)} %bitcast.713), channel_id=1, source_target_pairs={{0,16},{4,20},{8,24},{12,28},{16,0},{20,4},{24,8},{28,12},{1,17},{... | collective-permute-start | bytes 5308424 | tf_op jit(solution)/shard_map/ppermute | solution.py:342
  875.2 62.6 %collective-permute-start.27 = (bf16[3,2,384,384]{3,2,1,0:T(8,128)(2,1)}, bf16[3,2,384,384]{3,2,1,0:T(8,128)(2,1)}, u32[]{:S(2)}, u32[]{:S(2)}) collective-permute-start(bf16[3,2,384,384]{3,2,1,0:T(8,128)(2,1)} %bitcast.714), channel_id=1, source_target_pairs={{0,8},{4,12},{8,0},{12,4},{16,24},{20,28},{24,16},{28,20},{1,9},{5... | collective-permute-start | bytes 5308424 | tf_op jit(solution)/shard_map/ppermute | solution.py:342
  933.7 144.7 %reduce-scatter.8.cloned.1.call-start = ((), (), s32[]{:S(2)}) async-start(), calls=%async_computation.4 | async-start | bytes 2211840 | tf_op jit(solution)/shard_map/reduce_scatter | solution.py:422
  936.5 19.7 %collective-permute-start.30 = (bf16[3,384,384]{2,1,0:T(8,128)(2,1)S(1)}, bf16[3,384,384]{2,1,0:T(8,128)(2,1)S(1)}, u32[]{:S(2)}, u32[]{:S(2)}) collective-permute-start(bf16[3,384,384]{2,1,0:T(8,128)(2,1)S(1)} %dynamic-slice_bitcast_fusion.4), channel_id=1, source_target_pairs={{0,8},{4,12},{8,0},{12,4},{16,24},{20,28},{24,16},{28,20},{1,9},{5... | collective-permute-start | bytes 2654216 | tf_op jit(solution)/shard_map/ppermute | solution.py:342
  939.9 19.4 %collective-permute-start.28 = (bf16[3,384,384]{2,1,0:T(8,128)(2,1)S(1)}, bf16[3,384,384]{2,1,0:T(8,128)(2,1)S(1)}, u32[]{:S(2)}, u32[]{:S(2)}) collective-permute-start(bf16[3,384,384]{2,1,0:T(8,128)(2,1)S(1)} %dynamic-slice_bitcast_fusion.5), channel_id=1, source_target_pairs={{0,16},{4,20},{8,24},{12,28},{16,0},{20,4},{24,8},{28,12},{1,17},{... | collective-permute-start | bytes 2654216 | tf_op jit(solution)/shard_map/ppermute | solution.py:342
  959.7 7.6 collective-permute-start.31
  962.9 71.2 %collective-permute-start.24 = (bf16[136,1536]{1,0:T(8,128)(2,1)S(1)}, bf16[136,1536]{1,0:T(8,128)(2,1)S(1)}, u32[]{:S(2)}, u32[]{:S(2)}) collective-permute-start(bf16[136,1536]{1,0:T(8,128)(2,1)S(1)} %get-tuple-element.97), channel_id=1, source_target_pairs={{0,0},{1,1},{4,2},{5,3},{2,4},{3,5},{6,6},{7,7},{8,8},{9,9},{12,10... | collective-permute-start | bytes 1253384 | tf_op jit(solution)/shard_map/ppermute | solution.py:380
  963.6 70.5 %collective-permute-start.25 = (bf16[136,1536]{1,0:T(8,128)(2,1)S(1)}, bf16[136,1536]{1,0:T(8,128)(2,1)S(1)}, u32[]{:S(2)}, u32[]{:S(2)}) collective-permute-start(bf16[136,1536]{1,0:T(8,128)(2,1)S(1)} %get-tuple-element.98), channel_id=1, source_target_pairs={{1,0},{0,1},{5,2},{4,3},{3,4},{2,5},{7,6},{6,7},{9,8},{8,9},{13,10... | collective-permute-start | bytes 1253384 | tf_op jit(solution)/shard_map/ppermute | solution.py:381
  1036.4 10.3 collective-permute-start.46
  1039.9 18.0 %collective-permute-start.43 = (bf16[2,2,192,384]{3,2,1,0:T(8,128)(2,1)S(1)}, bf16[2,2,192,384]{3,2,1,0:T(8,128)(2,1)S(1)}, u32[]{:S(2)}, u32[]{:S(2)}) collective-permute-start(bf16[2,2,192,384]{3,2,1,0:T(8,128)(2,1)S(1)} %dynamic-slice_bitcast_fusion.6), channel_id=1, source_target_pairs={{0,16},{4,20},{8,24},{12,28},{16,0},{20,4},{24,8},{28,12},{1,17},{... | collective-permute-start | bytes 1769480 | tf_op jit(solution)/shard_map/ppermute | solution.py:342
  1047.8 12.2 %collective-permute-start.47 = (bf16[1,192,2,384]{3,1,2,0:T(8,128)(2,1)S(1)}, bf16[1,192,2,384]{3,1,2,0:T(8,128)(2,1)S(1)}, u32[]{:S(2)}, u32[]{:S(2)}) collective-permute-start(bf16[1,192,2,384]{3,1,2,0:T(8,128)(2,1)S(1)} %fusion.93), channel_id=1, source_target_pairs={{0,8},{4,12},{8,0},{12,4},{16,24},{20,28},{24,16},{28,20},{1,9},{5... | collective-permute-start | bytes 884744 | tf_op jit(solution)/shard_map/ppermute | solution.py:342
  1059.4 14.0 %collective-permute-start.44 = (bf16[2,192,2,384]{3,1,2,0:T(8,128)(2,1)S(1)}, bf16[2,192,2,384]{3,1,2,0:T(8,128)(2,1)S(1)}, u32[]{:S(2)}, u32[]{:S(2)}) collective-permute-start(bf16[2,192,2,384]{3,1,2,0:T(8,128)(2,1)S(1)} %bitcast.729), channel_id=1, source_target_pairs={{0,8},{4,12},{8,0},{12,4},{16,24},{20,28},{24,16},{28,20},{1,9},{5... | collective-permute-start | bytes 1769480 | tf_op jit(solution)/shard_map/ppermute | solution.py:342
  (111 other events, 726.4 us)
Sparse Core Ops, SparseCore 0:
  53.7 172.9 all-gather.4
  642.9 56.3 reduce-scatter.13
  745.9 187.6 all-reduce.2
  935.7 20.8 reduce-scatter.9
  958.8 50.6 reduce-scatter.11
  1011.9 38.5 reduce-scatter.7

commit v2 on v1

--- a/solution.py
+++ b/solution.py
@@ -374,14 +374,6 @@
     return ordered(z % 2, first, second, 0).reshape(-1, value.shape[-1])
 
 
-def rows_out(half, z):
-    blocks = half.reshape(2, -1, half.shape[-1])
-    back = [[(b, a) for a, b in z_routes(turn)] for turn in range(2)]
-    first = lax.ppermute(take(blocks, z % 2, 0), ("dp", "tensor"), back[0])
-    second = lax.ppermute(take(blocks, 1 - z % 2, 0), ("dp", "tensor"), back[1])
-    return ordered(z % 2, first, second, 0)
-
-
 def plane_rows(half):
     cut = half.shape[0] // 2
     upper, lower = half[:cut], half[cut:]
@@ -406,34 +398,6 @@
     return jnp.concatenate([upper_sum, lower_sum])
 
 
-def narrow_share(grads, place):
-    core, xbit, ybit, z = place
-    count, depth, width = grads.shape[0], grads.shape[1] // 8, grads.shape[2] // 2
-    grid = grads.astype(BF).reshape(count, 2, 2, 2 * depth, 2 * width)
-    left, right = grid[..., :width], grid[..., width:]
-    left = added(take(left, xbit, 2), swap(take(left, 1 - xbit, 2), XBIT)).astype(BF)
-    right = added(take(right, ybit, 1), swap(take(right, 1 - ybit, 1), YBIT)).astype(BF)
-    left = added(take(left, ybit, 1), swap(take(left, 1 - ybit, 1), YBIT)).astype(BF)
-    right = added(take(right, xbit, 1), swap(take(right, 1 - xbit, 1), XBIT)).astype(BF)
-    both = jnp.stack([left, right]).reshape(2, count, 2, depth, width)
-    mine = take(both, core, 2)
-    theirs = swap(take(both, 1 - core, 2), CORE)
-    parts = ordered(core, mine, theirs, 0).reshape(4, count, depth, width)
-    return lax.psum_scatter(parts, "tensor", scatter_dimension=0, tiled=False)
-
-
-def wide_share(grads, place):
-    core, xbit, ybit, z = place
-    count, depth, width = grads.shape[0], grads.shape[1] // 8, grads.shape[2]
-    grid = grads.astype(BF).reshape(count, 2, 2, 2, depth, 4, width // 4)
-    grid = added(take(grid, core, 3), swap(take(grid, 1 - core, 3), CORE)).astype(BF)
-    grid = jnp.moveaxis(grid, 4, 0)
-    grid = lax.psum_scatter(grid, "tensor", scatter_dimension=0, tiled=False)
-    grid = ordered(ybit, take(grid, ybit, 1), swap(take(grid, 1 - ybit, 1), YBIT), 3)
-    grid = ordered(xbit, take(grid, xbit, 1), swap(take(grid, 1 - xbit, 1), XBIT), 3)
-    return grid.reshape(count, depth, width)
-
-
 MESH = pl.DeviceIdType.MESH
 
 
@@ -481,7 +445,23 @@
 
 
 def first_kernel(
-    rows_ref, wide_ref, seq_ref, block_ref, send_a, recv_a, send_b, recv_b, send_c, recv_c, local
+    rows_ref,
+    wide_ref,
+    cond_ref,
+    size_ref,
+    seq_ref,
+    block_ref,
+    cond_both,
+    size_both,
+    send_a,
+    recv_a,
+    send_b,
+    recv_b,
+    send_c,
+    recv_c,
+    send_d,
+    recv_d,
+    local,
 ):
     dp, plane, core, z = spot()
     sibling = (flip(dp, 1), z)
@@ -512,6 +492,13 @@
         wide.append(copy)
     own = pltpu.make_async_copy(wide_ref.at[:, plane], block_ref.at[:, plane], local.at[1])
     own.start()
+    small = []
+    for slot, (source, target) in enumerate([(cond_ref, cond_both), (size_ref, size_both)]):
+        copy = push(source, target.at[core], send_d.at[slot], recv_d.at[slot], sibling)
+        copy.start()
+        keep = pltpu.make_async_copy(source, target.at[core], local.at[2 + slot])
+        keep.start()
+        small.append((copy, keep, slot, target))
     for j in range(2):
         block = 2 * core + j
         stays = jnp.logical_and(home, block == z)
@@ -539,6 +526,11 @@
     for copy in wide:
         copy.wait()
     own.wait()
+    for copy, keep, slot, target in small:
+        keep.wait()
+        copy.wait_send()
+        theirs = target.at[1 - core]
+        push(theirs, theirs, send_d.at[slot], recv_d.at[slot], sibling).wait_recv()
 
 
 def any_specs(count):
@@ -556,25 +548,34 @@
     return pltpu.SemaphoreType.DMA(shape)
 
 
-def first_moves(rows, wide):
+def first_moves(rows, wide, cond, size):
     _, height, width = rows.shape
     return pl.pallas_call(
         first_kernel,
         out_shape=[
             jax.ShapeDtypeStruct((4, height, width), BF),
             jax.ShapeDtypeStruct(wide.shape, BF),
+            jax.ShapeDtypeStruct((2, *cond.shape), BF),
+            jax.ShapeDtypeStruct((2, *size.shape), size.dtype),
         ],
-        in_specs=near_specs(2),
-        out_specs=any_specs(2),
-        scratch_shapes=[dma(2), dma(2), dma(3), dma(3), dma(2), dma(2), dma(2)],
+        in_specs=near_specs(4),
+        out_specs=any_specs(4),
+        scratch_shapes=[dma(2), dma(2), dma(3), dma(3), dma(2), dma(2), dma(2), dma(2), dma(4)],
         compiler_params=pltpu.CompilerParams(
             collective_id=1, has_side_effects=True, vmem_limit_bytes=ROOM
         ),
         name="first_moves",
-    )(rows, wide)
-
-
-def narrow_kernel(shard_ref, whole_ref, send_s, recv_s, send_z, recv_z, send_p, recv_p, local, *, groups):
+    )(rows, wide, cond, size)
+
+
+def weights_kernel(
+    shard_ref, block_ref, *refs, groups, wides
+):
+    count = len(groups)
+    arrays = max(which for which, _ in groups) + 1
+    whole_refs, wide_ref = refs[:arrays], refs[arrays]
+    send_s, recv_s, send_z, recv_z, send_p, recv_p, local = refs[arrays + 1 : arrays + 8]
+    send_w, recv_w, send_v, recv_v, local_w = refs[arrays + 8 :]
     dp, plane, core, z = spot()
     width = shard_ref.shape[2]
     sibling = (flip(dp, 1), z)
@@ -587,32 +588,33 @@
     def columns(which):
         return pl.ds(pl.multiple_of(which * width, width), width)
 
-    for g, (low, count) in enumerate(groups):
-        piece = shard_ref.at[pl.ds(low, count)]
+    def slab(g):
+        array, index = groups[g]
+        return whole_refs[array].at[index]
+
+    for g in range(count):
+        target = slab(g).at[plane, core, :, columns(z % 2)]
 
         @pl.when(home)
-        def _(g=g, low=low, count=count, piece=piece):
-            spot_ref = whole_ref.at[pl.ds(low, count), plane, core, :, columns(z % 2)]
-            pltpu.make_async_copy(piece, spot_ref, local.at[g]).start()
+        def _(g=g, target=target):
+            pltpu.make_async_copy(shard_ref.at[g], target, local.at[g]).start()
 
         @pl.when(jnp.logical_not(home))
-        def _(g=g, low=low, count=count, piece=piece):
-            spot_ref = whole_ref.at[pl.ds(low, count), plane, core, :, columns(z % 2)]
-            push(piece, spot_ref, send_s.at[g], recv_s.at[g], sibling).start()
+        def _(g=g, target=target):
+            push(shard_ref.at[g], target, send_s.at[g], recv_s.at[g], sibling).start()
 
     near = jnp.where(core == 0, jnp.where(z >= 1, 1, 0), jnp.where(z <= 2, 0, 1))
-
-    def area(g, which, chip):
-        low, count = groups[g]
-        return whole_ref.at[pl.ds(low, count), chip, :, :, columns(which)]
 
     def order(turn):
         return near if turn == 0 else 1 - near
+
+    def area(g, which, chip):
+        return slab(g).at[chip, :, :, columns(which)]
 
     def on_z(g, turn, act):
         which = order(turn)
         source_z = 2 * core + which
-        spot_ref = area(g, which, plane)
+        place = area(g, which, plane)
         for way, (wanted, target) in enumerate(
             [
                 (jnp.logical_and(z >= source_z, z < 3), above),
@@ -622,28 +624,27 @@
 
             @pl.when(wanted)
             def _(way=way, target=target):
-                act(push(spot_ref, spot_ref, send_z.at[g, which, way], recv_z.at[g, which], target))
+                act(push(place, place, send_z.at[g, turn, way], recv_z.at[g, which], target))
 
     def arrive(g, turn):
         which = order(turn)
         source_z = 2 * core + which
-        low, count = groups[g]
 
         @pl.when(z == source_z)
         def _():
-            mine = whole_ref.at[pl.ds(low, count), plane, core, :, columns(which)]
-            other = whole_ref.at[pl.ds(low, count), plane, 1 - core, :, columns(which)]
-            pltpu.make_async_copy(shard_ref.at[pl.ds(low, count)], mine, local.at[g]).wait()
+            mine = slab(g).at[plane, core, :, columns(which)]
+            other = slab(g).at[plane, 1 - core, :, columns(which)]
+            pltpu.make_async_copy(shard_ref.at[g], mine, local.at[g]).wait()
             push(mine, other, send_s.at[g], recv_s.at[g], sibling).wait_recv()
 
         @pl.when(z != source_z)
         def _():
-            spot_ref = area(g, which, plane)
-            push(spot_ref, spot_ref, send_z.at[g, which, 0], recv_z.at[g, which], sibling).wait_recv()
+            place = area(g, which, plane)
+            push(place, place, send_z.at[g, turn, 0], recv_z.at[g, which], sibling).wait_recv()
 
     def hop(g, turn, chip, slot, mate):
-        spot_ref = area(g, order(turn), chip)
-        return push(spot_ref, spot_ref, send_p.at[g, turn, slot], recv_p.at[g, turn, slot], mate)
+        place = area(g, order(turn), chip)
+        return push(place, place, send_p.at[g, turn, slot], recv_p.at[g, turn, slot], mate)
 
     mates = (xmate, ymate)
 
@@ -658,16 +659,62 @@
         hop(g, turn, chip, turn, mates[turn]).wait_recv()
         hop(g, turn, chip, 2, mates[1 - turn]).start()
 
-    count = len(groups)
-    spread(0, 0)
-    spread(0, 1)
-    for g in range(count):
-        relay(g, 0)
-        if g + 1 < count:
-            spread(g + 1, 0)
-        relay(g, 1)
-        if g + 1 < count:
-            spread(g + 1, 1)
+    wide_width = block_ref.shape[3]
+
+    def quarter(k, block, side):
+        return wide_ref.at[k, :, side, :, pl.ds(pl.multiple_of(block * wide_width, wide_width), wide_width)]
+
+    def wide_copy(k, block, way, target):
+        place = quarter(k, block, core)
+        return push(place, place, send_w.at[k, block, way], recv_w.at[k, block], target)
+
+    def to_sibling(k, block, side):
+        place = quarter(k, block, side)
+        return push(place, place, send_v.at[k, block], recv_v.at[k, block], sibling)
+
+    def wide_own(k):
+        pltpu.make_async_copy(block_ref.at[k], quarter(k, z, core), local_w.at[k]).start()
+        pltpu.make_async_copy(block_ref.at[k], quarter(k, z, core), local_w.at[k]).wait()
+        for way, (wanted, target) in enumerate([(z < 3, above), (z > 0, below)]):
+
+            @pl.when(wanted)
+            def _(way=way, target=target):
+                wide_copy(k, z, way, target).start()
+
+        to_sibling(k, z, core).start()
+
+    def wide_step(k, step):
+        for way, (block, wanted, further, target) in enumerate(
+            [
+                (z - step, z - step >= 0, z < 3, above),
+                (z + step, z + step <= 3, z > 0, below),
+            ]
+        ):
+
+            @pl.when(wanted)
+            def _(block=block, way=way, target=target):
+                wide_copy(k, block, way, target).wait_recv()
+                to_sibling(k, block, core).start()
+
+            @pl.when(jnp.logical_and(wanted, further))
+            def _(block=block, way=way, target=target):
+                wide_copy(k, block, way, target).start()
+
+    script = (
+        "S0 S1 R0 S2 R1 S3 R2 S4 R3 S5 S6 W0 R4 W1 R5 V01 R6 V11 V02 V12 V03 V13"
+    )
+    for word in script.split():
+        kind = word[0]
+        if kind == "S":
+            spread(int(word[1]), 0)
+            spread(int(word[1]), 1)
+        elif kind == "R":
+            relay(int(word[1]), 0)
+            relay(int(word[1]), 1)
+        elif kind == "W" and int(word[1]) < wides:
+            wide_own(int(word[1]))
+        elif kind == "V" and int(word[1]) < wides:
+            wide_step(int(word[1]), int(word[2]))
     for g in range(count):
         for turn in range(2):
             hop(g, turn, mates[1 - turn][0] // 2, 1 - turn, mates[1 - turn]).wait_recv()
@@ -675,37 +722,57 @@
             for slot in range(3):
                 hop(g, turn, plane, slot, xmate).wait_send()
             on_z(g, turn, lambda copy: copy.wait_send())
-        low, size = groups[g]
 
         @pl.when(jnp.logical_not(home))
-        def _(g=g, low=low, size=size):
-            piece = shard_ref.at[pl.ds(low, size)]
-            push(piece, piece, send_s.at[g], recv_s.at[g], sibling).wait_send()
-
-
-def narrow_moves(shard, groups):
+        def _(g=g):
+            push(shard_ref.at[g], shard_ref.at[g], send_s.at[g], recv_s.at[g], sibling).wait_send()
+
+    for k in range(wides):
+        for block in range(4):
+            to_sibling(k, block, core).wait_send()
+            to_sibling(k, block, 1 - core).wait_recv()
+
+            @pl.when(jnp.logical_and(block <= z, z < 3))
+            def _(k=k, block=block):
+                wide_copy(k, block, 0, above).wait_send()
+
+            @pl.when(jnp.logical_and(block >= z, z > 0))
+            def _(k=k, block=block):
+                wide_copy(k, block, 1, below).wait_send()
+
+
+def weights_moves(shard, block, groups, wides):
     count, depth, width = shard.shape
-    parts = len(groups)
-    whole = pl.pallas_call(
-        functools.partial(narrow_kernel, groups=groups),
-        out_shape=jax.ShapeDtypeStruct((count, 4, 2, depth, 2 * width), BF),
-        in_specs=near_specs(1),
-        out_specs=pl.BlockSpec(memory_space=pl.ANY),
+    sizes = [0] * (max(which for which, _ in groups) + 1)
+    for which, _ in groups:
+        sizes[which] += 1
+    _, chips, _, unit = block.shape
+    out = pl.pallas_call(
+        functools.partial(weights_kernel, groups=groups, wides=wides),
+        out_shape=[jax.ShapeDtypeStruct((size, 4, 2, depth, 2 * width), BF) for size in sizes]
+        + [jax.ShapeDtypeStruct((wides, chips, 2, depth, 4 * unit), BF)],
+        in_specs=near_specs(2),
+        out_specs=any_specs(len(sizes) + 1),
         scratch_shapes=[
-            dma(parts),
-            dma(parts),
-            dma(parts, 2, 2),
-            dma(parts, 2),
-            dma(parts, 2, 3),
-            dma(parts, 2, 3),
-            dma(parts),
+            dma(count),
+            dma(count),
+            dma(count, 2, 2),
+            dma(count, 2),
+            dma(count, 2, 3),
+            dma(count, 2, 3),
+            dma(count),
+            dma(wides, 4, 2),
+            dma(wides, 4),
+            dma(wides, 4),
+            dma(wides, 4),
+            dma(wides),
         ],
         compiler_params=pltpu.CompilerParams(
             collective_id=2, has_side_effects=True, vmem_limit_bytes=ROOM
         ),
-        name="narrow_moves",
-    )(shard)
-    return whole.reshape(count, 8 * depth, 2 * width)
+        name="weights_moves",
+    )(shard, block)
+    return [whole.reshape(whole.shape[0], 8 * depth, whole.shape[-1]) for whole in out]
 
 
 def second_kernel(
@@ -790,6 +857,411 @@
     )(rows, quarter)
 
 
+def third_kernel(
+    part_ref, *refs, counts
+):
+    many = len(counts)
+    grad_refs = refs[:many]
+    sum_ref, quarter_ref = refs[many : many + 2]
+    got, far_x, far_y, own, theirs = refs[many + 2 : many + 7]
+    send_r, recv_r, send_w, recv_w, load, store = refs[many + 7 :]
+    dp, plane, core, z = spot()
+    sibling = (flip(dp, 1), z)
+    xmate, ymate, _ = plane_mates(dp, z)
+    greet([sibling, xmate, ymate])
+
+    def rows(source, slot, mate):
+        return push(source, got.at[slot], send_r.at[slot], recv_r.at[slot], mate)
+
+    first = [
+        rows(part_ref.at[3, 0], 0, xmate),
+        rows(part_ref.at[3, 1], 1, ymate),
+        rows(part_ref.at[1, 0], 2, xmate),
+        rows(part_ref.at[2, 1], 3, ymate),
+    ]
+    for copy in first:
+        copy.start()
+    wide, loads, base = [], [], 0
+    for grad, count in zip(grad_refs, counts, strict=True):
+        for k in range(count):
+            slot = base + k
+            wide.append(
+                push(grad.at[k, :, 1 - core], theirs.at[slot], send_w.at[slot], recv_w.at[slot], sibling)
+            )
+            loads.append(pltpu.make_async_copy(grad.at[k, :, core], own.at[slot], load.at[slot]))
+        base += count
+    for copy in wide + loads:
+        copy.start()
+    slabs = base
+    chips, depth, width = own.shape[1:]
+    unit = width // 4
+
+    def core_sums(slot):
+        loads[slot].wait()
+        wide[slot].wait_recv()
+
+        def body(chip, carry):
+            own[slot, chip] = own[slot, chip] + theirs[slot, chip]
+            return carry
+
+        lax.fori_loop(0, chips, body, 0)
+        for block in range(4):
+            pltpu.make_async_copy(
+                own.at[slot, :, :, pl.ds(block * unit, unit)],
+                quarter_ref.at[block, slot],
+                store.at[slot, block],
+            ).start()
+
+    core_sums(0)
+    first[0].wait_recv()
+    far_x[...] = (part_ref[2, 0].astype(F32) + got[0].astype(F32)).astype(BF)
+    upper = rows(far_x, 4, ymate)
+    upper.start()
+    first[1].wait_recv()
+    far_y[...] = (part_ref[1, 1].astype(F32) + got[1].astype(F32)).astype(BF)
+    lower = rows(far_y, 5, xmate)
+    lower.start()
+    for slot in range(1, slabs):
+        core_sums(slot)
+    first[2].wait_recv()
+    first[3].wait_recv()
+    upper.wait_recv()
+    sum_ref[0] = part_ref[0, 0].astype(F32) + got[2].astype(F32) + got[4].astype(F32)
+    lower.wait_recv()
+    sum_ref[1] = part_ref[0, 1].astype(F32) + got[3].astype(F32) + got[5].astype(F32)
+    for copy in first + wide + [upper, lower]:
+        copy.wait_send()
+    for slot in range(slabs):
+        for block in range(4):
+            pltpu.make_async_copy(
+                own.at[slot, :, :, pl.ds(block * unit, unit)],
+                quarter_ref.at[block, slot],
+                store.at[slot, block],
+            ).wait()
+
+
+def third_moves(part, grads):
+    _, _, height, width = part.shape
+    counts = tuple(grad.shape[0] for grad in grads)
+    slabs = sum(counts)
+    depth, units = grads[0].shape[1] // 8, grads[0].shape[2]
+    return pl.pallas_call(
+        functools.partial(third_kernel, counts=counts),
+        out_shape=[
+            jax.ShapeDtypeStruct((2, height, width), F32),
+            jax.ShapeDtypeStruct((4, slabs, 4, depth, units // 4), BF),
+        ],
+        in_specs=near_specs(1) + any_specs(len(grads)),
+        out_specs=near_specs(1) + any_specs(1),
+        scratch_shapes=[
+            pltpu.VMEM((6, height, width), BF),
+            pltpu.VMEM((height, width), BF),
+            pltpu.VMEM((height, width), BF),
+            pltpu.VMEM((slabs, 4, depth, units), BF),
+            pltpu.VMEM((slabs, 4, depth, units), BF),
+            dma(6),
+            dma(6),
+            dma(slabs),
+            dma(slabs),
+            dma(slabs),
+            dma(slabs, 4),
+        ],
+        compiler_params=pltpu.CompilerParams(
+            collective_id=4, has_side_effects=True, vmem_limit_bytes=ROOM
+        ),
+        name="third_moves",
+    )(part, *[grad.reshape(grad.shape[0], 4, 2, depth, units) for grad in grads])
+
+
+def share_kernel(
+    *refs, groups, arrays
+):
+    count = len(groups)
+    grad_refs, refs = refs[:arrays], refs[arrays:]
+    rows_ref, gain_ref, cond_ref = refs[:3]
+    out_ref, back_ref, gain_out, cond_out = refs[3:7]
+    one, got, two, line, gain_got, gain_sum, gain_line = refs[7:14]
+    (
+        load,
+        send_x,
+        recv_x,
+        send_y,
+        recv_y,
+        send_z,
+        recv_z,
+        send_c,
+        recv_c,
+        send_r,
+        recv_r,
+        send_g,
+        recv_g,
+        send_h,
+        recv_h,
+        send_k,
+        recv_k,
+        local,
+    ) = refs[14:]
+    dp, plane, core, z = spot()
+    xbit, ybit = plane % 2, plane // 2
+    sibling = (flip(dp, 1), z)
+    xmate, ymate, _ = plane_mates(dp, z)
+    plane_all = [(lax.rem(dp + step, 8), z) for step in range(1, 8)]
+    greet(plane_all + column_mates(dp, z)[1:])
+    home = z // 2 == core
+    above, below = (dp, z + 1), (dp, z - 1)
+    width = out_ref.shape[2]
+    near = jnp.where(core == 0, jnp.where(z >= 1, 1, 0), jnp.where(z <= 2, 0, 1))
+    mates = (xmate, ymate)
+
+    def order(turn):
+        return 1 - near if turn == 0 else near
+
+    def columns(which):
+        return pl.ds(pl.multiple_of(which * width, width), width)
+
+    def strip(g, turn, bit):
+        array, index = groups[g]
+        grid = grad_refs[array].at[index]
+        if turn == 0:
+            return grid.at[:, bit, :, :, columns(order(turn))]
+        return grid.at[bit, :, :, :, columns(order(turn))]
+
+    bits = (xbit, ybit)
+
+    def step_one(g, turn):
+        return push(
+            strip(g, turn, 1 - bits[turn]), got.at[g, turn], send_x.at[g, turn], recv_x.at[g, turn], mates[turn]
+        )
+
+    def fetch(g, turn):
+        return pltpu.make_async_copy(strip(g, turn, bits[turn]), one.at[g, turn], load.at[g, turn])
+
+    def step_two(g, turn):
+        return push(
+            one.at[g, turn, 1 - bits[1 - turn]],
+            two.at[g, turn],
+            send_y.at[g, turn],
+            recv_y.at[g, turn],
+            mates[1 - turn],
+        )
+
+    def after_one(g, turn):
+        fetch(g, turn).wait()
+        step_one(g, turn).wait_recv()
+
+        def body(i, carry):
+            side, part = i // 2, i % 2
+            one[g, turn, side, part] = one[g, turn, side, part] + got[g, turn, side, part]
+            return carry
+
+        lax.fori_loop(0, 4, body, 0)
+        step_two(g, turn).start()
+
+    def z_of(turn):
+        return 2 * core + order(turn)
+
+    def add_held(g, turn, source):
+        side = bits[1 - turn]
+
+        def body(part, carry):
+            one[g, turn, side, part] = one[g, turn, side, part] + source[part]
+            return carry
+
+        lax.fori_loop(0, 2, body, 0)
+
+    def line_copy(g, turn, way, target):
+        held = one.at[g, turn, bits[1 - turn]]
+        which = order(turn)
+        return push(held, line.at[g, which, way], send_z.at[g, turn], recv_z.at[g, which, way], target)
+
+    def after_two(g, turn):
+        step_two(g, turn).wait_recv()
+        add_held(g, turn, two.at[g, turn])
+        which, goal = order(turn), z_of(turn)
+
+        @pl.when(jnp.logical_and(z > 0, z <= goal))
+        def _():
+            line_copy(g, turn, 0, above).wait_recv()
+            add_held(g, turn, line.at[g, which, 0])
+
+        @pl.when(jnp.logical_and(z < 3, z >= goal))
+        def _():
+            line_copy(g, turn, 1, below).wait_recv()
+            add_held(g, turn, line.at[g, which, 1])
+
+        @pl.when(z < goal)
+        def _():
+            line_copy(g, turn, 0, above).start()
+
+        @pl.when(z > goal)
+        def _():
+            line_copy(g, turn, 1, below).start()
+
+        @pl.when(z == goal)
+        def _():
+            held = one.at[g, turn, bits[1 - turn]]
+            pltpu.make_async_copy(held.at[core], out_ref.at[g], local.at[g]).start()
+            push(held.at[1 - core], out_ref.at[g], send_c.at[g], recv_c.at[g], sibling).start()
+
+    for g in range(count):
+        for turn in range(2):
+            step_one(g, turn).start()
+            fetch(g, turn).start()
+    many = rows_ref.shape[0]
+    for a in range(many):
+        for j in range(2):
+            stays = jnp.logical_and(home, 2 * core + j == z)
+
+            @pl.when(stays)
+            def _(a=a, j=j):
+                pltpu.make_async_copy(rows_ref.at[a, j], back_ref.at[a, z % 2], local.at[count + a]).start()
+
+            @pl.when(jnp.logical_not(stays))
+            def _(a=a, j=j):
+                target = (plane * 2 + z // 2, 2 * core + j)
+                push(
+                    rows_ref.at[a, j], back_ref.at[a, z % 2], send_r.at[a, j], recv_r.at[a, z % 2], target
+                ).start()
+
+    gains = []
+    for step in range(1, 8):
+        mate = lax.rem(dp + step, 8)
+        gains.append(
+            push(gain_ref.at[mate], gain_got.at[8 - step], send_g.at[step], recv_g.at[8 - step], (mate, z))
+        )
+    for copy in gains:
+        copy.start()
+
+    @pl.when(home)
+    def _():
+        pltpu.make_async_copy(cond_ref, cond_out.at[z % 2], local.at[count + many]).start()
+        for step in range(1, 4):
+            target = (dp, lax.rem(z + step, 4))
+            push(cond_ref, cond_out.at[z % 2], send_k.at[step], recv_k.at[z % 2], target).start()
+
+    for copy in gains:
+        copy.wait()
+    total = gain_ref[dp]
+    for step in range(1, 8):
+        total = total + gain_got[step]
+    gain_sum[...] = total
+    sums = []
+    for step in range(1, 4):
+        target = (dp, lax.rem(z + step, 4))
+        sums.append(push(gain_sum, gain_line.at[4 - step], send_h.at[step], recv_h.at[4 - step], target))
+    for copy in sums:
+        copy.start()
+
+    pieces = [(g, turn) for g in range(count) for turn in range(2)]
+    lag = 2
+    for i in range(len(pieces) + lag):
+        if i < len(pieces):
+            after_one(*pieces[i])
+        if i >= lag:
+            after_two(*pieces[i - lag])
+
+    for copy in sums:
+        copy.wait()
+    total = gain_sum[...]
+    for step in range(1, 4):
+        total = total + gain_line[step]
+    gain_out[...] = total
+    for g in range(count):
+        for turn in range(2):
+            goal = z_of(turn)
+            step_one(g, turn).wait_send()
+            step_two(g, turn).wait_send()
+
+            @pl.when(z != goal)
+            def _(g=g, turn=turn):
+                line_copy(g, turn, 0, above).wait_send()
+
+        @pl.when(home)
+        def _(g=g):
+            pltpu.make_async_copy(out_ref.at[g], out_ref.at[g], local.at[g]).wait()
+            push(out_ref.at[g], out_ref.at[g], send_c.at[g], recv_c.at[g], sibling).wait_send()
+
+        @pl.when(jnp.logical_not(home))
+        def _(g=g):
+            push(out_ref.at[g], out_ref.at[g], send_c.at[g], recv_c.at[g], sibling).wait_recv()
+
+    for a in range(many):
+        for j in range(2):
+            stays = jnp.logical_and(home, 2 * core + j == z)
+
+            @pl.when(stays)
+            def _(a=a, j=j):
+                pltpu.make_async_copy(rows_ref.at[a, j], back_ref.at[a, z % 2], local.at[count + a]).wait()
+
+            @pl.when(jnp.logical_not(stays))
+            def _(a=a, j=j):
+                push(rows_ref.at[a, j], back_ref.at[a, 0], send_r.at[a, j], recv_r.at[a, 0], sibling).wait_send()
+
+            @pl.when(jnp.logical_not(jnp.logical_and(home, z % 2 == j)))
+            def _(a=a, j=j):
+                push(rows_ref.at[a, j], back_ref.at[a, j], send_r.at[a, j], recv_r.at[a, j], sibling).wait_recv()
+
+    @pl.when(home)
+    def _():
+        pltpu.make_async_copy(cond_ref, cond_out.at[z % 2], local.at[count + many]).wait()
+        for step in range(1, 4):
+            push(cond_ref, cond_out.at[0], send_k.at[step], recv_k.at[0], sibling).wait_send()
+
+    for s in range(2):
+
+        @pl.when(z != 2 * core + s)
+        def _(s=s):
+            push(cond_ref, cond_out.at[s], send_k.at[1], recv_k.at[s], sibling).wait_recv()
+
+
+def share_moves(grads, groups, rows, gains, cond):
+    count = len(groups)
+    depth, width = grads[0].shape[1] // 8, grads[0].shape[2] // 2
+    many = rows.shape[0]
+    return pl.pallas_call(
+        functools.partial(share_kernel, groups=groups, arrays=len(grads)),
+        out_shape=[
+            jax.ShapeDtypeStruct((count, depth, width), BF),
+            jax.ShapeDtypeStruct(rows.shape, BF),
+            jax.ShapeDtypeStruct(gains.shape[1:], F32),
+            jax.ShapeDtypeStruct((2, *cond.shape), BF),
+        ],
+        in_specs=any_specs(len(grads)) + near_specs(3),
+        out_specs=near_specs(1) + any_specs(1) + near_specs(1) + any_specs(1),
+        scratch_shapes=[
+            pltpu.VMEM((count, 2, 2, 2, depth, width), BF),
+            pltpu.VMEM((count, 2, 2, 2, depth, width), BF),
+            pltpu.VMEM((count, 2, 2, depth, width), BF),
+            pltpu.VMEM((count, 2, 2, 2, depth, width), BF),
+            pltpu.VMEM(gains.shape, F32),
+            pltpu.VMEM(gains.shape[1:], F32),
+            pltpu.VMEM((4, *gains.shape[1:]), F32),
+            dma(count, 2),
+            dma(count, 2),
+            dma(count, 2),
+            dma(count, 2),
+            dma(count, 2),
+            dma(count, 2),
+            dma(count, 2, 2),
+            dma(count),
+            dma(count),
+            dma(many, 2),
+            dma(many, 2),
+            dma(8),
+            dma(8),
+            dma(4),
+            dma(4),
+            dma(4),
+            dma(2),
+            dma(count + many + 1),
+        ],
+        compiler_params=pltpu.CompilerParams(
+            collective_id=5, has_side_effects=True, vmem_limit_bytes=ROOM
+        ),
+        name="share_moves",
+    )(*[grad.reshape(grad.shape[0], 2, 2, 2, depth, 2 * width) for grad in grads], rows, gains, cond)
+
+
 def chip_shards(
     inputs,
     context,
@@ -811,10 +1283,6 @@
     padded = inputs.shape[1] * 4
     half_rows = padded // 2
 
-    def sibling_owned(value):
-        mine = take(value, z % 2, 0)
-        return jnp.where(core == z // 2, mine, swap(mine, CORE))
-
     def own_half(value):
         return take(value.reshape(2, half_rows, -1), core, 0)
 
@@ -824,6 +1292,7 @@
     pair_sum = lambda value: value + swap(value.astype(BF), CORE).astype(F32)
 
     cc_depth = cross_context.shape[1]
+    tokens = context.shape[1]
     narrow = jnp.concatenate(
         [
             self_qkv,
@@ -836,14 +1305,20 @@
     depth, units = gate_up.shape[1], gate_up.shape[2]
     wide = jnp.concatenate([gate_up, down_proj.T[None]]).astype(BF)
     wide = jnp.moveaxis(wide.reshape(3, depth, 4, units // 4), 2, 1)
-    sequence, wide = first_moves(inputs, wide)
-    quarter = lax.all_gather(wide, "tensor", axis=0)
+    room = -tokens % 16
+    cond = jnp.pad(take(context, z % 2, 0), ((0, room), (0, 0)))
+    size = jnp.broadcast_to(take(lengths, z % 2, 0), (8, 128))
+    sequence, wide, cond, size = first_moves(inputs, wide, cond, size)
     stream = sequence.reshape(padded, model_width).astype(F32)
-    length = sibling_owned(lengths[:, None])[0]
-    cond = sibling_owned(context)
-    narrow_all = narrow_moves(narrow, ((0, 3), (3, 4)))
-    qkv_whole, so_whole, cq_whole, co_whole = narrow_all[:3], narrow_all[3], narrow_all[4], narrow_all[6]
-    cc_whole = narrow_all[5].reshape(8, 2, cc_depth, -1)
+    length = take(size, z // 2, 0)[0, 0]
+    cond = take(cond, z // 2, 0)[:tokens]
+    qkv_whole, so_whole, cq_whole, cc_whole, co_whole, gu_whole = weights_moves(
+        narrow, wide, ((0, 0), (0, 1), (0, 2), (1, 0), (2, 0), (3, 0), (4, 0)), 2
+    )
+    wide, qkv_whole = lax.optimization_barrier((wide, qkv_whole))
+    quarter = lax.all_gather(wide[2:], "tensor", axis=0)
+    so_whole, cq_whole, co_whole = so_whole[0], cq_whole[0], co_whole[0]
+    cc_whole = cc_whole[0].reshape(8, 2, cc_depth, -1)
     cc_whole = jnp.moveaxis(cc_whole, 1, 0).reshape(2, 8 * cc_depth, -1)
     cot_half = rows_in(cotangent, z)
     cot = both_halves(cot_half, swap(cot_half, CORE)).astype(F32)
@@ -869,12 +1344,11 @@
     stream = stream + row_keep * pair_sum(branch)
     stream_half = own_half(stream)
     normed_three, scaled_three, inverse_three = norm_rows(stream_half, norm_gains[2])
-    rows_three, wide_all = second_moves(
+    rows_three, down_whole = second_moves(
         normed_three.astype(BF).reshape(2, -1, model_width), quarter
     )
     rows_three = rows_three.reshape(-1, model_width)
-    wide_all = wide_all.reshape(3, model_width, units)
-    gu_whole, down_whole = wide_all[:2], wide_all[2]
+    down_whole = down_whole.reshape(model_width, units)
     gate_rows = jnp.einsum("td,kde->kte", rows_three, gu_whole, preferred_element_type=F32)
     sigmoid_gate = jax.nn.sigmoid(gate_rows[0])
     hidden = (gate_rows[0] * sigmoid_gate * gate_rows[1]).astype(BF)
@@ -888,17 +1362,20 @@
     grad_upper = grad_hidden * gate_rows[0] * sigmoid_gate
     grad_expand = jnp.stack([grad_gate, grad_upper]).astype(BF)
     partial_value = jnp.einsum("ktf,kdf->td", grad_expand, gu_whole, preferred_element_type=F32)
+    grad_down = jnp.einsum("td,tf->df", grad_branch, hidden, preferred_element_type=F32)
+    grad_gates = jnp.einsum("td,ktf->kdf", rows_three, grad_expand, preferred_element_type=F32)
+    sums, wide_grads = third_moves(
+        partial_value.astype(BF).reshape(4, 2, -1, model_width),
+        [grad_gates.astype(BF), grad_down.astype(BF)[None]],
+    )
     grad_norm, gain_rows = norm_back(
-        plane_sums(partial_value), scaled_three, inverse_three, norm_gains[2]
+        sums.reshape(half_rows, model_width), scaled_three, inverse_three, norm_gains[2]
     )
     gain_three = jnp.sum(gain_rows, axis=0)
+    wide_grads = lax.psum_scatter(wide_grads, "tensor", scatter_dimension=0, tiled=False)
     branch = jnp.einsum("tf,df->td", hidden, down_whole, preferred_element_type=F32)
     stream_half = stream_half + keep_half * plane_sums(branch)
-    output = rows_out((keep_half * stream_half).astype(BF), z)
-    grad_down = jnp.einsum("td,tf->df", grad_branch, hidden, preferred_element_type=F32)
-    grad_gates = jnp.einsum("td,ktf->kdf", rows_three, grad_expand, preferred_element_type=F32)
-    grad_gates = wide_share(grad_gates, place)
-    grad_down = wide_share(grad_down[None], place)[0]
+    output = (keep_half * stream_half).astype(BF)
 
     grad_stream = grad_stream + both_halves(grad_norm, swap(grad_norm.astype(BF), CORE).astype(F32))
     grad_branch = (row_keep * grad_stream).astype(BF)
@@ -916,43 +1393,54 @@
     grad_pairs = jnp.stack([grad_key, grad_value])
     grad_cc = jnp.einsum("sd,kse->kde", cond, grad_pairs, preferred_element_type=F32)
     grad_cc = jnp.moveaxis(grad_cc.reshape(2, 8, cc_depth, -1), 0, 1).reshape(model_width, -1)
-    crossed = narrow_share(
-        jnp.stack([grad_merge.astype(BF), grad_cross.astype(BF), grad_cc.astype(BF)]), place
-    )
     context_part = jnp.einsum("kse,kde->sd", grad_pairs, cc_whole, preferred_element_type=F32)
-    context_all = lax.all_gather(pair_sum(context_part).astype(BF), "tensor", axis=0)
-    grad_context = take(context_all.reshape(2, 2, *context_part.shape), core, 0).astype(F32)
+    context_part = jnp.pad(pair_sum(context_part).astype(BF), ((0, room), (0, 0)))
 
     grad_stream = grad_stream + grad_norm
     grad_branch = (row_keep * grad_stream).astype(BF)
     grad_mixed = jnp.einsum("td,de->te", grad_branch, so_whole, preferred_element_type=F32).astype(BF)
     grad_after = jnp.einsum("td,te->de", grad_branch, mixed_one, preferred_element_type=F32)
-    after = narrow_share(grad_after.astype(BF)[None], place)[0]
     grad_triple = jnp.stack(
         attend_backward((qkv[0], qkv[1], qkv[2], logsum_one, grad_mixed, key_valid))
     )
     grad_self = jnp.einsum("td,kte->kde", normed_one, grad_triple, preferred_element_type=F32)
-    selfed = narrow_share(grad_self, place)
     partial_value = jnp.einsum("kte,kde->td", grad_triple, qkv_whole, preferred_element_type=F32)
     grad_norm, gain_rows = norm_back(
         pair_sum(partial_value), scaled_one, inverse_one, norm_gains[0]
     )
     gain_one = 0.5 * jnp.sum(gain_rows, axis=0)
-    grad_inputs = rows_out(own_half(grad_stream + grad_norm).astype(BF), z).astype(F32)
-    gains = lax.psum(jnp.stack([gain_one, gain_two, gain_three]), ("dp", "tensor"))
-    gains = lax.dynamic_slice_in_dim(gains, dp * (model_width // 8), model_width // 8, 1)
+    grad_inputs = own_half(grad_stream + grad_norm).astype(BF)
+    back = jnp.stack([output, grad_inputs]).reshape(2, 2, -1, model_width)
+    gains = jnp.stack([gain_one, gain_two, gain_three]).reshape(3, 8, -1)
+    gains = jnp.pad(jnp.moveaxis(gains, 0, 1), ((0, 0), (0, 5), (0, 0)))
+    shares, back, gains, conds = share_moves(
+        [
+            grad_merge.astype(BF)[None],
+            grad_cross.astype(BF)[None],
+            grad_cc.astype(BF)[None],
+            grad_after.astype(BF)[None],
+            grad_self.astype(BF),
+        ],
+        ((0, 0), (1, 0), (2, 0), (3, 0), (4, 0), (4, 1), (4, 2)),
+        back,
+        gains,
+        context_part,
+    )
+    shared = lax.all_to_all(wide_grads, "dp", 1, 1, axis_index_groups=[[0, 2, 4, 6], [1, 3, 5, 7]])
+    shared = jnp.moveaxis(shared, 1, 2).reshape(3, depth, units).astype(F32)
+    shares = shares.astype(F32)
     return (
-        output,
-        grad_inputs,
-        grad_context,
-        selfed.astype(F32),
-        after.T.astype(F32),
-        crossed[1].astype(F32),
-        crossed[2].reshape(2, cc_depth, -1).astype(F32),
-        crossed[0].T.astype(F32),
-        grad_gates.astype(F32),
-        grad_down.T.astype(F32),
-        gains,
+        back[0],
+        back[1].astype(F32),
+        conds[:, :tokens].astype(F32),
+        shares[4:],
+        shares[3].T,
+        shares[1],
+        shares[2].reshape(2, cc_depth, -1),
+        shares[0].T,
+        shared[:2],
+        shared[2].T,
+        gains[:3],
     )
 
 

time: 1100 us -> 905 us (0.82)
  Pallas kernels: 237 us -> 461 us
  local copies, waits for them, and re-layouts: 236 us -> 75 us
  blocking collectives: 98.6 us -> 0 us
  starting transfers between devices: 107 us -> 21.9 us
  waiting for transfers between devices: 85.2 us -> 24.7 us
  other arithmetic: 121 us -> 93.3 us
  matrix products: 184 us -> 204 us
    pallas_call x1 -> x3, Pallas kernels: 177 us -> 403 us  [the longest x1 194 us: share_moves(): pl.pallas_call(functools.partial(share_kernel, groups=groups, arrays=len(...]
    ppermute x42 -> x15, starting transfers between devices: 93.8 us -> 9.84 us  [swap(): return lax.ppermute(value, 'dp', [(i, i ^ bit) for i in range(count)])]
    psum x1 -> x0, blocking collectives: 64.4 us -> none  [chip_shards(): lax.psum(jnp.stack([gain_one, gain_two, gain_three]), ('dp', 'tensor'))]
    ppermute x42 -> x15, waiting for transfers between devices: 84.8 us -> 24.6 us  [swap(): return lax.ppermute(value, 'dp', [(i, i ^ bit) for i in range(count)])]
    reshape x3 -> x0, local copies, waits for them, and re-layouts: 40.5 us -> none  [the longest x2 25.5 us: wide_share(): grid = grads.astype(BF).reshape(count, 2, 2, 2, depth, 4, width // 4)]
    unnamed x254 -> x188, local copies, waits for them, and re-layouts: 56.2 us -> 17.3 us
    dynamic_slice x9 -> x2, local copies, waits for them, and re-layouts: 38 us -> 1.01 us  [take(): return lax.dynamic_index_in_dim(value, index, axis, keepdims=False)]
    all_gather x1 -> x0, blocking collectives: 34.2 us -> none  [chip_shards(): lax.all_gather(pair_sum(context_part).astype(BF), 'tensor', axis=0)]
  transfers between devices with their start and end apart: 54 -> 20, of which waited for: 13 -> 4; matrix products, arithmetic and copies ran while one was open for 39% -> 29% of each run, Pallas kernels for 19% -> 44%
where the time goes in v2:
time: 905 us; the launch traced here: 897 us
  Pallas kernels  461 us (51%)
  matrix products  204 us (23%)
  other arithmetic  93.3 us (10%)
  local copies, waits for them, and re-layouts  75 us (8%)
  waiting for transfers between devices  24.7 us (3%)
  starting transfers between devices  21.9 us (2%)
  between operations  16 us (2%)
    pallas_call x1, Pallas kernels, share_moves(): pl.pallas_call(functools.partial(share_kernel, groups=groups, arrays=len(...  194 us
    pallas_call x1, Pallas kernels, weights_moves(): pl.pallas_call(functools.partial(weights_kernel, groups=groups, wides=wid...  176 us
    pallas_call x1, Pallas kernels, third_moves(): pl.pallas_call(functools.partial(third_kernel, counts=counts), out_shape=...  33.1 us
    pallas_call x1, Pallas kernels, second_moves(): pl.pallas_call(second_kernel, out_shape=[jax.ShapeDtypeStruct((4, *rows.s...  32.4 us
    pallas_call x1, Pallas kernels, first_moves(): pl.pallas_call(first_kernel, out_shape=[jax.ShapeDtypeStruct((4, height,...  26.2 us
    ppermute x15, waiting for transfers between devices, swap(): return lax.ppermute(value, 'dp', [(i, i ^ bit) for i in range(count)])  24.6 us
    dot_general x1, matrix products, chip_shards(): jnp.einsum('td,ktf->kdf', rows_three, grad_expand, preferred_element_type...  18.2 us
  transfers between devices with their start and end apart: 20, of which 4 were waited for; matrix products, arithmetic and copies ran while one was open for 29% of the time, Pallas kernels for 44%

profile of v2, /device:TPU:0, one launch (start us, length us, event | category | flops | bytes accessed | tf_op | source)
XLA Modules:
  0.0 896.6 jit_solution(11584731571596418436)
XLA Ops:
  7.3 2.2 dynamic-slice_bitcast_fusion.1
  9.5 4.9 collective-permute-start
  14.4 3.0 collective-permute-start.1
  25.6 26.2 %first_moves.1 = (bf16[4,136,1536]{2,1,0:T(8,128)(2,1)}, bf16[3,4,192,384]{3,2,1,0:T(8,128)(2,1)}, bf16[2,144,768]{2,1,0:T(8,128)(2,1)}, s32[2,8,128]{2,1,0:T(8,128)}) custom-call(bf16[2,136,1536]{2,1,0:T(8,128)(2,1)} %rows_ref.1, bf16[3,4,192,384]{3,2,1,0:T(8,128)(2,1)} %maximum_bitcast_fusion.wide_ref, bf16[144,768]{1,0:T(8,128)(2,1)} %pad.11.cond_ref, ...), custom_call_target="tpu_custom_call" | custom-call | tf_op jit(solution)/shard_map/first_moves/pallas_call | solution.py:553
  53.5 2.0 multiply_reduce_fusion.8
  61.2 175.5 %weights_moves.1 = (bf16[3,4,2,192,768]{4,3,2,1,0:T(8,128)(2,1)}, bf16[1,4,2,192,768]{4,3,2,1,0:T(8,128)(2,1)}, bf16[1,4,2,192,768]{4,3,2,1,0:T(8,128)(2,1)}, bf...) custom-call(bf16[7,192,384]{2,1,0:T(8,128)(2,1)} %copy-done.35, ...), custom_call_target="tpu_custom_call" | custom-call | tf_op jit(solution)/shard_map/weights_moves/pallas_call | solution.py:750
  237.4 7.9 convert_bitcast_fusion.2
  246.6 2.2 copy.83
  253.2 10.4 %fusion.81 = (f32[12,544]{1,0:T(8,128)S(1)}, f32[12,544,544]{1,2,0:T(8,128)}) fusion(bf16[544,12,64]{0,2,1:T(8,128)(2,1)} %bitcast.397, bf16[544,12,64]{0,2,1:T(8,128)(2,1)S(1)} %bitcast.392, pred[544]{0:T(1024)(128)(4,1)S(1)} %iota_compare_fusion), kind=kOutput, calls=%fused_computation.236 | convolution fusion | flops 465204864 | bytes 15902752 | tf_op jit(solution)/shard_map/qhd,khd->hqk/dot_general | solution.py:37
  263.6 8.2 fusion
  271.8 9.0 %fusion.40 = bf16[12,64,544]{2,1,0:T(8,128)(2,1)S(1)} fusion(bf16[544,12,64]{0,2,1:T(8,128)(2,1)S(1)} %bitcast.412, f32[12,544,544]{1,2,0:T(8,128)} %get-tuple-element.135, f32[12,544]{1,0:T(8,128)S(1)} %fusion, f32[12,544]{1,0:T(8,128)S(1)} %get-tuple-element.134), kind=kOutput, calls=%fused_computation.114 | convolution fusion | flops 465629184 | bytes 15928320 | tf_op jit(solution)/shard_map/hqk,khd->qhd/dot_general | solution.py:50
  280.8 4.1 fusion.82
  285.0 1.9 slice.189
  301.6 2.4 collective-permute-start.5
  304.0 1.9 maximum_convert_fusion
  305.9 3.9 multiply_add_fusion.2
  309.8 2.2 reduce_sum.174
  312.1 2.6 multiply_reduce_fusion.7
  315.1 4.1 convolution_convert_fusion.9
  328.2 2.1 collective-permute-start.8
  332.7 8.5 collective-permute-done.7
  342.0 7.5 collective-permute-done.8
  355.2 32.4 %second_moves.1 = (bf16[4,2,136,1536]{3,2,1,0:T(8,128)(2,1)}, bf16[1,4,2,192,1536]{4,3,2,1,0:T(8,128)(2,1)}) custom-call(bf16[2,136,1536]{2,1,0:T(8,128)(2,1)} %multiply_convert_fusion.11.rows_ref, bf16[4,1,4,192,384]{4,3,2,1,0:T(8,128)(2,1)} %bitcast.429), custom_call_target="tpu_custom_call" | custom-call | tf_op jit(solution)/shard_map/second_moves/pallas_call | solution.py:836
  387.6 17.2 %convolution_bitcast_fusion = f32[2,1088,1536]{2,1,0:T(8,128)} fusion(bf16[1088,1536,1]{1,0,2:T(8,128)(2,1)} %bitcast.456, bf16[2,1536,1536]{2,1,0:T(8,128)(2,1)} %bitcast.446), kind=kOutput, calls=%fused_computation.7 | convolution fusion | flops 10267656192 | bytes 26148864 | tf_op jit(solution)/shard_map/td,kde->kte/dot_general | solution.py:1352
  404.8 12.3 %fusion.23 = (bf16[1,1088,1536]{2,1,0:T(8,128)(2,1)}, bf16[1,1088,1536]{2,1,0:T(8,128)(2,1)}) fusion(f32[2,1088,1536]{2,1,0:T(8,128)} %convolution_bitcast_fusion, bf16[1088,1536]{1,0:T(8,128)(2,1)S(1)} %copy-done.50, bf16[1536,1536]{1,0:T(8,128)(2,1)S(1)} %bitcast.452), kind=kOutput, calls=%fused_computation.70 | convolution fusion | flops 5155553280 | bytes 28114944 | tf_op jit(solution)/shard_map/td,df->tf/dot_general | solution.py:1358
  417.1 13.9 %fusion.6 = bf16[1088,1536]{1,0:T(8,128)(2,1)} fusion(bf16[2,1536,1536]{2,1,0:T(8,128)(2,1)S(1)} %bitcast.449, bf16[1,1088,1536]{2,1,0:T(8,128)(2,1)} %get-tuple-element.103, bf16[1,1088,1536]{2,1,0:T(8,128)(2,1)} %get-tuple-element.102), kind=kOutput, calls=%fused_computation.14 | convolution fusion | flops 10272669696 | bytes 19464192 | tf_op jit(solution)/shard_map/ktf,kdf->td/dot_general | solution.py:1364
  431.0 18.2 %convolution_convert_fusion = bf16[2,1536,1536]{1,2,0:T(8,128)(2,1)} fusion(bf16[1088,1536,1]{1,0,2:T(8,128)(2,1)} %bitcast.457, bf16[1,1088,1536]{2,1,0:T(8,128)(2,1)} %get-tuple-element.103, bf16[1,1088,1536]{2,1,0:T(8,128)(2,1)} %get-tuple-element.102), kind=kOutput, calls=%fused_computation.9 | convolution fusion | flops 10275717120 | bytes 19464192 | tf_op jit(solution)/shard_map/td,ktf->kdf/dot_general | solution.py:1366
  449.2 13.3 %convolution_convert_fusion.2 = bf16[1536,1536]{1,0:T(8,128)(2,1)} fusion(bf16[1088,1536]{1,0:T(8,128)(2,1)S(1)} %copy-done.50, f32[2,1088,1536]{2,1,0:T(8,128)} %convolution_bitcast_fusion), kind=kOutput, calls=%fused_computation.16 | convolution fusion | flops 5146214400 | bytes 21430272 | tf_op jit(solution)/shard_map/td,tf->df/dot_general | solution.py:1365
  462.5 9.9 %convolution_convert_fusion.1 = bf16[1088,1536]{1,0:T(8,128)(2,1)} fusion(bf16[1536,1536]{1,0:T(8,128)(2,1)S(1)} %bitcast.455, f32[2,1088,1536]{2,1,0:T(8,128)} %convolution_bitcast_fusion), kind=kOutput, calls=%fused_computation.15 | convolution fusion | flops 5145526272 | bytes 21430272 | tf_op jit(solution)/shard_map/tf,df->td/dot_general | solution.py:1376
  472.4 33.1 %third_moves.1 = (f32[2,136,1536]{2,1,0:T(8,128)}, bf16[4,3,4,192,384]{4,3,2,1,0:T(8,128)(2,1)}) custom-call(bf16[4,2,136,1536]{3,2,1,0:T(8,128)(2,1)} %bitcast.425, bf16[2,4,2,192,1536]{4,3,2,1,0:T(8,128)(2,1)} %bitcast.395, bf16[1,4,2,192,1536]{4,3,2,1,0:T(8,128)(2,1)} %bitcast.410), custom_call_target="tpu_custom_call" | custom-call | tf_op jit(solution)/shard_map/third_moves/pallas_call | solution.py:948
  505.5 2.2 multiply_reduce_fusion.11
  507.9 3.6 fusion.75
  515.8 2.0 fusion.30
  517.8 2.7 pad_maximum_fusion.3
  521.7 2.4 convolution_convert_fusion.8
  524.0 1.9 copy.91
  526.0 3.5 multiply_reduce_fusion.1
  534.3 2.3 multiply_convert_fusion.10
  542.3 3.9 convolution_convert_fusion.4
  546.2 6.0 collective-permute-done.12
  552.1 2.3 fusion.56
  555.4 3.5 convolution_convert_fusion.5
  558.9 2.0 convolution_convert_fusion.6
  563.2 2.7 collective-permute-done.14
  565.8 2.0 fusion.53
  574.7 2.4 convolution_convert_fusion.7
  578.6 9.5 %fusion.42 = bf16[12,64,544]{2,1,0:T(8,128)(2,1)} fusion(bf16[544,12,64]{0,2,1:T(8,128)(2,1)S(1)} %bitcast.401, f32[12,544,544]{1,2,0:T(8,128)} %get-tuple-element.135, f32[12,544]{1,0:T(8,128)S(1)} %copy-done.45), kind=kOutput, calls=%fused_computation.116 | convolution fusion | flops 462077952 | bytes 15902208 | tf_op jit(solution)/shard_map/hqk,qhd->khd/dot_general | solution.py:69
  588.1 2.2 copy.103
  590.3 11.0 %multiply_reduce_fusion = (f32[12,544]{1,0:T(8,128)S(1)}, f32[12,544,544]{1,2,0:T(8,128)}) fusion(f32[12,544,544]{1,2,0:T(8,128)} %get-tuple-element.135, f32[12,544]{1,0:T(8,128)S(1)} %copy-done.45, bf16[544,12,64]{0,2,1:T(8,128)(2,1)S(1)} %bitcast.402, bf16[544,12,64]{0,2,1:T(8,128)(2,1)} %bitcast.411), kind=kOutput, calls=%fused_computation.1 | convolution fusion | flops 465204864 | bytes 30133248 | tf_op jit(solution)/shard_map/qhd,khd->hqk/dot_general | solution.py:66
  601.3 11.9 %multiply_convert_fusion = bf16[12,544,544]{1,2,0:T(8,128)(2,1)S(1)} fusion(f32[12,544,544]{1,2,0:T(8,128)} %get-tuple-element.147, f32[12,544,544]{1,2,0:T(8,128)} %get-tuple-element.135, f32[12,544]{1,0:T(8,128)S(1)} %get-tuple-element.146, f32[12,544]{1,0:T(8,128)S(1)} %copy-done.45), kind=kLoop, calls=%fused_computation | loop fusion | flops 14204928 | bytes 35564544 | tf_op jit(solution)/shard_map/convert_element_type | solution.py:68
  613.2 3.7 multiply_convert_fusion.8
  616.9 2.3 copy.102
  619.3 6.1 multiply_convert_fusion.9
  626.9 10.1 %bitcast_convert_fusion = (bf16[544,1536]{1,0:T(8,128)(2,1)}, f32[544,1536,1]{1,0,2:T(8,128)}) fusion(bf16[3,1536,768]{2,1,0:T(8,128)(2,1)} %bitcast.451, bf16[1,544,768]{2,1,0:T(8,128)(2,1)} %copy.103, bf16[1,544,768]{2,1,0:T(8,128)(2,1)} %copy.102, bf16[1,544,768]{2,1,0:T(8,128)(2,1)S(1)} %copy.101), kind=kOutput, calls=%fused_computation.49 | convolution fusion | flops 3853713408 | bytes 14598144 | tf_op jit(solution)/shard_map/kte,kde->td/dot_general | solution.py:1407
  639.4 7.8 convert_bitcast_fusion
  647.2 10.4 %copy.104 = bf16[3,1536,768]{2,1,0:T(8,128)(2,1)} copy(bf16[3,1536,768]{1,2,0:T(8,128)(2,1)} %convert_bitcast_fusion) | data formatting | bytes 14155776 | tf_op jit(solution)/shard_map/convert_element_type | solution.py:1422
  657.7 5.7 convolution_convert_fusion.3
  663.5 3.3 multiply_reduce_fusion.4
  667.5 4.5 multiply_add_fusion
  672.1 2.9 copy.105
  675.0 3.6 all-to-all-start
  678.6 2.5 pad_maximum_fusion.5.refs_5_
  681.0 194.3 %share_moves.1 = (bf16[7,192,384]{2,1,0:T(8,128)(2,1)}, bf16[2,2,136,1536]{3,2,1,0:T(8,128)(2,1)}, f32[8,192]{1,0:T(8,128)}, bf16[2,144,768]{2,1,0:T(8,128)(2,1)}) custom-call(bf16[1,2,2,2,192,768]{5,4,3,2,1,0:T(8,128)(2,1)} %bitcast.427, bf16[1,2,2,2,192,768]{5,4,3,2,1,0:T(8,128)(2,1)} %bitcast.426, bf16[1,2,2,2,192,768]{5,4,3,2,1,0:T(8,128)(2,1)} %bitcast.394, ...), custom_call_target="tpu_custom_call" | custom-call | tf_op jit(solution)/shard_map/share_moves/pallas_call | solution.py:1221
  875.4 2.0 slice.245
  (329 shorter events, 98.5 us)
Async XLA Ops:
  7.2 14.0 %copy-start = (bf16[2,130,768]{2,0,1:T(2,128)(2,1)S(1)}, bf16[2,130,768]{2,0,1:T(2,128)(2,1)}, u32[]{:S(2)}) copy-start(bf16[2,130,768]{2,0,1:T(2,128)(2,1)} %param.13) | copy-start | bytes 1198084
  7.2 13.7 %copy-start.34 = (f32[2,192,1536]{2,1,0:T(8,128)S(1)}, f32[2,192,1536]{2,1,0:T(8,128)}, u32[]{:S(2)}) copy-start(f32[2,192,1536]{2,1,0:T(8,128)} %param.21) | copy-start | bytes 7077892
  7.2 348.0 %all-gather.3.cloned.1.call-start = ((), (), s32[]{:S(2)}) async-start(), calls=%async_computation.3 | async-start | bytes 2949120 | tf_op jit(solution)/shard_map/all_gather | solution.py:1319
  9.5 279.8 %collective-permute-start = (bf16[136,1536]{1,0:T(8,128)(2,1)}, bf16[136,1536]{1,0:T(8,128)(2,1)}, u32[]{:S(2)}, u32[]{:S(2)}) collective-permute-start(bf16[136,1536]{1,0:T(8,128)(2,1)} %get-tuple-element.130), channel_id=1, source_target_pairs={{0,0},{1,1},{2,4},{3,5},{4,2},{5,3},{6,6},{7,7},{8,8},{9,9},{10,12... | collective-permute-start | bytes 1253384 | tf_op jit(solution)/shard_map/ppermute | solution.py:372
  14.4 274.9 %collective-permute-start.1 = (bf16[136,1536]{1,0:T(8,128)(2,1)}, bf16[136,1536]{1,0:T(8,128)(2,1)}, u32[]{:S(2)}, u32[]{:S(2)}) collective-permute-start(bf16[136,1536]{1,0:T(8,128)(2,1)} %get-tuple-element.131), channel_id=1, source_target_pairs={{0,1},{1,0},{2,5},{3,4},{4,3},{5,2},{6,7},{7,6},{8,9},{9,8},{10,13... | collective-permute-start | bytes 1253384 | tf_op jit(solution)/shard_map/ppermute | solution.py:373
  25.6 31.4 %copy-start.49 = (f32[2,96,384]{2,1,0:T(8,128)S(1)}, f32[2,96,384]{2,1,0:T(8,128)}, u32[]{:S(2)}) copy-start(f32[2,96,384]{2,1,0:T(8,128)} %param.19) | copy-start | bytes 884740
  25.6 31.5 %copy-start.70 = (f32[3,1536]{1,0:T(4,128)S(1)}, f32[3,1536]{1,0:T(4,128)}, u32[]{:S(2)}) copy-start(f32[3,1536]{1,0:T(4,128)} %param.23) | copy-start | bytes 55300
  55.6 181.2 %copy-start.8 = (bf16[4,136,1536]{2,1,0:T(8,128)(2,1)S(1)}, bf16[4,136,1536]{2,1,0:T(8,128)(2,1)}, u32[]{:S(2)}) copy-start(bf16[4,136,1536]{2,1,0:T(8,128)(2,1)} %get-tuple-element.32) | copy-start | bytes 5013508
  55.7 181.7 %copy-start.56 = (f32[544]{0:T(1024)}, f32[544]{0:T(1024)S(1)}, u32[]{:S(2)}) copy-start(f32[544]{0:T(1024)S(1)} %div.79) | copy-start | bytes 6532
  57.1 180.2 %copy-start.52 = (f32[1536]{0:T(1024)}, f32[1536]{0:T(1024)S(1)}, u32[]{:S(2)}) copy-start(f32[1536]{0:T(1024)S(1)} %get-tuple-element.94) | copy-start | bytes 18436
  57.1 257.6 %copy-start.54 = (f32[1536]{0:T(1024)}, f32[1536]{0:T(1024)S(1)}, u32[]{:S(2)}) copy-start(f32[1536]{0:T(1024)S(1)} %get-tuple-element.95) | copy-start | bytes 18436
  57.2 180.1 %copy-start.58 = (f32[544]{0:T(1024)}, f32[544]{0:T(1024)S(1)}, u32[]{:S(2)}) copy-start(f32[544]{0:T(1024)S(1)} %rsqrt.32) | copy-start | bytes 6532
  237.4 7.9 copy-start.36
  246.6 5.3 copy-start.71
  251.9 11.7 %copy-start.21 = (bf16[1,544,768]{1,2,0:T(8,128)(2,1)}, bf16[1,544,768]{1,2,0:T(8,128)(2,1)S(1)}, u32[]{:S(2)}) copy-start(bf16[1,544,768]{1,2,0:T(8,128)(2,1)S(1)} %copy.85) | copy-start | bytes 2506756
  263.6 8.2 copy-start.48
  263.6 8.2 copy-start.26
  271.7 9.0 %copy-start.51 = (f32[12,544]{1,0:T(8,128)}, f32[12,544]{1,0:T(8,128)S(1)}, u32[]{:S(2)}) copy-start(f32[12,544]{1,0:T(8,128)S(1)} %fusion) | copy-start | bytes 78340
  271.8 9.0 %copy-start.74 = (bf16[1,4,2,192,768]{4,3,2,1,0:T(8,128)(2,1)S(1)}, bf16[1,4,2,192,768]{4,3,2,1,0:T(8,128)(2,1)}, u32[]{:S(2)}) copy-start(bf16[1,4,2,192,768]{4,3,2,1,0:T(8,128)(2,1)} %get-tuple-element.36) | copy-start | bytes 7077892
  284.9 21.1 %collective-permute-start.3 = (bf16[544,1536]{1,0:T(8,128)(2,1)}, bf16[544,1536]{1,0:T(8,128)(2,1)}, u32[]{:S(2)}, u32[]{:S(2)}) collective-permute-start(bf16[544,1536]{1,0:T(8,128)(2,1)} %get-tuple-element.136), channel_id=1, source_target_pairs={{0,4},{4,0},{8,12},{12,8},{16,20},{20,16},{24,28},{28,24},{1,5},{5... | collective-permute-start | bytes 5013512 | tf_op jit(solution)/shard_map/ppermute | solution.py:342
  287.0 385.1 %reduce-scatter.2.cloned.1.call-start = ((), (), s32[]{:S(2)}) async-start(), calls=%async_computation.2 | async-start | bytes 8847360 | tf_op jit(solution)/shard_map/reduce_scatter | solution.py:1375
  291.3 6.5 collective-permute-start.2
  294.3 26.6 %copy-start.27 = (bf16[1,130,768]{1,2,0:T(8,128)(2,1)}, bf16[1,130,768]{1,2,0:T(8,128)(2,1)S(1)}, u32[]{:S(2)}) copy-start(bf16[1,130,768]{1,2,0:T(8,128)(2,1)S(1)} %copy.114) | copy-start | bytes 599044
  296.3 56.4 %copy-start.60 = (f32[544]{0:T(1024)}, f32[544]{0:T(1024)S(1)}, u32[]{:S(2)}) copy-start(f32[544]{0:T(1024)S(1)} %fusion.64) | copy-start | bytes 6532
  299.0 5.0 copy-start.13
  299.0 5.0 copy-start.15
  300.5 5.4 copy-start.29
  301.6 25.4 %collective-permute-start.5 = (bf16[136,1536]{1,0:T(8,128)(2,1)}, bf16[136,1536]{1,0:T(8,128)(2,1)}, u32[]{:S(2)}, u32[]{:S(2)}) collective-permute-start(bf16[136,1536]{1,0:T(8,128)(2,1)} %get-tuple-element.127), channel_id=1, source_target_pairs={{0,8},{4,12},{8,0},{12,4},{16,24},{20,28},{24,16},{28,20},{1,9},{5... | collective-permute-start | bytes 1253384 | tf_op jit(solution)/shard_map/ppermute | solution.py:342
  304.0 16.7 %collective-permute-start.6 = (bf16[136,1536]{1,0:T(8,128)(2,1)}, bf16[136,1536]{1,0:T(8,128)(2,1)S(1)}, u32[]{:S(2)}, u32[]{:S(2)}) collective-permute-start(bf16[136,1536]{1,0:T(8,128)(2,1)} %get-tuple-element.126), channel_id=1, source_target_pairs={{0,16},{4,20},{8,24},{12,28},{16,0},{20,4},{24,8},{28,12},{1,17},{... | collective-permute-start | bytes 1253384 | tf_op jit(solution)/shard_map/ppermute | solution.py:342
  312.1 7.1 copy-start.62
  320.8 20.4 %collective-permute-start.7 = (bf16[2,136,1536]{2,1,0:T(8,128)(2,1)S(1)}, bf16[2,136,1536]{2,1,0:T(8,128)(2,1)S(1)}, u32[]{:S(2)}, u32[]{:S(2)}) collective-permute-start(bf16[2,136,1536]{2,1,0:T(8,128)(2,1)S(1)} %pad_maximum_fusion.9), channel_id=1, source_target_pairs={{0,8},{4,12},{8,0},{12,4},{16,24},{20,28},{24,16},{28,20},{1,9},{5... | collective-permute-start | bytes 2506760 | tf_op jit(solution)/shard_map/ppermute | solution.py:342
  326.9 25.9 %collective-permute-start.4 = (bf16[544,1536]{1,0:T(8,128)(2,1)S(1)}, bf16[544,1536]{1,0:T(8,128)(2,1)S(1)}, u32[]{:S(2)}, u32[]{:S(2)}) collective-permute-start(bf16[544,1536]{1,0:T(8,128)(2,1)S(1)} %get-tuple-element.140), channel_id=1, source_target_pairs={{0,4},{4,0},{8,12},{12,8},{16,20},{20,16},{24,28},{28,24},{1,5},{5... | collective-permute-start | bytes 5013512 | tf_op jit(solution)/shard_map/ppermute | solution.py:342
  327.0 25.8 %copy-start.3 = (f32[544,1536]{1,0:T(8,128)S(1)}, f32[544,1536]{1,0:T(8,128)}, u32[]{:S(2)}) copy-start(f32[544,1536]{1,0:T(8,128)} %multiply_add_fusion.2) | copy-start | bytes 10027012
  328.2 21.3 %collective-permute-start.8 = (bf16[2,136,1536]{2,1,0:T(8,128)(2,1)S(1)}, bf16[2,136,1536]{2,1,0:T(8,128)(2,1)S(1)}, u32[]{:S(2)}, u32[]{:S(2)}) collective-permute-start(bf16[2,136,1536]{2,1,0:T(8,128)(2,1)S(1)} %pad_maximum_fusion.10), channel_id=1, source_target_pairs={{0,16},{4,20},{8,24},{12,28},{16,0},{20,4},{24,8},{28,12},{1,17},{... | collective-permute-start | bytes 2506760 | tf_op jit(solution)/shard_map/ppermute | solution.py:342
  387.6 17.2 %copy-start.50 = (bf16[1088,1536]{1,0:T(8,128)(2,1)S(1)}, bf16[1088,1536]{1,0:T(8,128)(2,1)}, u32[]{:S(2)}) copy-start(bf16[1088,1536]{1,0:T(8,128)(2,1)} %fusion.57) | copy-start | bytes 10027012
  387.6 17.2 %copy-start.73 = (bf16[1,4,2,192,1536]{4,3,2,1,0:T(8,128)(2,1)S(1)}, bf16[1,4,2,192,1536]{4,3,2,1,0:T(8,128)(2,1)}, u32[]{:S(2)}) copy-start(bf16[1,4,2,192,1536]{4,3,2,1,0:T(8,128)(2,1)} %get-tuple-element.42) | copy-start | bytes 14155780
  387.6 29.5 %slice-start = ((s8[9437184]{0:T(1024)(128)(4,1)}), s8[4194304]{0:T(1024)(128)(4,1)S(1)}, s32[]{:S(2)}) async-start(s8[9437184]{0:T(1024)(128)(4,1)} %bitcast.447), calls=%async_computation.4 | async-start | bytes 8388608
  387.6 29.5 %slice-start.1 = ((s8[9437184]{0:T(1024)(128)(4,1)}), s8[4194304]{0:T(1024)(128)(4,1)S(1)}, s32[]{:S(2)}) async-start(s8[9437184]{0:T(1024)(128)(4,1)} %bitcast.447), calls=%async_computation.5 | async-start | bytes 8388608
  404.8 12.3 %slice-start.2 = ((s8[9437184]{0:T(1024)(128)(4,1)}), s8[1048576]{0:T(1024)(128)(4,1)S(1)}, s32[]{:S(2)}) async-start(s8[9437184]{0:T(1024)(128)(4,1)} %bitcast.447), calls=%async_computation.6 | async-start | bytes 2097152
  417.1 45.4 %slice-start.3 = ((s8[4718592]{0:T(1024)(128)(4,1)}), s8[524288]{0:T(1024)(128)(4,1)S(1)}, s32[]{:S(2)}) async-start(s8[4718592]{0:T(1024)(128)(4,1)} %bitcast.453), calls=%async_computation.7 | async-start | bytes 1048576
  431.0 31.5 %slice-start.4 = ((s8[4718592]{0:T(1024)(128)(4,1)}), s8[4194304]{0:T(1024)(128)(4,1)S(1)}, s32[]{:S(2)}) async-start(s8[4718592]{0:T(1024)(128)(4,1)} %bitcast.453), calls=%async_computation.8 | async-start | bytes 8388608
  511.5 4.3 collective-permute-start.9
  512.6 26.0 %collective-permute-start.11 = (bf16[2,136,1536]{2,1,0:T(8,128)(2,1)}, bf16[2,136,1536]{2,1,0:T(8,128)(2,1)}, u32[]{:S(2)}, u32[]{:S(2)}) collective-permute-start(bf16[2,136,1536]{2,1,0:T(8,128)(2,1)} %pad_maximum_fusion.11), channel_id=1, source_target_pairs={{0,8},{4,12},{8,0},{12,4},{16,24},{20,28},{24,16},{28,20},{1,9},{5... | collective-permute-start | bytes 2506760 | tf_op jit(solution)/shard_map/ppermute | solution.py:342
  514.6 31.5 %collective-permute-start.13 = (bf16[2,136,1536]{2,1,0:T(8,128)(2,1)}, bf16[2,136,1536]{2,1,0:T(8,128)(2,1)}, u32[]{:S(2)}, u32[]{:S(2)}) collective-permute-start(bf16[2,136,1536]{2,1,0:T(8,128)(2,1)} %pad_maximum_fusion.12), channel_id=1, source_target_pairs={{0,16},{4,20},{8,24},{12,28},{16,0},{20,4},{24,8},{28,12},{1,17},{... | collective-permute-start | bytes 2506760 | tf_op jit(solution)/shard_map/ppermute | solution.py:342
  538.5 29.4 %collective-permute-start.10 = (bf16[544,1536]{1,0:T(8,128)(2,1)S(1)}, bf16[544,1536]{1,0:T(8,128)(2,1)S(1)}, u32[]{:S(2)}, u32[]{:S(2)}) collective-permute-start(bf16[544,1536]{1,0:T(8,128)(2,1)S(1)} %get-tuple-element.144), channel_id=1, source_target_pairs={{0,4},{4,0},{8,12},{12,8},{16,20},{20,16},{24,28},{28,24},{1,5},{5... | collective-permute-start | bytes 5013512 | tf_op jit(solution)/shard_map/ppermute | solution.py:342
  539.9 12.2 %collective-permute-start.12 = (bf16[136,1536]{1,0:T(8,128)(2,1)S(1)}, bf16[136,1536]{1,0:T(8,128)(2,1)S(1)}, u32[]{:S(2)}, u32[]{:S(2)}) collective-permute-start(bf16[136,1536]{1,0:T(8,128)(2,1)S(1)} %fusion.54), channel_id=1, source_target_pairs={{0,16},{4,20},{8,24},{12,28},{16,0},{20,4},{24,8},{28,12},{1,17},{... | collective-permute-start | bytes 1253384 | tf_op jit(solution)/shard_map/ppermute | solution.py:342
  541.9 20.5 %collective-permute-start.16 = (bf16[130,768]{1,0:T(8,128)(2,1)S(1)}, bf16[130,768]{1,0:T(8,128)(2,1)S(1)}, u32[]{:S(2)}, u32[]{:S(2)}) collective-permute-start(bf16[130,768]{1,0:T(8,128)(2,1)S(1)} %get-tuple-element.150), channel_id=1, source_target_pairs={{0,4},{4,0},{8,12},{12,8},{16,20},{20,16},{24,28},{28,24},{1,5},{5... | collective-permute-start | bytes 599048 | tf_op jit(solution)/shard_map/ppermute | solution.py:342
  546.1 9.2 %copy-start.39 = (bf16[2,272,1536]{2,1,0:T(8,128)(2,1)S(1)}, bf16[2,272,1536]{2,1,0:T(8,128)(2,1)}, u32[]{:S(2)}) copy-start(bf16[2,272,1536]{2,1,0:T(8,128)(2,1)} %copy-done.38) | copy-start | bytes 5013508
  546.1 9.2 %copy-start.83 = (bf16[12,64,544]{2,1,0:T(8,128)(2,1)S(1)}, bf16[12,64,544]{2,1,0:T(8,128)(2,1)}, u32[]{:S(2)}) copy-start(bf16[12,64,544]{2,1,0:T(8,128)(2,1)} %copy-done.82) | copy-start | bytes 2506756
  554.4 11.5 %collective-permute-start.14 = (bf16[136,1536]{1,0:T(8,128)(2,1)S(1)}, bf16[136,1536]{1,0:T(8,128)(2,1)S(1)}, u32[]{:S(2)}, u32[]{:S(2)}) collective-permute-start(bf16[136,1536]{1,0:T(8,128)(2,1)S(1)} %get-tuple-element.105), channel_id=1, source_target_pairs={{0,8},{4,12},{8,0},{12,4},{16,24},{20,28},{24,16},{28,20},{1,9},{5... | collective-permute-start | bytes 1253384 | tf_op jit(solution)/shard_map/ppermute | solution.py:342
  601.3 11.9 %copy-start.23 = (bf16[1,544,768]{1,2,0:T(8,128)(2,1)S(1)}, bf16[1,544,768]{1,2,0:T(8,128)(2,1)}, u32[]{:S(2)}) copy-start(bf16[1,544,768]{1,2,0:T(8,128)(2,1)} %copy.84) | copy-start | bytes 2506756
  613.2 6.0 copy-start.22
  626.9 10.3 %copy-start.32 = (f32[1,136,1536]{2,1,0:T(8,128)S(1)}, f32[1,136,1536]{2,1,0:T(8,128)}, u32[]{:S(2)}) copy-start(f32[1,136,1536]{2,1,0:T(8,128)} %get-tuple-element.104) | copy-start | bytes 2506756
  626.9 10.3 %copy-start.33 = (f32[1,136,1536]{2,1,0:T(8,128)S(1)}, f32[1,136,1536]{2,1,0:T(8,128)}, u32[]{:S(2)}) copy-start(f32[1,136,1536]{2,1,0:T(8,128)} %fusion.53) | copy-start | bytes 2506756
  626.9 10.3 %copy-start.69 = (f32[272]{0:T(512)S(1)}, f32[272]{0:T(512)}, u32[]{:S(2)}) copy-start(f32[272]{0:T(512)} %copy-done.68) | copy-start | bytes 3268
  637.1 26.4 %collective-permute-start.15 = (bf16[544,1536]{1,0:T(8,128)(2,1)}, bf16[544,1536]{1,0:T(8,128)(2,1)}, u32[]{:S(2)}, u32[]{:S(2)}) collective-permute-start(bf16[544,1536]{1,0:T(8,128)(2,1)} %get-tuple-element.148), channel_id=1, source_target_pairs={{0,4},{4,0},{8,12},{12,8},{16,20},{20,16},{24,28},{28,24},{1,5},{5... | collective-permute-start | bytes 5013512 | tf_op jit(solution)/shard_map/ppermute | solution.py:342
  647.2 10.5 %copy-start.81 = (bf16[12,64,544]{2,1,0:T(8,128)(2,1)S(1)}, bf16[12,64,544]{2,1,0:T(8,128)(2,1)}, u32[]{:S(2)}) copy-start(bf16[12,64,544]{2,1,0:T(8,128)(2,1)} %copy-done.80) | copy-start | bytes 2506756
  657.6 5.8 copy-start.9
  657.6 5.8 copy-start.19
  657.6 5.8 copy-start.53
  657.7 5.8 copy-start.57
  657.7 5.8 copy-start.59
  675.0 210.1 %all-to-all-start = ((bf16[3,4,192,384]{3,2,0,1:T(8,128)(2,1)}), bf16[3,4,192,384]{3,2,0,1:T(8,128)(2,1)S(1)}, u32[]{:S(2)}, u32[]{:S(2)}) async-start(bf16[3,4,192,384]{3,2,0,1:T(8,128)(2,1)} %copy.105), calls=%async_computation.1 | async-start | bytes 3538944 | tf_op jit(solution)/shard_map/all_to_all | solution.py:1429
  875.4 5.2 copy-start.47
  (45 other events, 128.9 us)
Sparse Core Ops, SparseCore 0:
  287.1 50.6 all-gather.2
  515.9 122.4 reduce-scatter.1

commit v3 on v2

--- a/solution.py
+++ b/solution.py
@@ -356,36 +356,6 @@
     return mine.astype(F32) + theirs.astype(F32)
 
 
-def z_routes(turn):
-    pairs = []
-    for plane in range(4):
-        for core in range(2):
-            for z in range(4):
-                picked = (z + turn) % 2
-                source = (plane * 2 + core) * 4 + z
-                target = (plane * 2 + z // 2) * 4 + 2 * core + picked
-                pairs.append((source, target))
-    return pairs
-
-
-def rows_in(value, z):
-    first = lax.ppermute(take(value, z % 2, 0), ("dp", "tensor"), z_routes(0))
-    second = lax.ppermute(take(value, 1 - z % 2, 0), ("dp", "tensor"), z_routes(1))
-    return ordered(z % 2, first, second, 0).reshape(-1, value.shape[-1])
-
-
-def plane_rows(half):
-    cut = half.shape[0] // 2
-    upper, lower = half[:cut], half[cut:]
-    upper_x = swap(upper, XBIT)
-    lower_y = swap(lower, YBIT)
-    upper_two = swap(jnp.stack([upper, upper_x]), YBIT)
-    lower_two = swap(jnp.stack([lower, lower_y]), XBIT)
-    return jnp.concatenate(
-        [upper, lower, upper_x, lower_two[0], upper_two[0], lower_y, upper_two[1], lower_two[1]]
-    )
-
-
 def plane_sums(partial_value):
     blocks = partial_value.astype(BF).reshape(4, 2, -1, partial_value.shape[-1])
     upper, lower = blocks[:, 0], blocks[:, 1]
@@ -444,146 +414,207 @@
     )
 
 
-def first_kernel(
+def any_specs(count):
+    return [pl.BlockSpec(memory_space=pl.ANY)] * count
+
+
+def near_specs(count):
+    return [pl.BlockSpec(memory_space=pltpu.VMEM)] * count
+
+
+ROOM = 56 << 20
+
+
+def dma(*shape):
+    return pltpu.SemaphoreType.DMA(shape)
+
+
+def forward_pair(queries, keys_in, values, valid):
+    lane = lax.broadcasted_iota(jnp.int32, (1, 2 * HD), 1)
+    total = None
+    for side in range(2):
+        only = jnp.where(lane // HD == side, 1.0, 0.0)
+        picked = (queries.astype(F32) * (only * HD ** (-0.5))).astype(BF)
+        turned = (values.astype(F32) * only).T.astype(BF)
+        scores = lax.dot_general(
+            keys_in, picked, (((1,), (1,)), ((), ())), preferred_element_type=F32
+        )
+        scores = jnp.where(valid, scores, NEGATIVE)
+        exponent = jnp.exp(scores - jnp.max(scores, axis=0, keepdims=True))
+        share = 1.0 / jnp.sum(exponent, axis=0, keepdims=True)
+        mixed = jnp.dot(turned, exponent.astype(BF), preferred_element_type=F32) * share
+        total = mixed if total is None else total + mixed
+    return total.T.astype(BF)
+
+
+class RowsIn:
+    def __init__(self, source, target, sems):
+        self.source, self.target = source, target
+        self.send, self.recv, self.send_on, self.recv_on, self.keep = sems
+        self.dp, self.plane, self.core, self.z = spot()
+        self.sibling = (flip(self.dp, 1), self.z)
+        self.home = self.z // 2 == self.core
+
+    def stays(self, s):
+        return jnp.logical_and(self.home, self.z % 2 == s)
+
+    def depart(self):
+        for s in range(2):
+
+            @pl.when(jnp.logical_not(self.stays(s)))
+            def _(s=s):
+                goal = (self.plane * 2 + self.z // 2, 2 * self.core + s)
+                push(
+                    self.source.at[s],
+                    self.target.at[self.z],
+                    self.send.at[s],
+                    self.recv.at[self.z % 2],
+                    goal,
+                ).start()
+
+            @pl.when(self.stays(s))
+            def _(s=s):
+                pltpu.make_async_copy(
+                    self.source.at[s], self.target.at[self.z], self.keep.at[0]
+                ).start()
+
+    def onward(self, j, core):
+        place = self.target.at[2 * core + j]
+        return push(place, place, self.send_on.at[j], self.recv_on.at[j], self.sibling)
+
+    def forward(self):
+        for j in range(2):
+            place = self.target.at[2 * self.core + j]
+            mine = jnp.logical_and(self.home, 2 * self.core + j == self.z)
+
+            @pl.when(mine)
+            def _():
+                pltpu.make_async_copy(self.source.at[0], place, self.keep.at[0]).wait()
+
+            @pl.when(jnp.logical_not(mine))
+            def _(j=j):
+                push(
+                    self.source.at[0], place, self.send.at[0], self.recv.at[j], self.sibling
+                ).wait_recv()
+
+            self.onward(j, self.core).start()
+
+    def settle(self):
+        for j in range(2):
+            self.onward(j, 1 - self.core).wait_recv()
+
+    def finish(self):
+        for j in range(2):
+            self.onward(j, self.core).wait_send()
+
+            @pl.when(jnp.logical_not(self.stays(j)))
+            def _(j=j):
+                push(
+                    self.source.at[j],
+                    self.target.at[self.z],
+                    self.send.at[j],
+                    self.recv.at[0],
+                    self.sibling,
+                ).wait_send()
+
+
+class PlaneRows:
+    def __init__(self, target, send, recv):
+        self.target, self.send, self.recv = target, send, recv
+        dp, _, _, z = spot()
+        self.xmate, self.ymate, _ = plane_mates(dp, z)
+
+    def copy(self, near, part, chip, slot, mate):
+        return push(
+            self.target.at[near, part],
+            self.target.at[chip, part],
+            self.send.at[slot],
+            self.recv.at[slot],
+            mate,
+        )
+
+    def hop(self, slot):
+        near, part, chip, mate = [
+            (0, 0, 1, self.xmate),
+            (0, 1, 2, self.ymate),
+            (0, 0, 2, self.ymate),
+            (0, 1, 1, self.xmate),
+            (1, 0, 3, self.ymate),
+            (2, 1, 3, self.xmate),
+        ][slot]
+        return self.copy(near, part, chip, slot, mate)
+
+    def start(self):
+        for slot in range(4):
+            self.hop(slot).start()
+
+    def relay(self):
+        for slot in range(2):
+            self.hop(slot).wait_recv()
+            self.hop(4 + slot).start()
+
+    def finish(self):
+        for slot in range(2, 6):
+            self.hop(slot).wait_recv()
+        for slot in range(6):
+            self.hop(slot).wait_send()
+
+
+def weights_kernel(
+    shard_ref,
+    units_ref,
     rows_ref,
-    wide_ref,
+    cot_ref,
+    size_ref,
     cond_ref,
-    size_ref,
-    seq_ref,
-    block_ref,
-    cond_both,
-    size_both,
-    send_a,
-    recv_a,
-    send_b,
-    recv_b,
-    send_c,
-    recv_c,
-    send_d,
-    recv_d,
-    local,
+    gain_ref,
+    *refs,
+    groups,
+    wides,
+    tokens,
 ):
+    count = len(groups)
+    arrays = max(which for which, _ in groups) + 1
+    whole_refs, refs = refs[:arrays], refs[arrays:]
+    wide_refs, refs = refs[:2], refs[1:]
+    one_ref, qkv_ref, mixed_ref, stream_ref, two_ref, query_ref, pair_ref, crossed_ref = refs[1:9]
+    after_ref, all_ref, seq_ref, grad_ref, grads_ref, keep_ref, conds_ref = refs[9:16]
+    held, part_out, part_in, three, block_ref, sizes = refs[16:22]
+    send_e, recv_e, send_n, recv_n, held_sem = refs[22:27]
+    send_s, recv_s, send_z, recv_z, send_p, recv_p, local = refs[27:34]
+    send_w, recv_w, send_v, recv_v, local_w = refs[34:39]
+    stream_rows = RowsIn(rows_ref, seq_ref, refs[39:44])
+    grad_rows = RowsIn(cot_ref, grad_ref, refs[44:49])
+    send_b, recv_b, send_d, recv_d, send_q, recv_q, keep_sem = refs[49:]
     dp, plane, core, z = spot()
+    width = shard_ref.shape[2]
     sibling = (flip(dp, 1), z)
+    xmate, ymate, far = plane_mates(dp, z)
     greet(plane_mates(dp, z) + column_mates(dp, z))
     home = z // 2 == core
-    for s in range(2):
-        stays = jnp.logical_and(home, z % 2 == s)
-
-        @pl.when(jnp.logical_not(stays))
-        def _(s=s):
-            target = (plane * 2 + z // 2, 2 * core + s)
-            push(rows_ref.at[s], seq_ref.at[z], send_a.at[s], recv_a.at[z % 2], target).start()
-
-        @pl.when(stays)
-        def _(s=s):
-            pltpu.make_async_copy(rows_ref.at[s], seq_ref.at[z], local.at[0]).start()
-
-    wide = []
-    for slot, mate in enumerate(plane_mates(dp, z)):
-        copy = push(
-            wide_ref.at[:, mate[0] // 2],
+    above, below = (dp, z + 1), (dp, z - 1)
+    stream_rows.depart()
+    units = [
+        push(
+            units_ref.at[:, mate[0] // 2],
             block_ref.at[:, plane],
             send_b.at[slot],
             recv_b.at[slot],
             mate,
         )
-        copy.start()
-        wide.append(copy)
-    own = pltpu.make_async_copy(wide_ref.at[:, plane], block_ref.at[:, plane], local.at[1])
-    own.start()
-    small = []
-    for slot, (source, target) in enumerate([(cond_ref, cond_both), (size_ref, size_both)]):
-        copy = push(source, target.at[core], send_d.at[slot], recv_d.at[slot], sibling)
-        copy.start()
-        keep = pltpu.make_async_copy(source, target.at[core], local.at[2 + slot])
-        keep.start()
-        small.append((copy, keep, slot, target))
-    for j in range(2):
-        block = 2 * core + j
-        stays = jnp.logical_and(home, block == z)
-
-        @pl.when(stays)
-        def _(block=block):
-            pltpu.make_async_copy(rows_ref.at[0], seq_ref.at[block], local.at[0]).wait()
-
-        @pl.when(jnp.logical_not(stays))
-        def _(block=block, j=j):
-            push(rows_ref.at[0], seq_ref.at[block], send_a.at[0], recv_a.at[j], sibling).wait_recv()
-
-        push(seq_ref.at[block], seq_ref.at[block], send_c.at[j], recv_c.at[j], sibling).start()
-    for j in range(2):
-        mine, other = 2 * core + j, 2 * (1 - core) + j
-        push(seq_ref.at[mine], seq_ref.at[mine], send_c.at[j], recv_c.at[j], sibling).wait_send()
-        push(seq_ref.at[other], seq_ref.at[other], send_c.at[j], recv_c.at[j], sibling).wait_recv()
-    for s in range(2):
-        stays = jnp.logical_and(home, z % 2 == s)
-
-        @pl.when(jnp.logical_not(stays))
-        def _(s=s):
-            push(rows_ref.at[s], seq_ref.at[z], send_a.at[s], recv_a.at[0], sibling).wait_send()
-
-    for copy in wide:
-        copy.wait()
-    own.wait()
-    for copy, keep, slot, target in small:
-        keep.wait()
-        copy.wait_send()
-        theirs = target.at[1 - core]
-        push(theirs, theirs, send_d.at[slot], recv_d.at[slot], sibling).wait_recv()
-
-
-def any_specs(count):
-    return [pl.BlockSpec(memory_space=pl.ANY)] * count
-
-
-def near_specs(count):
-    return [pl.BlockSpec(memory_space=pltpu.VMEM)] * count
-
-
-ROOM = 56 << 20
-
-
-def dma(*shape):
-    return pltpu.SemaphoreType.DMA(shape)
-
-
-def first_moves(rows, wide, cond, size):
-    _, height, width = rows.shape
-    return pl.pallas_call(
-        first_kernel,
-        out_shape=[
-            jax.ShapeDtypeStruct((4, height, width), BF),
-            jax.ShapeDtypeStruct(wide.shape, BF),
-            jax.ShapeDtypeStruct((2, *cond.shape), BF),
-            jax.ShapeDtypeStruct((2, *size.shape), size.dtype),
-        ],
-        in_specs=near_specs(4),
-        out_specs=any_specs(4),
-        scratch_shapes=[dma(2), dma(2), dma(3), dma(3), dma(2), dma(2), dma(2), dma(2), dma(4)],
-        compiler_params=pltpu.CompilerParams(
-            collective_id=1, has_side_effects=True, vmem_limit_bytes=ROOM
-        ),
-        name="first_moves",
-    )(rows, wide, cond, size)
-
-
-def weights_kernel(
-    shard_ref, block_ref, *refs, groups, wides
-):
-    count = len(groups)
-    arrays = max(which for which, _ in groups) + 1
-    whole_refs, wide_ref = refs[:arrays], refs[arrays]
-    send_s, recv_s, send_z, recv_z, send_p, recv_p, local = refs[arrays + 1 : arrays + 8]
-    send_w, recv_w, send_v, recv_v, local_w = refs[arrays + 8 :]
-    dp, plane, core, z = spot()
-    width = shard_ref.shape[2]
-    sibling = (flip(dp, 1), z)
-    xmate, ymate, far = plane_mates(dp, z)
-    lines = [(dp, lax.rem(z + step, 4)) for step in range(1, 4)]
-    greet([sibling, xmate, ymate] + lines)
-    home = z // 2 == core
-    above, below = (dp, z + 1), (dp, z - 1)
+        for slot, mate in enumerate([xmate, ymate, far])
+    ]
+    units_own = pltpu.make_async_copy(
+        units_ref.at[:, plane], block_ref.at[:, plane], keep_sem.at[0]
+    )
+    small = [
+        push(size_ref, sizes.at[core], send_d.at[0], recv_d.at[0], sibling),
+        push(cond_ref, conds_ref.at[core], send_d.at[1], recv_d.at[1], sibling),
+    ]
+    small_own = [
+        pltpu.make_async_copy(size_ref, sizes.at[core], keep_sem.at[1]),
+        pltpu.make_async_copy(cond_ref, conds_ref.at[core], keep_sem.at[2]),
+    ]
 
     def columns(which):
         return pl.ds(pl.multiple_of(which * width, width), width)
@@ -602,6 +633,9 @@
         @pl.when(jnp.logical_not(home))
         def _(g=g, target=target):
             push(shard_ref.at[g], target, send_s.at[g], recv_s.at[g], sibling).start()
+
+    for copy in small + small_own + units + [units_own]:
+        copy.start()
 
     near = jnp.where(core == 0, jnp.where(z >= 1, 1, 0), jnp.where(z <= 2, 0, 1))
 
@@ -662,7 +696,8 @@
     wide_width = block_ref.shape[3]
 
     def quarter(k, block, side):
-        return wide_ref.at[k, :, side, :, pl.ds(pl.multiple_of(block * wide_width, wide_width), wide_width)]
+        spots = pl.ds(pl.multiple_of(block * wide_width, wide_width), wide_width)
+        return wide_refs[k // 2].at[k % 2, :, side, :, spots]
 
     def wide_copy(k, block, way, target):
         place = quarter(k, block, core)
@@ -700,25 +735,233 @@
             def _(block=block, way=way, target=target):
                 wide_copy(k, block, way, target).start()
 
-    script = (
-        "S0 S1 R0 S2 R1 S3 R2 S4 R3 S5 S6 W0 R4 W1 R5 V01 R6 V11 V02 V12 V03 V13"
-    )
-    for word in script.split():
-        kind = word[0]
-        if kind == "S":
-            spread(int(word[1]), 0)
-            spread(int(word[1]), 1)
-        elif kind == "R":
-            relay(int(word[1]), 0)
-            relay(int(word[1]), 1)
-        elif kind == "W" and int(word[1]) < wides:
-            wide_own(int(word[1]))
-        elif kind == "V" and int(word[1]) < wides:
-            wide_step(int(word[1]), int(word[2]))
-    for g in range(count):
+
+    def both(step, g):
+        step(g, 0)
+        step(g, 1)
+
+    def settle(g):
         for turn in range(2):
             hop(g, turn, mates[1 - turn][0] // 2, 1 - turn, mates[1 - turn]).wait_recv()
             hop(g, turn, far[0] // 2, 2, mates[1 - turn]).wait_recv()
+        copy = pltpu.make_async_copy(slab(g), held.at[g % 2], held_sem.at[g % 2])
+        copy.start()
+        copy.wait()
+
+    height = seq_ref.shape[0] * seq_ref.shape[1]
+    model_width = seq_ref.shape[2]
+    half = height // 2
+    tile = 256
+
+    def norm(value, which):
+        centred = value - jnp.mean(value, axis=1, keepdims=True)
+        inverse = lax.rsqrt(jnp.mean(centred * centred, axis=1, keepdims=True) + EPSILON)
+        return (centred * inverse * gain_ref[which : which + 1]).astype(BF)
+
+    def project(g, source, put):
+        def body(step, carry):
+            rows = source.shape[0] // 2
+            lines = pl.ds(pl.multiple_of(step // 3 * rows, 16), rows)
+            spots = pl.ds(pl.multiple_of(step % 3 * tile, tile), tile)
+            weight = held[g % 2, :, :, :, spots].reshape(model_width, tile)
+            put(lines, spots, jnp.dot(source[lines, :], weight, preferred_element_type=F32).astype(BF))
+            return carry
+
+        lax.fori_loop(0, 6, body, 0)
+
+    def give(g, source, turn):
+        def body(step, carry):
+            lines = pl.ds(pl.multiple_of(step // 4 * half, 16), half)
+            chip = step % 4
+            span = model_width // 4
+            weight = held[g % 2, chip].reshape(span, -1)
+            value = lax.dot_general(
+                source[lines, :], weight, (((1,), (1,)), ((), ())), preferred_element_type=F32
+            )
+            spots = pl.ds(pl.multiple_of(chip * span, 128), span)
+            part_out[turn, lines, spots] = value.astype(BF)
+            return carry
+
+        lax.fori_loop(0, 8, body, 0)
+        exchange(turn).start()
+
+    def exchange(turn):
+        return push(part_out.at[turn], part_in.at[turn], send_e.at[turn], recv_e.at[turn], sibling)
+
+    slices = height // 32
+
+    def first_norm():
+        for part in range(seq_ref.shape[0]):
+            lines = slice(part * seq_ref.shape[1], (part + 1) * seq_ref.shape[1])
+            stream_ref[lines, :] = seq_ref[part].astype(F32)
+
+        def body(i, carry):
+            lines = pl.ds(pl.multiple_of(i * 32, 32), 32)
+            one_ref[lines, :] = norm(stream_ref[lines, :], 0)
+            return carry
+
+        lax.fori_loop(0, slices, body, 0)
+
+    def summed(lines, turn):
+        both_parts = part_out[turn, lines, :].astype(F32) + part_in[turn, lines, :].astype(F32)
+        return stream_ref[lines, :] + keep_ref[lines, :1] * both_parts
+
+    def second_norm():
+        exchange(0).wait_recv()
+
+        def body(i, carry):
+            lines = pl.ds(pl.multiple_of(i * 32, 32), 32)
+            value = summed(lines, 0)
+            stream_ref[lines, :] = value
+            two_ref[lines, :] = norm(value, 1)
+            return carry
+
+        lax.fori_loop(0, slices, body, 0)
+
+    def third_norm():
+        count_rows = half // 2
+        for j in range(2):
+
+            def body(i, carry, j=j):
+                start = pl.multiple_of(i * 8, 8)
+                lines = pl.ds(pl.multiple_of(core * half + j * count_rows + i * 8, 8), 8)
+                added = three[pl.ds(pl.multiple_of(j * count_rows + i * 8, 8), 8), :]
+                value = stream_ref[lines, :] + keep_ref[lines, :1] * added
+                after_ref[j, pl.ds(start, 8), :] = value
+                return carry
+
+            lax.fori_loop(0, count_rows // 8, body, 0)
+            all_ref[0, j] = norm(after_ref[j], 2)
+
+    def unpack():
+        def body(i, carry):
+            lines = pl.ds(pl.multiple_of(core * half + i * 16, 16), 16)
+            value = part_out[1, lines, :].astype(F32) + part_in[1, lines, :].astype(F32)
+            three[pl.ds(pl.multiple_of(i * 16, 16), 16), :] = value
+            return carry
+
+        lax.fori_loop(0, half // 16, body, 0)
+
+    def own_heads(pair, carry):
+        lanes = pl.ds(pl.multiple_of(pair * 128, 128), 128)
+        mixed_ref[:, lanes] = forward_pair(
+            qkv_ref[0, :, lanes], qkv_ref[1, :, lanes], qkv_ref[2, :, lanes], keep_ref[:, :1] > 0.0
+        )
+        return carry
+
+    def cross_heads(pair, carry):
+        lanes = pl.ds(pl.multiple_of(pair * 128, 128), 128)
+        line = lax.broadcasted_iota(jnp.int32, (pair_ref.shape[1], 1), 0)
+        crossed_ref[:, lanes] = forward_pair(
+            query_ref[:, lanes], pair_ref[0, :, lanes], pair_ref[1, :, lanes], line < tokens
+        )
+        return carry
+
+    pairs = qkv_ref.shape[2] // 128
+
+    def put_in(target):
+        def put(lines, spots, value):
+            target[lines, spots] = value
+
+        return put
+
+    def put_cond(which):
+        def body(step, carry):
+            spots = pl.ds(pl.multiple_of(step * tile, tile), tile)
+            weight = held[5 % 2, :, :, :, spots].reshape(model_width, tile)
+            value = jnp.dot(conds_ref[z // 2, which], weight, preferred_element_type=F32)
+            pair_ref[which, :, spots] = value.astype(BF)
+            return carry
+
+        lax.fori_loop(0, 3, body, 0)
+
+    def set_keep():
+        for copy in small_own:
+            copy.wait()
+        for copy in small:
+            copy.wait()
+        line = lax.broadcasted_iota(jnp.int32, keep_ref.shape, 0)
+        keep_ref[...] = jnp.where(line < sizes[z // 2, :1, :], 1.0, 0.0)
+
+    def set_grads():
+        for j in range(2):
+            lines = pl.ds(pl.multiple_of((2 * core + j) * grad_ref.shape[1], 8), grad_ref.shape[1])
+            value = grad_ref[2 * core + j].astype(F32) * keep_ref[lines, :1]
+            grads_ref[0, j] = value.astype(BF)
+
+    plane_norms = PlaneRows(all_ref, send_n, recv_n)
+    plane_grads = PlaneRows(grads_ref, send_q, recv_q)
+
+    both(spread, 0)
+    stream_rows.forward()
+    set_keep()
+    stream_rows.settle()
+    first_norm()
+    both(spread, 1)
+    both(spread, 2)
+    both(relay, 0)
+    both(spread, 3)
+    both(relay, 1)
+    both(spread, 4)
+    settle(0)
+    project(0, one_ref, put_in(qkv_ref.at[0]))
+    both(relay, 2)
+    both(spread, 5)
+    both(spread, 6)
+    grad_rows.depart()
+    for copy in units:
+        copy.wait()
+    units_own.wait()
+    wide_own(0)
+    settle(1)
+    project(1, one_ref, put_in(qkv_ref.at[1]))
+    both(relay, 3)
+    wide_own(1)
+    settle(2)
+    project(2, one_ref, put_in(qkv_ref.at[2]))
+    both(relay, 4)
+    wide_own(2)
+    lax.fori_loop(0, pairs, own_heads, 0)
+    wide_step(0, 1)
+    grad_rows.forward()
+    set_grads()
+    plane_grads.start()
+    both(relay, 5)
+    settle(3)
+    give(3, mixed_ref, 0)
+    wide_step(1, 1)
+    both(relay, 6)
+    second_norm()
+    wide_step(2, 1)
+    plane_grads.relay()
+    settle(4)
+    project(4, two_ref, put_in(query_ref))
+    wide_step(0, 2)
+    settle(5)
+    put_cond(0)
+    put_cond(1)
+    lax.fori_loop(0, pairs, cross_heads, 0)
+    wide_step(1, 2)
+    settle(6)
+    give(6, crossed_ref, 1)
+    wide_step(2, 2)
+    exchange(1).wait_recv()
+    unpack()
+    third_norm()
+    plane_norms.start()
+    wide_step(0, 3)
+    plane_norms.relay()
+    wide_step(1, 3)
+    wide_step(2, 3)
+    grad_rows.settle()
+    plane_grads.finish()
+    plane_norms.finish()
+    grad_rows.finish()
+    stream_rows.finish()
+    for turn in range(2):
+        exchange(turn).wait_send()
+    for g in range(count):
+        for turn in range(2):
             for slot in range(3):
                 hop(g, turn, plane, slot, xmate).wait_send()
             on_z(g, turn, lambda copy: copy.wait_send())
@@ -741,19 +984,52 @@
                 wide_copy(k, block, 1, below).wait_send()
 
 
-def weights_moves(shard, block, groups, wides):
+def weights_moves(shard, units, rows, cot, size, cond, gains, groups, tokens):
     count, depth, width = shard.shape
     sizes = [0] * (max(which for which, _ in groups) + 1)
     for which, _ in groups:
         sizes[which] += 1
-    _, chips, _, unit = block.shape
+    wides, chips, _, unit = units.shape
+    _, block, model_width = rows.shape
+    height, columns = 4 * block, 2 * width
+    like = jax.ShapeDtypeStruct
+    row_sems = [dma(2), dma(2), dma(2), dma(2), dma(1)]
     out = pl.pallas_call(
-        functools.partial(weights_kernel, groups=groups, wides=wides),
-        out_shape=[jax.ShapeDtypeStruct((size, 4, 2, depth, 2 * width), BF) for size in sizes]
-        + [jax.ShapeDtypeStruct((wides, chips, 2, depth, 4 * unit), BF)],
-        in_specs=near_specs(2),
-        out_specs=any_specs(len(sizes) + 1),
+        functools.partial(weights_kernel, groups=groups, wides=wides, tokens=tokens),
+        out_shape=[like((slabs, 4, 2, depth, columns), BF) for slabs in sizes]
+        + [
+            like((2, chips, 2, depth, 4 * unit), BF),
+            like((wides - 2, chips, 2, depth, 4 * unit), BF),
+            like((height, model_width), BF),
+            like((3, height, columns), BF),
+            like((height, columns), BF),
+            like((height, model_width), F32),
+            like((height, model_width), BF),
+            like((height, columns), BF),
+            like((2, cond.shape[1], columns), BF),
+            like((height, columns), BF),
+            like((2, block, model_width), F32),
+            like((4, 2, block, model_width), BF),
+            like((4, block, model_width), BF),
+            like((4, block, model_width), BF),
+            like((4, 2, block, model_width), BF),
+            like((height, 128), F32),
+            like((2, *cond.shape), BF),
+        ],
+        in_specs=near_specs(7),
+        out_specs=any_specs(len(sizes) + 2) + near_specs(15),
         scratch_shapes=[
+            pltpu.VMEM((2, 4, 2, depth, columns), BF),
+            pltpu.VMEM((2, height, model_width), BF),
+            pltpu.VMEM((2, height, model_width), BF),
+            pltpu.VMEM((2 * block, model_width), F32),
+            pltpu.VMEM(units.shape, BF),
+            pltpu.VMEM((2, *size.shape), size.dtype),
+            dma(2),
+            dma(2),
+            dma(6),
+            dma(6),
+            dma(2),
             dma(count),
             dma(count),
             dma(count, 2, 2),
@@ -766,95 +1042,25 @@
             dma(wides, 4),
             dma(wides, 4),
             dma(wides),
+            *row_sems,
+            *row_sems,
+            dma(3),
+            dma(3),
+            dma(2),
+            dma(2),
+            dma(6),
+            dma(6),
+            dma(3),
         ],
         compiler_params=pltpu.CompilerParams(
-            collective_id=2, has_side_effects=True, vmem_limit_bytes=ROOM
+            collective_id=2, has_side_effects=True, vmem_limit_bytes=60 << 20
         ),
         name="weights_moves",
-    )(shard, block)
-    return [whole.reshape(whole.shape[0], 8 * depth, whole.shape[-1]) for whole in out]
-
-
-def second_kernel(
-    rows_ref, quarter_ref, all_ref, wide_ref, send_r, recv_r, send_w, recv_w, local, held, held_sem
-):
-    dp, plane, core, z = spot()
-    sibling = (flip(dp, 1), z)
-    xmate, ymate, far = plane_mates(dp, z)
-    greet([sibling, xmate, ymate])
-    width = quarter_ref.shape[4]
-
-    def rows(source, chip, part, slot, mate):
-        return push(source, all_ref.at[chip, part], send_r.at[slot], recv_r.at[slot], mate)
-
-    own = [
-        rows(rows_ref.at[0], 1, 0, 0, xmate),
-        rows(rows_ref.at[1], 2, 1, 1, ymate),
-        rows(rows_ref.at[0], 2, 0, 2, ymate),
-        rows(rows_ref.at[1], 1, 1, 3, xmate),
-    ]
-    for copy in own:
-        copy.start()
-    wide, loads = [], []
-    for block in range(4):
-        columns = pl.ds(block * width, width)
-        target = wide_ref.at[:, :, core, :, columns]
-        loads.append(pltpu.make_async_copy(quarter_ref.at[block], held.at[block], held_sem.at[block]))
-        wide.append(pltpu.make_async_copy(held.at[block], target, local.at[block]))
-        wide.append(push(held.at[block], target, send_w.at[block], recv_w.at[block], sibling))
-    for copy in loads:
-        copy.start()
-    keep = pltpu.make_async_copy(rows_ref, all_ref.at[0], local.at[4])
-    keep.start()
-    for block in range(4):
-        loads[block].wait()
-        wide[2 * block].start()
-        wide[2 * block + 1].start()
-    own[0].wait_recv()
-    upper = rows(all_ref.at[1, 0], 3, 0, 4, ymate)
-    upper.start()
-    own[1].wait_recv()
-    lower = rows(all_ref.at[2, 1], 3, 1, 5, xmate)
-    lower.start()
-    own[2].wait_recv()
-    own[3].wait_recv()
-    for copy in own:
-        copy.wait_send()
-    upper.wait()
-    lower.wait()
-    keep.wait()
-    for block in range(4):
-        columns = pl.ds(block * width, width)
-        wide[2 * block].wait()
-        wide[2 * block + 1].wait_send()
-        theirs = wide_ref.at[:, :, 1 - core, :, columns]
-        push(theirs, theirs, send_w.at[block], recv_w.at[block], sibling).wait_recv()
-
-
-def second_moves(rows, quarter):
-    blocks, count, chips, depth, width = quarter.shape
-    return pl.pallas_call(
-        second_kernel,
-        out_shape=[
-            jax.ShapeDtypeStruct((4, *rows.shape), BF),
-            jax.ShapeDtypeStruct((count, chips, 2, depth, blocks * width), BF),
-        ],
-        in_specs=near_specs(1) + any_specs(1),
-        out_specs=any_specs(2),
-        scratch_shapes=[
-            dma(6),
-            dma(6),
-            dma(4),
-            dma(4),
-            dma(5),
-            pltpu.VMEM(quarter.shape, BF),
-            dma(4),
-        ],
-        compiler_params=pltpu.CompilerParams(
-            collective_id=3, has_side_effects=True, vmem_limit_bytes=ROOM
-        ),
-        name="second_moves",
-    )(rows, quarter)
+    )(shard, units, rows, cot, size, cond, gains)
+    weights = out[: len(sizes) + 2]
+    return [
+        whole.reshape(whole.shape[0], 8 * depth, whole.shape[-1]) for whole in weights
+    ], out[len(sizes) + 2 :]
 
 
 def third_kernel(
@@ -973,14 +1179,51 @@
     )(part, *[grad.reshape(grad.shape[0], 4, 2, depth, units) for grad in grads])
 
 
-def share_kernel(
-    *refs, groups, arrays
-):
-    count = len(groups)
+def backward_pair(queries, keys_in, values, grads, valid):
+    lane = lax.broadcasted_iota(jnp.int32, (1, 2 * HD), 1)
+    totals = [None, None, None]
+    for side in range(2):
+        only = jnp.where(lane // HD == side, 1.0, 0.0)
+        picked = (queries.astype(F32) * (only * HD ** (-0.5))).astype(BF)
+        given = (grads.astype(F32) * only).astype(BF)
+        turned = (keys_in.astype(F32) * only).T.astype(BF)
+        rows_rows = (((1,), (1,)), ((), ()))
+        scores = lax.dot_general(keys_in, picked, rows_rows, preferred_element_type=F32)
+        scores = jnp.where(valid, scores, NEGATIVE)
+        exponent = jnp.exp(scores - jnp.max(scores, axis=0, keepdims=True))
+        probs = exponent * (1.0 / jnp.sum(exponent, axis=0, keepdims=True))
+        grad_probs = lax.dot_general(values, given, rows_rows, preferred_element_type=F32)
+        inner = jnp.sum(probs * grad_probs, axis=0, keepdims=True)
+        grad_scores = (probs * (grad_probs - inner)).astype(BF)
+        new = (
+            jnp.dot(turned, grad_scores, preferred_element_type=F32).T * HD ** (-0.5),
+            jnp.dot(grad_scores, picked, preferred_element_type=F32),
+            jnp.dot(probs.astype(BF), given, preferred_element_type=F32),
+        )
+        totals = [b if a is None else a + b for a, b in zip(totals, new, strict=True)]
+    return [total.astype(BF) for total in totals]
+
+
+def share_kernel(*refs, arrays):
+    count = arrays + 3
     grad_refs, refs = refs[:arrays], refs[arrays:]
-    rows_ref, gain_ref, cond_ref = refs[:3]
-    out_ref, back_ref, gain_out, cond_out = refs[3:7]
-    one, got, two, line, gain_got, gain_sum, gain_line = refs[7:14]
+    (
+        qkv_ref,
+        mixed_ref,
+        valid_ref,
+        turned_ref,
+        whole_ref,
+        stream_ref,
+        scaled_ref,
+        inverse_ref,
+        factor_ref,
+        first_ref,
+        gain_in,
+        cond_ref,
+    ) = refs[:12]
+    out_ref, back_ref, gain_out, cond_out = refs[12:16]
+    one, got, two, line, gain_got, gain_ref, gain_sum, gain_line = refs[16:24]
+    made, whole, thirds, part_out, part_in, part_own, rows_ref = refs[24:31]
     (
         load,
         send_x,
@@ -1000,7 +1243,8 @@
         send_k,
         recv_k,
         local,
-    ) = refs[14:]
+        extra,
+    ) = refs[31:]
     dp, plane, core, z = spot()
     xbit, ybit = plane % 2, plane // 2
     sibling = (flip(dp, 1), z)
@@ -1020,13 +1264,19 @@
         return pl.ds(pl.multiple_of(which * width, width), width)
 
     def strip(g, turn, bit):
-        array, index = groups[g]
-        grid = grad_refs[array].at[index]
+        grid = grad_refs[g].at[0] if g < arrays else made.at[g - arrays]
         if turn == 0:
             return grid.at[:, bit, :, :, columns(order(turn))]
         return grid.at[bit, :, :, :, columns(order(turn))]
 
     bits = (xbit, ybit)
+
+    def add_to(target, source):
+        def body(part, carry):
+            target[part] = target[part] + source[part]
+            return carry
+
+        lax.fori_loop(0, 2, body, 0)
 
     def step_one(g, turn):
         return push(
@@ -1036,9 +1286,17 @@
     def fetch(g, turn):
         return pltpu.make_async_copy(strip(g, turn, bits[turn]), one.at[g, turn], load.at[g, turn])
 
+    def kept(g, turn, side):
+        if g < arrays:
+            return one.at[g, turn, side]
+        grid = made.at[g - arrays]
+        if turn == 0:
+            return grid.at[side, xbit, :, :, columns(order(turn))]
+        return grid.at[ybit, side, :, :, columns(order(turn))]
+
     def step_two(g, turn):
         return push(
-            one.at[g, turn, 1 - bits[1 - turn]],
+            kept(g, turn, 1 - bits[1 - turn]),
             two.at[g, turn],
             send_y.at[g, turn],
             recv_y.at[g, turn],
@@ -1046,31 +1304,21 @@
         )
 
     def after_one(g, turn):
-        fetch(g, turn).wait()
+        if g < arrays:
+            fetch(g, turn).wait()
         step_one(g, turn).wait_recv()
-
-        def body(i, carry):
-            side, part = i // 2, i % 2
-            one[g, turn, side, part] = one[g, turn, side, part] + got[g, turn, side, part]
-            return carry
-
-        lax.fori_loop(0, 4, body, 0)
+        for side in range(2):
+            add_to(kept(g, turn, side), got.at[g, turn, side])
         step_two(g, turn).start()
 
     def z_of(turn):
         return 2 * core + order(turn)
 
     def add_held(g, turn, source):
-        side = bits[1 - turn]
-
-        def body(part, carry):
-            one[g, turn, side, part] = one[g, turn, side, part] + source[part]
-            return carry
-
-        lax.fori_loop(0, 2, body, 0)
+        add_to(kept(g, turn, bits[1 - turn]), source)
 
     def line_copy(g, turn, way, target):
-        held = one.at[g, turn, bits[1 - turn]]
+        held = kept(g, turn, bits[1 - turn])
         which = order(turn)
         return push(held, line.at[g, which, way], send_z.at[g, turn], recv_z.at[g, which, way], target)
 
@@ -1099,38 +1347,39 @@
 
         @pl.when(z == goal)
         def _():
-            held = one.at[g, turn, bits[1 - turn]]
+            held = kept(g, turn, bits[1 - turn])
             pltpu.make_async_copy(held.at[core], out_ref.at[g], local.at[g]).start()
             push(held.at[1 - core], out_ref.at[g], send_c.at[g], recv_c.at[g], sibling).start()
 
-    for g in range(count):
+    for g in range(arrays):
         for turn in range(2):
             step_one(g, turn).start()
             fetch(g, turn).start()
     many = rows_ref.shape[0]
-    for a in range(many):
+
+    def rows_leave(a):
         for j in range(2):
             stays = jnp.logical_and(home, 2 * core + j == z)
 
             @pl.when(stays)
-            def _(a=a, j=j):
-                pltpu.make_async_copy(rows_ref.at[a, j], back_ref.at[a, z % 2], local.at[count + a]).start()
+            def _(j=j):
+                pltpu.make_async_copy(
+                    rows_ref.at[a, j], back_ref.at[a, z % 2], local.at[count + a]
+                ).start()
 
             @pl.when(jnp.logical_not(stays))
-            def _(a=a, j=j):
+            def _(j=j):
                 target = (plane * 2 + z // 2, 2 * core + j)
                 push(
-                    rows_ref.at[a, j], back_ref.at[a, z % 2], send_r.at[a, j], recv_r.at[a, z % 2], target
+                    rows_ref.at[a, j],
+                    back_ref.at[a, z % 2],
+                    send_r.at[a, j],
+                    recv_r.at[a, z % 2],
+                    target,
                 ).start()
 
-    gains = []
-    for step in range(1, 8):
-        mate = lax.rem(dp + step, 8)
-        gains.append(
-            push(gain_ref.at[mate], gain_got.at[8 - step], send_g.at[step], recv_g.at[8 - step], (mate, z))
-        )
-    for copy in gains:
-        copy.start()
+    rows_ref[0] = first_ref[...]
+    rows_leave(0)
 
     @pl.when(home)
     def _():
@@ -1139,9 +1388,124 @@
             target = (dp, lax.rem(z + step, 4))
             push(cond_ref, cond_out.at[z % 2], send_k.at[step], recv_k.at[z % 2], target).start()
 
+    def heads(pair, carry):
+        lanes = pl.ds(pl.multiple_of(pair * 128, 128), 128)
+        grads = backward_pair(
+            qkv_ref[0, :, lanes],
+            qkv_ref[1, :, lanes],
+            qkv_ref[2, :, lanes],
+            mixed_ref[:, lanes],
+            valid_ref[:, :1] > 0.0,
+        )
+        for i in range(3):
+            thirds[i, :, lanes] = grads[i]
+        return carry
+
+    lax.fori_loop(0, qkv_ref.shape[2] // 128, heads, 0)
+
+    def weight_grads(i):
+        def body(block, carry):
+            value = jnp.dot(turned_ref[block], thirds[i], preferred_element_type=F32)
+            made[i, block // 4, block // 2 % 2, block % 2] = value.astype(BF)
+            return carry
+
+        lax.fori_loop(0, 8, body, 0)
+        for turn in range(2):
+            step_one(arrays + i, turn).start()
+
+    half = thirds.shape[1] // 2
+    tile = 256
+
+    def row_grads(side, put):
+        rows = pl.ds(pl.multiple_of(side * half, 16), half)
+        blocks = whole_ref.shape[1] // tile
+
+        def fill(block, slot):
+            spots = pl.ds(pl.multiple_of(block * tile, tile), tile)
+            return pltpu.make_async_copy(whole_ref.at[:, spots, :], whole.at[slot], extra.at[slot])
+
+        fill(0, 0).start()
+
+        def body(block, carry):
+            slot = block % 2
+
+            @pl.when(block + 1 < blocks)
+            def _():
+                fill(block + 1, 1 - slot).start()
+
+            fill(block, slot).wait()
+            spots = pl.ds(pl.multiple_of(block * tile, tile), tile)
+            total = None
+            for i in range(3):
+                value = lax.dot_general(
+                    thirds[i, rows, :],
+                    whole[slot, i],
+                    (((1,), (1,)), ((), ())),
+                    preferred_element_type=F32,
+                )
+                total = value if total is None else total + value
+            put(spots, total)
+            return carry
+
+        lax.fori_loop(0, blocks, body, 0)
+
+    def put_out(spots, value):
+        for j in range(2):
+            part_out[j, :, spots] = value[j * (half // 2) : (j + 1) * (half // 2)].astype(BF)
+
+    def put_own(spots, value):
+        for j in range(2):
+            part_own[j, :, spots] = value[j * (half // 2) : (j + 1) * (half // 2)]
+
+    def ones(g):
+        after_one(g, 0)
+        after_one(g, 1)
+
+    def twos(g):
+        after_two(g, 0)
+        after_two(g, 1)
+
+    ones(0)
+    weight_grads(0)
+    ones(1)
+    twos(0)
+    weight_grads(1)
+    weight_grads(2)
+    ones(2)
+    twos(1)
+    row_grads(1 - core, put_out)
+    parts = push(part_out, part_in, extra.at[3], extra.at[4], sibling)
+    parts.start()
+    row_grads(core, put_own)
+    parts.wait()
+    gain_one = jnp.zeros((1, part_own.shape[2]), F32)
+    for j in range(2):
+        value = part_own[j] + part_in[j].astype(F32)
+        scaled = scaled_ref[j]
+        grad_scaled = value * factor_ref[:1]
+        centre = jnp.mean(grad_scaled, axis=1, keepdims=True)
+        slope = jnp.mean(grad_scaled * scaled, axis=1, keepdims=True)
+        moved = inverse_ref[j, :, :1] * (grad_scaled - centre - scaled * slope)
+        rows_ref[1, j] = (stream_ref[j] + moved).astype(BF)
+        gain_one = gain_one + jnp.sum(value * scaled, axis=0, keepdims=True)
+    rows_leave(1)
+    line_of = lax.broadcasted_iota(jnp.int32, gain_ref.shape, 0)
+    gain_ref[...] = gain_in[...] + jnp.where(line_of == 0, gain_one, 0.0)
+    gains = []
+    for step in range(1, 8):
+        mate = lax.rem(dp + step, 8)
+        gains.append(
+            push(gain_ref, gain_got.at[8 - step], send_g.at[step], recv_g.at[8 - step], (mate, z))
+        )
+    for copy in gains:
+        copy.start()
+    ones(3)
+    twos(2)
+    ones(4)
+    twos(3)
     for copy in gains:
         copy.wait()
-    total = gain_ref[dp]
+    total = gain_ref[...]
     for step in range(1, 8):
         total = total + gain_got[step]
     gain_sum[...] = total
@@ -1151,14 +1515,11 @@
         sums.append(push(gain_sum, gain_line.at[4 - step], send_h.at[step], recv_h.at[4 - step], target))
     for copy in sums:
         copy.start()
-
-    pieces = [(g, turn) for g in range(count) for turn in range(2)]
-    lag = 2
-    for i in range(len(pieces) + lag):
-        if i < len(pieces):
-            after_one(*pieces[i])
-        if i >= lag:
-            after_two(*pieces[i - lag])
+    ones(5)
+    twos(4)
+    ones(6)
+    twos(5)
+    twos(6)
 
     for copy in sums:
         copy.wait()
@@ -1214,28 +1575,38 @@
             push(cond_ref, cond_out.at[s], send_k.at[1], recv_k.at[s], sibling).wait_recv()
 
 
-def share_moves(grads, groups, rows, gains, cond):
-    count = len(groups)
+def share_moves(grads, qkv, mixed, valid, turned, whole, stream, scaled, inverse, factor, output, gains, cond):
+    arrays = len(grads)
+    count = arrays + 3
     depth, width = grads[0].shape[1] // 8, grads[0].shape[2] // 2
-    many = rows.shape[0]
+    many, parts, height, model_width = 2, *output.shape
+    padded, columns = qkv.shape[1:]
     return pl.pallas_call(
-        functools.partial(share_kernel, groups=groups, arrays=len(grads)),
+        functools.partial(share_kernel, arrays=arrays),
         out_shape=[
             jax.ShapeDtypeStruct((count, depth, width), BF),
-            jax.ShapeDtypeStruct(rows.shape, BF),
-            jax.ShapeDtypeStruct(gains.shape[1:], F32),
+            jax.ShapeDtypeStruct((many, *output.shape), BF),
+            jax.ShapeDtypeStruct(gains.shape, F32),
             jax.ShapeDtypeStruct((2, *cond.shape), BF),
         ],
-        in_specs=any_specs(len(grads)) + near_specs(3),
+        in_specs=any_specs(arrays) + near_specs(4) + any_specs(1) + near_specs(7),
         out_specs=near_specs(1) + any_specs(1) + near_specs(1) + any_specs(1),
         scratch_shapes=[
-            pltpu.VMEM((count, 2, 2, 2, depth, width), BF),
+            pltpu.VMEM((arrays, 2, 2, 2, depth, width), BF),
             pltpu.VMEM((count, 2, 2, 2, depth, width), BF),
             pltpu.VMEM((count, 2, 2, depth, width), BF),
             pltpu.VMEM((count, 2, 2, 2, depth, width), BF),
+            pltpu.VMEM((8, *gains.shape), F32),
             pltpu.VMEM(gains.shape, F32),
-            pltpu.VMEM(gains.shape[1:], F32),
-            pltpu.VMEM((4, *gains.shape[1:]), F32),
+            pltpu.VMEM(gains.shape, F32),
+            pltpu.VMEM((4, *gains.shape), F32),
+            pltpu.VMEM((3, 2, 2, 2, depth, 2 * width), BF),
+            pltpu.VMEM((2, 3, 256, 2 * width), BF),
+            pltpu.VMEM(qkv.shape, BF),
+            pltpu.VMEM(output.shape, BF),
+            pltpu.VMEM(output.shape, BF),
+            pltpu.VMEM(output.shape, F32),
+            pltpu.VMEM((many, *output.shape), BF),
             dma(count, 2),
             dma(count, 2),
             dma(count, 2),
@@ -1254,12 +1625,27 @@
             dma(4),
             dma(2),
             dma(count + many + 1),
+            dma(5),
         ],
         compiler_params=pltpu.CompilerParams(
-            collective_id=5, has_side_effects=True, vmem_limit_bytes=ROOM
+            collective_id=5, has_side_effects=True, vmem_limit_bytes=61 << 20
         ),
         name="share_moves",
-    )(*[grad.reshape(grad.shape[0], 2, 2, 2, depth, 2 * width) for grad in grads], rows, gains, cond)
+    )(
+        *[grad.reshape(1, 2, 2, 2, depth, 2 * width) for grad in grads],
+        qkv,
+        mixed,
+        valid,
+        turned,
+        whole,
+        stream,
+        scaled,
+        inverse,
+        factor,
+        output,
+        gains,
+        cond,
+    )
 
 
 def chip_shards(
@@ -1307,54 +1693,49 @@
     wide = jnp.moveaxis(wide.reshape(3, depth, 4, units // 4), 2, 1)
     room = -tokens % 16
     cond = jnp.pad(take(context, z % 2, 0), ((0, room), (0, 0)))
-    size = jnp.broadcast_to(take(lengths, z % 2, 0), (8, 128))
-    sequence, wide, cond, size = first_moves(inputs, wide, cond, size)
-    stream = sequence.reshape(padded, model_width).astype(F32)
-    length = take(size, z // 2, 0)[0, 0]
-    cond = take(cond, z // 2, 0)[:tokens]
-    qkv_whole, so_whole, cq_whole, cc_whole, co_whole, gu_whole = weights_moves(
-        narrow, wide, ((0, 0), (0, 1), (0, 2), (1, 0), (2, 0), (3, 0), (4, 0)), 2
-    )
-    wide, qkv_whole = lax.optimization_barrier((wide, qkv_whole))
-    quarter = lax.all_gather(wide[2:], "tensor", axis=0)
+    apart = cond.reshape(-1, 8, 1, cc_depth)
+    none = jnp.zeros_like(apart)
+    spread_cond = jnp.stack(
+        [jnp.concatenate([apart, none], 2), jnp.concatenate([none, apart], 2)]
+    ).reshape(2, -1, model_width)
+    weights, kept = weights_moves(
+        narrow,
+        wide,
+        inputs,
+        cotangent,
+        jnp.broadcast_to(take(lengths, z % 2, 0), (8, 128)),
+        spread_cond,
+        jnp.pad(norm_gains, ((0, 5), (0, 0))),
+        ((0, 0), (0, 1), (0, 2), (1, 0), (2, 0), (3, 0), (4, 0)),
+        tokens,
+    )
+    qkv_whole, so_whole, cq_whole, cc_whole, co_whole, gu_whole, down_whole = weights
     so_whole, cq_whole, co_whole = so_whole[0], cq_whole[0], co_whole[0]
+    down_whole = down_whole[0]
     cc_whole = cc_whole[0].reshape(8, 2, cc_depth, -1)
     cc_whole = jnp.moveaxis(cc_whole, 1, 0).reshape(2, 8 * cc_depth, -1)
-    cot_half = rows_in(cotangent, z)
-    cot = both_halves(cot_half, swap(cot_half, CORE)).astype(F32)
-
-    positions = jnp.arange(padded, dtype=jnp.int32)
-    key_valid = positions < length
-    row_keep = key_valid.astype(F32)[:, None]
+    normed_one, qkv, mixed_one, stream, normed_two, cross_rows, cond_rows = kept[:7]
+    mixed_two, stream_half, rows_three, sequence, cot, grad_branch, row_keep, conds = kept[7:]
+    row_keep = row_keep[:, :1]
     keep_half = own_half(row_keep)
-    context_valid = jnp.ones((cond.shape[0],), dtype=jnp.bool_)
-
-    normed_one, scaled_one, inverse_one = norm_rows(stream, norm_gains[0])
-    normed_one = normed_one.astype(BF)
-    qkv = jnp.einsum("td,kde->kte", normed_one, qkv_whole, preferred_element_type=F32).astype(BF)
-    mixed_one, logsum_one = attend_forward((qkv[0], qkv[1], qkv[2], key_valid))
-    branch = jnp.einsum("te,de->td", mixed_one, so_whole, preferred_element_type=F32)
-    stream = stream + row_keep * pair_sum(branch)
-    normed_two, scaled_two, inverse_two = norm_rows(stream, norm_gains[1])
-    normed_two = normed_two.astype(BF)
-    cross_rows = jnp.einsum("td,de->te", normed_two, cq_whole, preferred_element_type=F32).astype(BF)
-    cond_rows = jnp.einsum("sd,kde->kse", cond, cc_whole, preferred_element_type=F32).astype(BF)
-    mixed_two, logsum_two = attend_forward((cross_rows, cond_rows[0], cond_rows[1], context_valid))
-    branch = jnp.einsum("te,de->td", mixed_two, co_whole, preferred_element_type=F32)
-    stream = stream + row_keep * pair_sum(branch)
-    stream_half = own_half(stream)
-    normed_three, scaled_three, inverse_three = norm_rows(stream_half, norm_gains[2])
-    rows_three, down_whole = second_moves(
-        normed_three.astype(BF).reshape(2, -1, model_width), quarter
-    )
+    context_valid = jnp.ones((tokens,), dtype=jnp.bool_)
+    cond = take(conds, z // 2, 0)[0].reshape(-1, 8, 2, cc_depth)[:tokens, :, 0]
+    cond = cond.reshape(tokens, -1)
+    cond_rows = cond_rows[:, :tokens]
+    stream_half = stream_half.reshape(half_rows, model_width)
     rows_three = rows_three.reshape(-1, model_width)
-    down_whole = down_whole.reshape(model_width, units)
+    grad_branch = grad_branch.reshape(-1, model_width)
+    cot = cot.reshape(padded, model_width).astype(F32)
+    _, scaled_one, inverse_one = norm_rows(
+        sequence.reshape(padded, model_width).astype(F32), norm_gains[0]
+    )
+    _, scaled_two, inverse_two = norm_rows(stream, norm_gains[1])
+    _, scaled_three, inverse_three = norm_rows(stream_half, norm_gains[2])
     gate_rows = jnp.einsum("td,kde->kte", rows_three, gu_whole, preferred_element_type=F32)
     sigmoid_gate = jax.nn.sigmoid(gate_rows[0])
     hidden = (gate_rows[0] * sigmoid_gate * gate_rows[1]).astype(BF)
 
     grad_stream = row_keep * cot
-    grad_branch = plane_rows((keep_half * own_half(grad_stream)).astype(BF))
     grad_hidden = jnp.einsum("td,df->tf", grad_branch, down_whole, preferred_element_type=F32)
     grad_gate = (
         grad_hidden * gate_rows[1] * sigmoid_gate * (1.0 + gate_rows[0] * (1.0 - sigmoid_gate))
@@ -1380,8 +1761,10 @@
     grad_stream = grad_stream + both_halves(grad_norm, swap(grad_norm.astype(BF), CORE).astype(F32))
     grad_branch = (row_keep * grad_stream).astype(BF)
     grad_mixed = jnp.einsum("td,de->te", grad_branch, co_whole, preferred_element_type=F32).astype(BF)
+    scores = masked_scores(split_heads(cross_rows), split_heads(cond_rows[0]), context_valid)
+    log_sums = jax.nn.logsumexp(scores, axis=-1)
     grad_query, grad_key, grad_value = attend_backward(
-        (cross_rows, cond_rows[0], cond_rows[1], logsum_two, grad_mixed, context_valid)
+        (cross_rows, cond_rows[0], cond_rows[1], log_sums, grad_mixed, context_valid)
     )
     partial_value = jnp.einsum("te,de->td", grad_query, cq_whole, preferred_element_type=F32)
     grad_norm, gain_rows = norm_back(
@@ -1400,35 +1783,32 @@
     grad_branch = (row_keep * grad_stream).astype(BF)
     grad_mixed = jnp.einsum("td,de->te", grad_branch, so_whole, preferred_element_type=F32).astype(BF)
     grad_after = jnp.einsum("td,te->de", grad_branch, mixed_one, preferred_element_type=F32)
-    grad_triple = jnp.stack(
-        attend_backward((qkv[0], qkv[1], qkv[2], logsum_one, grad_mixed, key_valid))
-    )
-    grad_self = jnp.einsum("td,kte->kde", normed_one, grad_triple, preferred_element_type=F32)
-    partial_value = jnp.einsum("kte,kde->td", grad_triple, qkv_whole, preferred_element_type=F32)
-    grad_norm, gain_rows = norm_back(
-        pair_sum(partial_value), scaled_one, inverse_one, norm_gains[0]
-    )
-    gain_one = 0.5 * jnp.sum(gain_rows, axis=0)
-    grad_inputs = own_half(grad_stream + grad_norm).astype(BF)
-    back = jnp.stack([output, grad_inputs]).reshape(2, 2, -1, model_width)
-    gains = jnp.stack([gain_one, gain_two, gain_three]).reshape(3, 8, -1)
-    gains = jnp.pad(jnp.moveaxis(gains, 0, 1), ((0, 0), (0, 5), (0, 0)))
+    gains = jnp.stack([jnp.zeros_like(gain_two), gain_two, gain_three])
     shares, back, gains, conds = share_moves(
         [
             grad_merge.astype(BF)[None],
             grad_cross.astype(BF)[None],
             grad_cc.astype(BF)[None],
             grad_after.astype(BF)[None],
-            grad_self.astype(BF),
         ],
-        ((0, 0), (1, 0), (2, 0), (3, 0), (4, 0), (4, 1), (4, 2)),
-        back,
-        gains,
+        qkv,
+        grad_mixed,
+        jnp.broadcast_to(row_keep, (padded, 128)),
+        normed_one.T.reshape(8, -1, padded),
+        qkv_whole,
+        own_half(grad_stream).reshape(2, -1, model_width),
+        own_half(scaled_one).reshape(2, -1, model_width),
+        jnp.broadcast_to(own_half(inverse_one), (half_rows, 128)).reshape(2, -1, 128),
+        jnp.broadcast_to(norm_gains[0], (8, model_width)),
+        output.reshape(2, -1, model_width),
+        jnp.pad(gains, ((0, 5), (0, 0))),
         context_part,
     )
+    gains = lax.dynamic_slice_in_dim(gains[:3], dp * depth, depth, 1)
+    shares = shares.astype(F32)
+    wide_grads, back = lax.optimization_barrier((wide_grads, back))
     shared = lax.all_to_all(wide_grads, "dp", 1, 1, axis_index_groups=[[0, 2, 4, 6], [1, 3, 5, 7]])
     shared = jnp.moveaxis(shared, 1, 2).reshape(3, depth, units).astype(F32)
-    shares = shares.astype(F32)
     return (
         back[0],
         back[1].astype(F32),
@@ -1440,7 +1820,7 @@
         shares[0].T,
         shared[:2],
         shared[2].T,
-        gains[:3],
+        gains,
     )
 
 

time: 905 us -> 750 us (0.83)
  matrix products: 204 us -> 106 us
  other arithmetic: 93.3 us -> 56.3 us
  starting transfers between devices: 21.9 us -> 8.81 us
  local copies, waits for them, and re-layouts: 75 us -> 64.8 us
    pallas_call x1, Pallas kernels: 176 us -> 244 us  [weights_moves(): pl.pallas_call(functools.partial(weights_kernel, groups=groups, wides=wid...]
    pallas_call x3 -> x1, Pallas kernels: 253 us -> 185 us  [share_moves(): pl.pallas_call(functools.partial(share_kernel, arrays=arrays), out_shape=...]
    dot_general x9 -> x0, matrix products: 47.4 us -> none  [the longest x2 10.2 us: attend_forward(): jnp.einsum('hqk,khd->qhd', probs, split_heads(value_rows), preferred_elem...]
    convert_element_type x5 -> x0, local copies, waits for them, and re-layouts: 15 us -> none  [the longest x1 10.4 us: chip_shards(): grad_self.astype(BF)]
    all_to_all x1, waiting for transfers between devices: 0.01 us -> 14.6 us  [chip_shards(): lax.all_to_all(wide_grads, 'dp', 1, 1, axis_index_groups=[[0, 2, 4, 6], [...]
    convert_element_type x2 -> x1, other arithmetic: 13 us -> 1 us  [attend_backward(): grad_scores = (probs * (grad_probs - inner_sum)).astype(jnp.bfloat16)]
    reduce_sum x3 -> x1, other arithmetic: 12.2 us -> 1.39 us  [chip_shards(): log_sums = jax.nn.logsumexp(scores, axis=-1)]
    dot_general x2 -> x1, matrix products: 14.6 us -> 3.94 us  [attend_backward(): jnp.einsum('qhd,khd->hqk', grads, values, preferred_element_type=jnp.floa...]
  transfers between devices with their start and end apart: 20 -> 9, of which waited for: 4 -> 3; matrix products, arithmetic and copies ran while one was open for 29% -> 16% of each run, Pallas kernels for 44% -> 25%
where the time goes in v3:
time: 750 us; the launch traced here: 743 us
  Pallas kernels  462 us (62%)
  matrix products  106 us (14%)
  local copies, waits for them, and re-layouts  64.8 us (9%)
  other arithmetic  56.3 us (8%)
  waiting for transfers between devices  29.6 us (4%)
  between operations  15.3 us (2%)
  starting transfers between devices  8.81 us (1%)
    pallas_call x1, Pallas kernels, weights_moves(): pl.pallas_call(functools.partial(weights_kernel, groups=groups, wides=wid...  244 us
    pallas_call x1, Pallas kernels, share_moves(): pl.pallas_call(functools.partial(share_kernel, arrays=arrays), out_shape=...  185 us
    pallas_call x1, Pallas kernels, third_moves(): pl.pallas_call(functools.partial(third_kernel, counts=counts), out_shape=...  33.6 us
    dot_general x1, matrix products, chip_shards(): jnp.einsum('td,ktf->kdf', rows_three, grad_expand, preferred_element_type...  17.9 us
    dot_general x1, matrix products, chip_shards(): jnp.einsum('ktf,kdf->td', grad_expand, gu_whole, preferred_element_type=F32)  16.6 us
  transfers between devices with their start and end apart: 9, of which 3 were waited for; matrix products, arithmetic and copies ran while one was open for 16% of the time, Pallas kernels for 25%

profile of v3, /device:TPU:0, one launch (start us, length us, event | category | flops | bytes accessed | tf_op | source)
XLA Modules:
  0.0 743.3 jit_solution(15783186356919881905)
XLA Ops:
  7.3 2.0 convert_dynamic-update-slice_fusion
  10.3 1.3 convert_bitcast_fusion.1
  11.8 1.8 convert.56
  15.3 2.5 fusion.48
  17.9 1.7 stack.49
  19.6 1.4 stack.48
  20.9 1.7 bitcast_dynamic-update-slice_fusion.1
  22.6 1.6 bitcast_dynamic-update-slice_fusion.3
  25.0 1.6 bitcast_dynamic-update-slice_fusion.shard_ref
  26.6 1.4 maximum_bitcast_fusion.units_ref
  30.9 243.6 %weights_moves.1 = (bf16[3,4,2,192,768]{4,3,2,1,0:T(8,128)(2,1)}, bf16[1,4,2,192,768]{4,3,2,1,0:T(8,128)(2,1)}, bf16[1,4,2,192,768]{4,3,2,1,0:T(8,128)(2,1)}, bf...) custom-call(bf16[7,192,384]{2,1,0:T(8,128)(2,1)} %bitcast_dynamic-up, ...), custom_call_target="tpu_custom_call" | custom-call | tf_op jit(solution)/shard_map/weights_moves/pallas_call | solution.py:997
  274.5 14.3 %convolution_bitcast_fusion = f32[2,1088,1536]{2,1,0:T(8,128)S(1)} fusion(bf16[1088,1536,1]{1,0,2:T(8,128)(2,1)} %bitcast.325, bf16[2,1536,1536]{2,1,0:T(8,128)(2,1)} %bitcast.319), kind=kOutput, calls=%fused_computation | convolution fusion | flops 10267656192 | bytes 26148864 | tf_op jit(solution)/shard_map/td,kde->kte/dot_general | solution.py:1734
  288.8 9.0 %fusion.16 = (bf16[1,1088,1536]{2,1,0:T(8,128)(2,1)}, bf16[1,1088,1536]{2,1,0:T(8,128)(2,1)}) fusion(f32[2,1088,1536]{2,1,0:T(8,128)S(1)} %convolution_bitcast_fusion, bf16[1088,1536]{1,0:T(8,128)(2,1)S(1)} %bitcast.323, bf16[1536,1536]{1,0:T(8,128)(2,1)S(1)} %bitcast.322), kind=kOutput, calls=%fused_computation.48 | convolution fusion | flops 5155553280 | bytes 28114944 | tf_op jit(solution)/shard_map/td,df->tf/dot_general | solution.py:1739
  297.9 16.6 %fusion = bf16[1088,1536]{1,0:T(8,128)(2,1)} fusion(bf16[2,1536,1536]{2,1,0:T(8,128)(2,1)} %bitcast.320, bf16[1,1088,1536]{2,1,0:T(8,128)(2,1)} %get-tuple-element.118, bf16[1,1088,1536]{2,1,0:T(8,128)(2,1)} %get-tuple-element.117), kind=kOutput, calls=%fused_computation.3 | convolution fusion | flops 10272669696 | bytes 19464192 | tf_op jit(solution)/shard_map/ktf,kdf->td/dot_general | solution.py:1745
  314.5 17.9 %convolution_convert_fusion = bf16[2,1536,1536]{1,2,0:T(8,128)(2,1)} fusion(bf16[1088,1536,1]{1,0,2:T(8,128)(2,1)} %bitcast.326, bf16[1,1088,1536]{2,1,0:T(8,128)(2,1)} %get-tuple-element.118, bf16[1,1088,1536]{2,1,0:T(8,128)(2,1)} %get-tuple-element.117), kind=kOutput, calls=%fused_computation.1 | convolution fusion | flops 10275717120 | bytes 19464192 | tf_op jit(solution)/shard_map/td,ktf->kdf/dot_general | solution.py:1747
  332.4 2.1 multiply_convert_fusion
  334.4 8.3 %convolution_convert_fusion.2 = bf16[1536,1536]{1,0:T(8,128)(2,1)} fusion(bf16[1088,1536]{1,0:T(8,128)(2,1)S(1)} %bitcast.324, bf16[1,1088,1536]{2,1,0:T(8,128)(2,1)S(1)} %multiply_convert_fusion), kind=kOutput, calls=%fused_computation.5 | convolution fusion | flops 5136187392 | bytes 11403264 | tf_op jit(solution)/shard_map/td,tf->df/dot_general | solution.py:1746
  342.7 33.6 %third_moves.1 = (f32[2,136,1536]{2,1,0:T(8,128)}, bf16[4,3,4,192,384]{4,3,2,1,0:T(8,128)(2,1)}) custom-call(bf16[4,2,136,1536]{3,2,1,0:T(8,128)(2,1)} %bitcast.301, bf16[2,4,2,192,1536]{4,3,2,1,0:T(8,128)(2,1)} %bitcast.278, bf16[1,4,2,192,1536]{4,3,2,1,0:T(8,128)(2,1)} %bitcast.294), custom_call_target="tpu_custom_call" | custom-call | tf_op jit(solution)/shard_map/third_moves/pallas_call | solution.py:1154
  376.3 8.3 %convolution_convert_fusion.1 = bf16[1088,1536]{1,0:T(8,128)(2,1)S(1)} fusion(bf16[1536,1536]{1,0:T(8,128)(2,1)} %bitcast.321, bf16[1,1088,1536]{2,1,0:T(8,128)(2,1)} %copy-done.19), kind=kOutput, calls=%fused_computation.4 | convolution fusion | flops 5135499264 | bytes 11403264 | tf_op jit(solution)/shard_map/tf,df->td/dot_general | solution.py:1757
  390.9 1.8 convert_reduce_fusion
  393.4 2.0 multiply_reduce_fusion.3
  396.2 2.2 reduce_sum.132
  399.3 1.5 copy.62
  402.2 3.6 convert_element_type.341
  407.0 1.8 constant_dynamic-slice_fusion.6
  408.8 2.3 reshape_squeeze.18
  411.1 3.2 slice_reduce_fusion
  414.3 1.9 reshape.495
  416.2 4.2 copy.71
  421.1 3.2 copy.73
  428.3 2.3 bitcast_convert_fusion.1
  433.6 8.6 %collective-permute-done.3 = bf16[136,1536]{1,0:T(8,128)(2,1)S(1)} collective-permute-done((bf16[136,1536]{1,0:T(8,128)(2,1)S(1)}, bf16[136,1536]{1,0:T(8,128)(2,1)S(1)}, u32[]{:S(2)}, u32[]{:S(2)}) %collective-permute-start.3) | collective-permute-done | bytes 417824 | tf_op jit(solution)/shard_map/ppermute | solution.py:342
  442.1 1.4 fusion.38
  445.5 1.4 exponential_reduce_fusion
  446.9 6.3 collective-permute-done.5
  454.5 1.8 multiply_reduce_fusion.7
  456.5 2.2 fusion.46
  459.7 1.5 fusion.24
  461.7 1.5 copy-done.8
  463.1 2.5 pad_maximum_fusion.3
  465.6 2.4 convolution_convert_fusion.8
  468.0 1.7 copy.64
  469.7 3.9 multiply_reduce_fusion
  475.3 1.4 copy-done.49
  476.7 4.1 fusion.50
  481.1 1.7 fusion.32
  484.0 1.7 fusion.31
  485.8 1.3 copy.67
  487.1 2.6 fusion.51
  489.8 3.5 convolution_convert_fusion.4
  494.3 1.6 copy.70
  497.5 3.1 multiply_reduce_fusion.2
  501.3 3.4 multiply_add_fusion
  504.7 1.3 constant_dynamic-slice_fusion.5
  506.1 3.6 convolution_convert_fusion.3
  509.7 3.6 convolution_convert_fusion.5
  513.3 2.4 convolution_convert_fusion.7.refs_5_
  518.0 185.1 %share_moves.1 = (bf16[7,192,384]{2,1,0:T(8,128)(2,1)}, bf16[2,2,136,1536]{3,2,1,0:T(8,128)(2,1)}, f32[8,1536]{1,0:T(8,128)}, bf16[2,144,768]{2,1,0:T(8,128)(2,1)}) custom-call(bf16[1,2,2,2,192,768]{5,4,3,2,1,0:T(8,128)(2,1)} %bitcast.304, bf16[1,2,2,2,192,768]{5,4,3,2,1,0:T(8,128)(2,1)} %bitcast.302, bf16[1,2,2,2,192,768]{5,4,3,2,1,0:T(8,128)(2,1)} %bitcast.277, ...), custom_call_target="tpu_custom_call" | custom-call | tf_op jit(solution)/shard_map/share_moves/pallas_call | solution.py:1584
  703.2 2.9 copy.74
  706.1 3.6 all-to-all-start
  712.6 1.3 copy.77
  715.5 1.6 bitcast_convert_fusion
  717.2 14.6 %all-to-all-done = bf16[3,4,192,384]{3,2,0,1:T(8,128)(2,1)S(1)} async-done(((bf16[3,4,192,384]{3,2,0,1:T(8,128)(2,1)}), bf16[3,4,192,384]{3,2,0,1:T(8,128)(2,1)S(1)}, u32[]{:S(2)}, u32[]{:S(2)}) %all-to-all-start) | async-done | bytes 1769504 | tf_op jit(solution)/shard_map/all_to_all | solution.py:1810
  732.4 1.7 copy.85
  (204 shorter events, 45.6 us)
Async XLA Ops:
  7.2 7.2 copy-start
  7.2 696.0 %reduce-scatter.2.cloned.1.call-start = ((), (), s32[]{:S(2)}) async-start(), calls=%async_computation.2 | async-start | bytes 8847360 | tf_op jit(solution)/shard_map/reduce_scatter | solution.py:1756
  11.7 2.0 copy-start.54
  20.9 7.1 copy-start.20
  22.6 6.4 copy-start.27
  274.4 14.4 %copy-start.46 = (bf16[1,4,2,192,1536]{4,3,2,1,0:T(8,128)(2,1)S(1)}, bf16[1,4,2,192,1536]{4,3,2,1,0:T(8,128)(2,1)}, u32[]{:S(2)}) copy-start(bf16[1,4,2,192,1536]{4,3,2,1,0:T(8,128)(2,1)} %get-tuple-element.42) | copy-start | bytes 14155780
  274.5 14.4 %copy-start.47 = (bf16[4,2,136,1536]{3,2,1,0:T(8,128)(2,1)S(1)}, bf16[4,2,136,1536]{3,2,1,0:T(8,128)(2,1)}, u32[]{:S(2)}) copy-start(bf16[4,2,136,1536]{3,2,1,0:T(8,128)(2,1)} %get-tuple-element.41) | copy-start | bytes 10027012
  334.4 8.3 %copy-start.19 = (bf16[1,1088,1536]{2,1,0:T(8,128)(2,1)}, bf16[1,1088,1536]{2,1,0:T(8,128)(2,1)S(1)}, u32[]{:S(2)}) copy-start(bf16[1,1088,1536]{2,1,0:T(8,128)(2,1)S(1)} %multiply_convert_fusion) | copy-start | bytes 10027012
  384.7 3.3 copy-start.17
  384.7 4.1 copy-start.6
  384.8 5.2 copy-start.26
  385.8 44.8 %collective-permute-start.2 = (bf16[2,136,1536]{2,1,0:T(8,128)(2,1)}, bf16[2,136,1536]{2,1,0:T(8,128)(2,1)}, u32[]{:S(2)}, u32[]{:S(2)}) collective-permute-start(bf16[2,136,1536]{2,1,0:T(8,128)(2,1)} %pad_maximum_fusion.6), channel_id=1, source_target_pairs={{0,8},{4,12},{8,0},{12,4},{16,24},{20,28},{24,16},{28,20},{1,9},{5... | collective-permute-start | bytes 2506760 | tf_op jit(solution)/shard_map/ppermute | solution.py:342
  388.0 45.6 %collective-permute-start.4 = (bf16[2,136,1536]{2,1,0:T(8,128)(2,1)}, bf16[2,136,1536]{2,1,0:T(8,128)(2,1)}, u32[]{:S(2)}, u32[]{:S(2)}) collective-permute-start(bf16[2,136,1536]{2,1,0:T(8,128)(2,1)} %pad_maximum_fusion.7), channel_id=1, source_target_pairs={{0,16},{4,20},{8,24},{12,28},{16,0},{20,4},{24,8},{28,12},{1,17},{... | collective-permute-start | bytes 2506760 | tf_op jit(solution)/shard_map/ppermute | solution.py:342
  389.0 9.4 %copy-start.32 = (f32[2,136]{1,0:T(2,128)}, f32[2,136]{1,0:T(2,128)S(1)}, u32[]{:S(2)}) copy-start(f32[2,136]{1,0:T(2,128)S(1)} %broadcast_multiply_fusion.7) | copy-start | bytes 3268
  390.9 7.5 %copy-start.25 = (bf16[2,144,768]{2,1,0:T(8,128)(2,1)S(1)}, bf16[2,144,768]{2,1,0:T(8,128)(2,1)}, u32[]{:S(2)}) copy-start(bf16[2,144,768]{2,1,0:T(8,128)(2,1)} %get-tuple-element.52) | copy-start | bytes 1327108
  400.8 5.0 copy-start.35
  424.3 2.2 copy-start.4
  424.4 3.9 copy-start.7
  425.2 20.2 %copy-start.2 = (f32[12,544,130]{1,2,0:T(8,128)}, f32[12,544,130]{1,2,0:T(8,128)S(1)}, u32[]{:S(2)}) copy-start(f32[12,544,130]{1,2,0:T(8,128)S(1)} %get-tuple-element.140) | copy-start | bytes 10183684
  427.0 3.6 copy-start.18
  430.6 14.2 %copy-start.28 = (f32[3,1536]{1,0:T(4,128)S(1)}, f32[3,1536]{1,0:T(4,128)}, u32[]{:S(2)}) copy-start(f32[3,1536]{1,0:T(4,128)} %param.23) | copy-start | bytes 55300
  431.7 10.4 %collective-permute-start.3 = (bf16[136,1536]{1,0:T(8,128)(2,1)S(1)}, bf16[136,1536]{1,0:T(8,128)(2,1)S(1)}, u32[]{:S(2)}, u32[]{:S(2)}) collective-permute-start(bf16[136,1536]{1,0:T(8,128)(2,1)S(1)} %fusion.37), channel_id=1, source_target_pairs={{0,16},{4,20},{8,24},{12,28},{16,0},{20,4},{24,8},{28,12},{1,17},{... | collective-permute-start | bytes 1253384 | tf_op jit(solution)/shard_map/ppermute | solution.py:342
  443.5 9.6 %collective-permute-start.5 = (bf16[136,1536]{1,0:T(8,128)(2,1)S(1)}, bf16[136,1536]{1,0:T(8,128)(2,1)S(1)}, u32[]{:S(2)}, u32[]{:S(2)}) collective-permute-start(bf16[136,1536]{1,0:T(8,128)(2,1)S(1)} %get-tuple-element.120), channel_id=1, source_target_pairs={{0,8},{4,12},{8,0},{12,4},{16,24},{20,28},{24,16},{28,20},{1,9},{5... | collective-permute-start | bytes 1253384 | tf_op jit(solution)/shard_map/ppermute | solution.py:342
  445.5 9.0 %copy-start.29 = (f32[1536]{0:T(1024)}, f32[1536]{0:T(1024)S(1)}, u32[]{:S(2)}) copy-start(f32[1536]{0:T(1024)S(1)} %get-tuple-element.111) | copy-start | bytes 18436
  446.9 7.6 %copy-start.15 = (f32[2,136,1536]{2,1,0:T(8,128)S(1)}, f32[2,136,1536]{2,1,0:T(8,128)}, u32[]{:S(2)}) copy-start(f32[2,136,1536]{2,1,0:T(8,128)} %get-tuple-element.49) | copy-start | bytes 5013508
  446.9 7.6 %copy-start.33 = (f32[2,136]{1,0:T(2,128)S(1)}, f32[2,136]{1,0:T(2,128)}, u32[]{:S(2)}) copy-start(f32[2,136]{1,0:T(2,128)} %copy-done.32) | copy-start | bytes 3268
  446.9 7.6 %copy-start.36 = (f32[2,136]{1,0:T(2,128)S(1)}, f32[2,136]{1,0:T(2,128)}, u32[]{:S(2)}) copy-start(f32[2,136]{1,0:T(2,128)} %copy-done.35) | copy-start | bytes 3268
  446.9 7.6 %copy-start.42 = (f32[2,136]{1,0:T(2,128)S(1)}, f32[2,136]{1,0:T(2,128)}, u32[]{:S(2)}) copy-start(f32[2,136]{1,0:T(2,128)} %mul.294) | copy-start | bytes 3268
  454.4 2.1 copy-start.40
  454.4 2.1 copy-start.41
  456.3 2.5 copy-start.43
  456.3 2.5 copy-start.44
  456.5 3.2 copy-start.13
  458.8 2.4 collective-permute-start
  461.2 1.9 copy-start.8
  461.2 1.9 copy-start.37
  463.1 2.5 copy-start.50
  469.7 4.0 copy-start.11
  469.7 4.0 copy-start.3
  474.7 2.0 copy-start.49
  475.3 5.5 copy-start.22
  476.7 4.5 copy-start.12
  480.8 15.8 %collective-permute-start.1 = (bf16[544,1536]{1,0:T(8,128)(2,1)}, bf16[544,1536]{1,0:T(8,128)(2,1)}, u32[]{:S(2)}, u32[]{:S(2)}) collective-permute-start(bf16[544,1536]{1,0:T(8,128)(2,1)} %get-tuple-element.143), channel_id=1, source_target_pairs={{0,4},{4,0},{8,12},{12,8},{16,20},{20,16},{24,28},{28,24},{1,5},{5... | collective-permute-start | bytes 5013512 | tf_op jit(solution)/shard_map/ppermute | solution.py:342
  485.8 4.1 copy-start.23
  485.8 4.1 copy-start.51
  489.6 6.2 collective-permute-start.6
  489.8 3.5 copy-start.24
  493.4 3.2 copy-start.10
  494.2 3.3 copy-start.5
  494.2 3.2 copy-start.30
  494.2 3.2 copy-start.31
  497.5 3.1 copy-start.45
  497.5 3.8 copy-start.9
  497.5 3.8 copy-start.14
  504.7 1.4 copy-start.53
  506.1 3.6 copy-start.52
  509.7 3.6 copy-start.48
  513.3 3.3 copy-start.39
  513.3 4.1 copy-start.34
  703.2 6.5 copy-start.16
  706.1 25.7 %all-to-all-start = ((bf16[3,4,192,384]{3,2,0,1:T(8,128)(2,1)}), bf16[3,4,192,384]{3,2,0,1:T(8,128)(2,1)S(1)}, u32[]{:S(2)}, u32[]{:S(2)}) async-start(bf16[3,4,192,384]{3,2,0,1:T(8,128)(2,1)} %copy.74), calls=%async_computation.1 | async-start | bytes 3538944 | tf_op jit(solution)/shard_map/all_to_all | solution.py:1810
  710.7 3.3 copy-start.38
  710.8 4.7 copy-start.21
  732.4 3.6 copy-start.1
Sparse Core Ops, SparseCore 0:
  376.5 123.3 reduce-scatter.1

commit v4 on v3

--- a/solution.py
+++ b/solution.py
@@ -332,40 +332,12 @@
     )
 
 
-CORE, XBIT, YBIT = 1, 2, 4
 BF = jnp.bfloat16
 F32 = jnp.float32
 
 
-def swap(value, bit):
-    count = lax.axis_size("dp")
-    return lax.ppermute(value, "dp", [(i, i ^ bit) for i in range(count)])
-
-
 def take(value, index, axis):
     return lax.dynamic_index_in_dim(value, index, axis, keepdims=False)
-
-
-def ordered(place, mine, theirs, axis):
-    low = jnp.where(place == 0, mine, theirs)
-    high = jnp.where(place == 0, theirs, mine)
-    return jnp.stack([low, high], axis)
-
-
-def added(mine, theirs):
-    return mine.astype(F32) + theirs.astype(F32)
-
-
-def plane_sums(partial_value):
-    blocks = partial_value.astype(BF).reshape(4, 2, -1, partial_value.shape[-1])
-    upper, lower = blocks[:, 0], blocks[:, 1]
-    got = swap(jnp.stack([upper[1], upper[3]]), XBIT)
-    upper_near, upper_far = added(upper[0], got[0]), added(upper[2], got[1])
-    got = swap(jnp.stack([lower[2], lower[3]]), YBIT)
-    lower_near, lower_far = added(lower[0], got[0]), added(lower[1], got[1])
-    upper_sum = added(upper_near, swap(upper_far.astype(BF), YBIT))
-    lower_sum = added(lower_near, swap(lower_far.astype(BF), XBIT))
-    return jnp.concatenate([upper_sum, lower_sum])
 
 
 MESH = pl.DeviceIdType.MESH
@@ -750,6 +722,7 @@
 
     height = seq_ref.shape[0] * seq_ref.shape[1]
     model_width = seq_ref.shape[2]
+    depth = shard_ref.shape[1]
     half = height // 2
     tile = 256
 
@@ -868,8 +841,9 @@
     def put_cond(which):
         def body(step, carry):
             spots = pl.ds(pl.multiple_of(step * tile, tile), tile)
-            weight = held[5 % 2, :, :, :, spots].reshape(model_width, tile)
-            value = jnp.dot(conds_ref[z // 2, which], weight, preferred_element_type=F32)
+            lines = slice(which * (depth // 2), (which + 1) * (depth // 2))
+            weight = held[5 % 2, :, :, lines, spots].reshape(model_width // 2, tile)
+            value = jnp.dot(conds_ref[z // 2], weight, preferred_element_type=F32)
             pair_ref[which, :, spots] = value.astype(BF)
             return carry
 
@@ -1006,7 +980,7 @@
             like((height, model_width), F32),
             like((height, model_width), BF),
             like((height, columns), BF),
-            like((2, cond.shape[1], columns), BF),
+            like((2, cond.shape[0], columns), BF),
             like((height, columns), BF),
             like((2, block, model_width), F32),
             like((4, 2, block, model_width), BF),
@@ -1064,13 +1038,25 @@
 
 
 def third_kernel(
-    part_ref, *refs, counts
+    part_ref,
+    left_ref,
+    right_ref,
+    other_ref,
+    last_ref,
+    sum_ref,
+    quarter_ref,
+    got,
+    far_x,
+    far_y,
+    made,
+    theirs,
+    turned,
+    send_r,
+    recv_r,
+    send_w,
+    recv_w,
+    store,
 ):
-    many = len(counts)
-    grad_refs = refs[:many]
-    sum_ref, quarter_ref = refs[many : many + 2]
-    got, far_x, far_y, own, theirs = refs[many + 2 : many + 7]
-    send_r, recv_r, send_w, recv_w, load, store = refs[many + 7 :]
     dp, plane, core, z = spot()
     sibling = (flip(dp, 1), z)
     xmate, ymate, _ = plane_mates(dp, z)
@@ -1087,38 +1073,54 @@
     ]
     for copy in first:
         copy.start()
-    wide, loads, base = [], [], 0
-    for grad, count in zip(grad_refs, counts, strict=True):
-        for k in range(count):
-            slot = base + k
-            wide.append(
-                push(grad.at[k, :, 1 - core], theirs.at[slot], send_w.at[slot], recv_w.at[slot], sibling)
-            )
-            loads.append(pltpu.make_async_copy(grad.at[k, :, core], own.at[slot], load.at[slot]))
-        base += count
-    for copy in wide + loads:
-        copy.start()
-    slabs = base
-    chips, depth, width = own.shape[1:]
-    unit = width // 4
+    slabs, chips, _, depth, units = made.shape
+    span = 2 * depth
+    unit = units // 4
+    tile = units // 3
+
+    def products(source, pairs):
+        def body(chip, carry):
+            spots = pl.ds(pl.multiple_of(chip * span, 128), span)
+            turned[...] = source[:, spots].T
+            for slot, value in pairs:
+                for step in range(3):
+                    columns = slice(step * tile, (step + 1) * tile)
+                    result = jnp.dot(turned[...], value[:, columns], preferred_element_type=F32)
+                    made[slot, chip, :, :, columns] = result.astype(BF).reshape(2, depth, tile)
+            return carry
+
+        lax.fori_loop(0, chips, body, 0)
+
+    def cross(slot):
+        return push(
+            made.at[slot, :, 1 - core],
+            theirs.at[slot],
+            send_w.at[slot],
+            recv_w.at[slot],
+            sibling,
+        )
+
+    def leave(slot, block):
+        return pltpu.make_async_copy(
+            made.at[slot, :, core, :, pl.ds(block * unit, unit)],
+            quarter_ref.at[block, slot],
+            store.at[slot, block],
+        )
 
     def core_sums(slot):
-        loads[slot].wait()
-        wide[slot].wait_recv()
+        cross(slot).wait_recv()
 
         def body(chip, carry):
-            own[slot, chip] = own[slot, chip] + theirs[slot, chip]
+            made[slot, chip, core] = made[slot, chip, core] + theirs[slot, chip]
             return carry
 
         lax.fori_loop(0, chips, body, 0)
         for block in range(4):
-            pltpu.make_async_copy(
-                own.at[slot, :, :, pl.ds(block * unit, unit)],
-                quarter_ref.at[block, slot],
-                store.at[slot, block],
-            ).start()
-
-    core_sums(0)
+            leave(slot, block).start()
+
+    products(left_ref, [(0, right_ref.at[0]), (1, right_ref.at[1])])
+    cross(0).start()
+    cross(1).start()
     first[0].wait_recv()
     far_x[...] = (part_ref[2, 0].astype(F32) + got[0].astype(F32)).astype(BF)
     upper = rows(far_x, 4, ymate)
@@ -1127,56 +1129,344 @@
     far_y[...] = (part_ref[1, 1].astype(F32) + got[1].astype(F32)).astype(BF)
     lower = rows(far_y, 5, xmate)
     lower.start()
-    for slot in range(1, slabs):
-        core_sums(slot)
+    products(other_ref, [(2, last_ref)])
+    cross(2).start()
+    core_sums(0)
+    core_sums(1)
     first[2].wait_recv()
     first[3].wait_recv()
     upper.wait_recv()
     sum_ref[0] = part_ref[0, 0].astype(F32) + got[2].astype(F32) + got[4].astype(F32)
     lower.wait_recv()
     sum_ref[1] = part_ref[0, 1].astype(F32) + got[3].astype(F32) + got[5].astype(F32)
-    for copy in first + wide + [upper, lower]:
+    core_sums(2)
+    for copy in first + [upper, lower]:
         copy.wait_send()
     for slot in range(slabs):
+        cross(slot).wait_send()
         for block in range(4):
-            pltpu.make_async_copy(
-                own.at[slot, :, :, pl.ds(block * unit, unit)],
-                quarter_ref.at[block, slot],
-                store.at[slot, block],
-            ).wait()
-
-
-def third_moves(part, grads):
+            leave(slot, block).wait()
+
+
+def third_moves(part, left, right, other, last):
     _, _, height, width = part.shape
-    counts = tuple(grad.shape[0] for grad in grads)
-    slabs = sum(counts)
-    depth, units = grads[0].shape[1] // 8, grads[0].shape[2]
+    tokens, units = last.shape
+    depth, slabs = width // 8, right.shape[0] + 1
     return pl.pallas_call(
-        functools.partial(third_kernel, counts=counts),
+        third_kernel,
         out_shape=[
             jax.ShapeDtypeStruct((2, height, width), F32),
             jax.ShapeDtypeStruct((4, slabs, 4, depth, units // 4), BF),
         ],
-        in_specs=near_specs(1) + any_specs(len(grads)),
+        in_specs=near_specs(5),
         out_specs=near_specs(1) + any_specs(1),
         scratch_shapes=[
             pltpu.VMEM((6, height, width), BF),
             pltpu.VMEM((height, width), BF),
             pltpu.VMEM((height, width), BF),
+            pltpu.VMEM((slabs, 4, 2, depth, units), BF),
             pltpu.VMEM((slabs, 4, depth, units), BF),
-            pltpu.VMEM((slabs, 4, depth, units), BF),
+            pltpu.VMEM((2 * depth, tokens), BF),
             dma(6),
             dma(6),
-            dma(slabs),
             dma(slabs),
             dma(slabs),
             dma(slabs, 4),
         ],
         compiler_params=pltpu.CompilerParams(
-            collective_id=4, has_side_effects=True, vmem_limit_bytes=ROOM
+            collective_id=4, has_side_effects=True, vmem_limit_bytes=60 << 20
         ),
         name="third_moves",
-    )(part, *[grad.reshape(grad.shape[0], 4, 2, depth, units) for grad in grads])
+    )(part, left, right, other, last)
+
+
+def turned_dot(source, chip, value):
+    span = source.shape[1] // 4
+    spots = pl.ds(pl.multiple_of(chip * span, 128), span)
+    product = lax.dot_general(
+        source[:, spots], value, (((0,), (0,)), ((), ())), preferred_element_type=F32
+    )
+    return product.astype(BF).reshape(2, span // 2, -1)
+
+
+def norm_parts(value):
+    centred = value - jnp.mean(value, axis=1, keepdims=True)
+    inverse = lax.rsqrt(jnp.mean(centred * centred, axis=1, keepdims=True) + EPSILON)
+    return centred * inverse, inverse
+
+
+def norm_grad(grad_out, scaled, inverse, gain):
+    grad_scaled = grad_out * gain
+    centre = jnp.mean(grad_scaled, axis=1, keepdims=True)
+    slope = jnp.mean(grad_scaled * scaled, axis=1, keepdims=True)
+    return inverse * (grad_scaled - centre - scaled * slope)
+
+
+def cross_kernel(*refs, tokens):
+    (
+        sums_ref,
+        part_ref,
+        after_ref,
+        stream_ref,
+        cot_ref,
+        keep_ref,
+        gain_ref,
+        two_ref,
+        query_ref,
+        pair_ref,
+        crossed_ref,
+        mixed_ref,
+        seq_ref,
+        conds_ref,
+        co_ref,
+        cq_ref,
+        cc_ref,
+        so_ref,
+    ) = refs[:18]
+    slabs_ref, grad_mixed, moved_ref, scaled_ref, inverse_ref, out_ref, gain_out, cond_out = refs[18:26]
+    held, grad, rounded, given, dquery, dpair, cond_mine, cond_got = refs[26:34]
+    got, far_x, far_y, half_mine, half_got, part_out, part_in = refs[34:41]
+    send_r, recv_r, send_e, recv_e, held_sem = refs[41:]
+    dp, plane, core, z = spot()
+    sibling = (flip(dp, 1), z)
+    xmate, ymate, _ = plane_mates(dp, z)
+    greet([sibling, xmate, ymate])
+    _, block, model_width = after_ref.shape
+    height = 4 * block
+    half = height // 2
+    tile = 256
+    wide = query_ref.shape[1]
+
+    def rows(source, slot, mate):
+        return push(source, got.at[slot], send_r.at[slot], recv_r.at[slot], mate)
+
+    first = [
+        rows(part_ref.at[3, 0], 0, xmate),
+        rows(part_ref.at[3, 1], 1, ymate),
+        rows(part_ref.at[1, 0], 2, xmate),
+        rows(part_ref.at[2, 1], 3, ymate),
+    ]
+    for copy in first:
+        copy.start()
+
+    def fetch(source, slot):
+        return pltpu.make_async_copy(source, held.at[slot], held_sem.at[slot])
+
+    fetch(co_ref, 0).start()
+    fetch(cq_ref, 1).start()
+
+    def exchange(slot, source, target):
+        return push(source, target, send_e.at[slot], recv_e.at[slot], sibling)
+
+    gain_three = jnp.zeros((1, model_width), F32)
+    for j in range(2):
+        scaled, inverse = norm_parts(after_ref[j])
+        value = norm_grad(sums_ref[j], scaled, inverse, gain_ref[2:3])
+        gain_three = gain_three + jnp.sum(sums_ref[j] * scaled, axis=0, keepdims=True)
+        half_mine[j] = value.astype(BF)
+        lines = pl.ds(pl.multiple_of((2 * core + j) * block, 8), block)
+        grad[lines, :] = keep_ref[lines, :1] * cot_ref[2 * core + j].astype(F32) + value
+    halves = exchange(0, half_mine, half_got)
+    halves.start()
+    for j in range(2):
+        scaled, inverse = norm_parts(seq_ref[2 * core + j].astype(F32))
+        scaled_ref[j] = scaled
+        inverse_ref[j] = jnp.broadcast_to(inverse, inverse_ref.shape[1:])
+    halves.wait()
+    for j in range(2):
+        lines = pl.ds(pl.multiple_of((2 * (1 - core) + j) * block, 8), block)
+        value = keep_ref[lines, :1] * cot_ref[2 * (1 - core) + j].astype(F32)
+        grad[lines, :] = value + half_got[j].astype(F32)
+
+    def round_rows(i, carry):
+        lines = pl.ds(pl.multiple_of(i * 32, 32), 32)
+        rounded[lines, :] = (keep_ref[lines, :1] * grad[lines, :]).astype(BF)
+        return carry
+
+    def project(slot, target):
+        def body(step, carry):
+            lines = pl.ds(pl.multiple_of(step // 3 * half, 16), half)
+            spots = pl.ds(pl.multiple_of(step % 3 * tile, tile), tile)
+            weight = held[slot, :, :, :, spots].reshape(model_width, tile)
+            value = jnp.dot(rounded[lines, :], weight, preferred_element_type=F32)
+            target[lines, spots] = value.astype(BF)
+            return carry
+
+        lax.fori_loop(0, 6, body, 0)
+
+    def slab_grad(index, source, value):
+        def body(chip, carry):
+            slabs_ref[index, chip // 2, chip % 2] = turned_dot(source, chip, value[...])
+            return carry
+
+        lax.fori_loop(0, 4, body, 0)
+
+    fetch(co_ref, 0).wait()
+    lax.fori_loop(0, height // 32, round_rows, 0)
+    project(0, given)
+    fetch(cc_ref, 0).start()
+
+    def heads(pair, carry):
+        lanes = pl.ds(pl.multiple_of(pair * 128, 128), 128)
+        line = lax.broadcasted_iota(jnp.int32, (pair_ref.shape[1], 1), 0)
+        grads = backward_pair(
+            query_ref[:, lanes],
+            pair_ref[0, :, lanes],
+            pair_ref[1, :, lanes],
+            given[:, lanes],
+            line < tokens,
+        )
+        dquery[:, lanes] = grads[0]
+        dpair[0, :, lanes] = grads[1]
+        dpair[1, :, lanes] = grads[2]
+        return carry
+
+    lax.fori_loop(0, wide // 128, heads, 0)
+    fetch(cq_ref, 1).wait()
+
+    def back(step, carry):
+        lines = pl.ds(pl.multiple_of(step // 4 * half, 16), half)
+        chip = step % 4
+        span = model_width // 4
+        value = lax.dot_general(
+            dquery[lines, :],
+            held[1, chip].reshape(span, wide),
+            (((1,), (1,)), ((), ())),
+            preferred_element_type=F32,
+        )
+        part_out[lines, pl.ds(pl.multiple_of(chip * span, 128), span)] = value.astype(BF)
+        return carry
+
+    lax.fori_loop(0, 8, back, 0)
+    parts = exchange(1, part_out, part_in)
+    parts.start()
+    fetch(so_ref, 1).start()
+    fetch(cc_ref, 0).wait()
+
+    part = held.shape[3] // 2
+    total = None
+    for which in range(2):
+        lines = slice(which * part, (which + 1) * part)
+        weight = held[0, :, :, lines, :].reshape(model_width // 2, wide)
+        value = lax.dot_general(
+            dpair[which], weight, (((1,), (1,)), ((), ())), preferred_element_type=F32
+        )
+        total = value if total is None else total + value
+        product = lax.dot_general(
+            conds_ref[z // 2], dpair[which], (((0,), (0,)), ((), ())), preferred_element_type=F32
+        )
+        slabs_ref[2, :, :, :, lines, :] = product.astype(BF).reshape(2, 2, 2, part, wide)
+    cond_mine[...] = total.astype(BF)
+    conds = exchange(2, cond_mine, cond_got)
+    conds.start()
+    slab_grad(0, rounded, crossed_ref)
+    first[0].wait_recv()
+    far_x[...] = (part_ref[2, 0].astype(F32) + got[0].astype(F32)).astype(BF)
+    upper = rows(far_x, 4, ymate)
+    upper.start()
+    first[1].wait_recv()
+    far_y[...] = (part_ref[1, 1].astype(F32) + got[1].astype(F32)).astype(BF)
+    lower = rows(far_y, 5, xmate)
+    lower.start()
+    parts.wait()
+    gain_row = lax.broadcasted_iota(jnp.int32, gain_out.shape, 0)
+    gain_out[...] = jnp.where(gain_row == 2, gain_three, 0.0)
+
+    def second_norm(i, carry):
+        lines = pl.ds(pl.multiple_of(i * 32, 32), 32)
+        scaled, inverse = norm_parts(stream_ref[lines, :])
+        value = part_out[lines, :].astype(F32) + part_in[lines, :].astype(F32)
+        total = grad[lines, :] + norm_grad(value, scaled, inverse, gain_ref[1:2])
+        grad[lines, :] = total
+        rounded[lines, :] = (keep_ref[lines, :1] * total).astype(BF)
+        return carry + jnp.sum(value * scaled, axis=0, keepdims=True)
+
+    gain_two = lax.fori_loop(0, height // 32, second_norm, jnp.zeros((1, model_width), F32))
+    gain_out[...] = jnp.where(gain_row == 1, 0.5 * gain_two, gain_out[...])
+    fetch(so_ref, 1).wait()
+    project(1, grad_mixed)
+    slab_grad(1, two_ref, dquery)
+    slab_grad(3, rounded, mixed_ref)
+    for j in range(2):
+        lines = pl.ds(pl.multiple_of((2 * core + j) * block, 8), block)
+        moved_ref[j] = grad[lines, :]
+    conds.wait()
+    cond_out[...] = (cond_mine[...].astype(F32) + cond_got[...].astype(F32)).astype(BF)
+    first[2].wait_recv()
+    first[3].wait_recv()
+    for j, copy in enumerate([upper, lower]):
+        copy.wait_recv()
+        value = part_ref[0, j].astype(F32) + got[2 + j].astype(F32) + got[4 + j].astype(F32)
+        lines = pl.ds(pl.multiple_of((2 * core + j) * block, 8), block)
+        keep = keep_ref[lines, :1]
+        out_ref[j] = (keep * (after_ref[j] + keep * value)).astype(BF)
+    for copy in first + [upper, lower]:
+        copy.wait_send()
+
+
+def cross_moves(sums, part, after, stream, cot, keep, gains, two, query, pair, crossed, mixed, seq, conds, weights, tokens):
+    _, block, model_width = after.shape
+    height, wide = query.shape
+    depth = model_width // 8
+    like = jax.ShapeDtypeStruct
+    slab = (4, 2, depth, wide)
+    return pl.pallas_call(
+        functools.partial(cross_kernel, tokens=tokens),
+        out_shape=[
+            like((4, 2, 2, 2, depth, wide), BF),
+            like(query.shape, BF),
+            like(after.shape, F32),
+            like(after.shape, F32),
+            like((2, block, 128), F32),
+            like(after.shape, BF),
+            like(gains.shape, F32),
+            like((pair.shape[1], model_width // 2), BF),
+        ],
+        in_specs=near_specs(14) + any_specs(4),
+        out_specs=near_specs(8),
+        scratch_shapes=[
+            pltpu.VMEM((2, *slab), BF),
+            pltpu.VMEM((height, model_width), F32),
+            pltpu.VMEM((height, model_width), BF),
+            pltpu.VMEM(query.shape, BF),
+            pltpu.VMEM(query.shape, BF),
+            pltpu.VMEM(pair.shape, BF),
+            pltpu.VMEM((pair.shape[1], model_width // 2), BF),
+            pltpu.VMEM((pair.shape[1], model_width // 2), BF),
+            pltpu.VMEM((6, block, model_width), BF),
+            pltpu.VMEM((block, model_width), BF),
+            pltpu.VMEM((block, model_width), BF),
+            pltpu.VMEM(after.shape, BF),
+            pltpu.VMEM(after.shape, BF),
+            pltpu.VMEM((height, model_width), BF),
+            pltpu.VMEM((height, model_width), BF),
+            dma(6),
+            dma(6),
+            dma(3),
+            dma(3),
+            dma(2),
+        ],
+        compiler_params=pltpu.CompilerParams(
+            collective_id=6, has_side_effects=True, vmem_limit_bytes=62 << 20
+        ),
+        name="cross_moves",
+    )(
+        sums,
+        part,
+        after,
+        stream,
+        cot,
+        keep,
+        gains,
+        two,
+        query,
+        pair,
+        crossed,
+        mixed,
+        seq,
+        conds,
+        *[weight.reshape(slab) for weight in weights],
+    )
 
 
 def backward_pair(queries, keys_in, values, grads, valid):
@@ -1206,7 +1496,7 @@
 
 def share_kernel(*refs, arrays):
     count = arrays + 3
-    grad_refs, refs = refs[:arrays], refs[arrays:]
+    grads_ref, refs = refs[0], refs[1:]
     (
         qkv_ref,
         mixed_ref,
@@ -1264,7 +1554,7 @@
         return pl.ds(pl.multiple_of(which * width, width), width)
 
     def strip(g, turn, bit):
-        grid = grad_refs[g].at[0] if g < arrays else made.at[g - arrays]
+        grid = grads_ref.at[g] if g < arrays else made.at[g - arrays]
         if turn == 0:
             return grid.at[:, bit, :, :, columns(order(turn))]
         return grid.at[bit, :, :, :, columns(order(turn))]
@@ -1404,12 +1694,11 @@
     lax.fori_loop(0, qkv_ref.shape[2] // 128, heads, 0)
 
     def weight_grads(i):
-        def body(block, carry):
-            value = jnp.dot(turned_ref[block], thirds[i], preferred_element_type=F32)
-            made[i, block // 4, block // 2 % 2, block % 2] = value.astype(BF)
+        def body(chip, carry):
+            made[i, chip // 2, chip % 2] = turned_dot(turned_ref, chip, thirds[i])
             return carry
 
-        lax.fori_loop(0, 8, body, 0)
+        lax.fori_loop(0, 4, body, 0)
         for turn in range(2):
             step_one(arrays + i, turn).start()
 
@@ -1576,9 +1865,8 @@
 
 
 def share_moves(grads, qkv, mixed, valid, turned, whole, stream, scaled, inverse, factor, output, gains, cond):
-    arrays = len(grads)
+    arrays, depth, width = grads.shape[0], grads.shape[4], grads.shape[5] // 2
     count = arrays + 3
-    depth, width = grads[0].shape[1] // 8, grads[0].shape[2] // 2
     many, parts, height, model_width = 2, *output.shape
     padded, columns = qkv.shape[1:]
     return pl.pallas_call(
@@ -1589,7 +1877,7 @@
             jax.ShapeDtypeStruct(gains.shape, F32),
             jax.ShapeDtypeStruct((2, *cond.shape), BF),
         ],
-        in_specs=any_specs(arrays) + near_specs(4) + any_specs(1) + near_specs(7),
+        in_specs=any_specs(1) + near_specs(4) + any_specs(1) + near_specs(7),
         out_specs=near_specs(1) + any_specs(1) + near_specs(1) + any_specs(1),
         scratch_shapes=[
             pltpu.VMEM((arrays, 2, 2, 2, depth, width), BF),
@@ -1632,7 +1920,7 @@
         ),
         name="share_moves",
     )(
-        *[grad.reshape(1, 2, 2, 2, depth, 2 * width) for grad in grads],
+        grads,
         qkv,
         mixed,
         valid,
@@ -1663,19 +1951,7 @@
     norm_gains,
 ):
     dp, z = lax.axis_index("dp"), lax.axis_index("tensor")
-    core, xbit, ybit = dp & 1, (dp >> 1) & 1, (dp >> 2) & 1
-    place = (core, xbit, ybit, z)
     model_width = inputs.shape[-1]
-    padded = inputs.shape[1] * 4
-    half_rows = padded // 2
-
-    def own_half(value):
-        return take(value.reshape(2, half_rows, -1), core, 0)
-
-    def both_halves(mine, theirs):
-        return ordered(core, mine, theirs, 0).reshape(padded, -1)
-
-    pair_sum = lambda value: value + swap(value.astype(BF), CORE).astype(F32)
 
     cc_depth = cross_context.shape[1]
     tokens = context.shape[1]
@@ -1693,49 +1969,27 @@
     wide = jnp.moveaxis(wide.reshape(3, depth, 4, units // 4), 2, 1)
     room = -tokens % 16
     cond = jnp.pad(take(context, z % 2, 0), ((0, room), (0, 0)))
-    apart = cond.reshape(-1, 8, 1, cc_depth)
-    none = jnp.zeros_like(apart)
-    spread_cond = jnp.stack(
-        [jnp.concatenate([apart, none], 2), jnp.concatenate([none, apart], 2)]
-    ).reshape(2, -1, model_width)
     weights, kept = weights_moves(
         narrow,
         wide,
         inputs,
         cotangent,
         jnp.broadcast_to(take(lengths, z % 2, 0), (8, 128)),
-        spread_cond,
+        cond,
         jnp.pad(norm_gains, ((0, 5), (0, 0))),
         ((0, 0), (0, 1), (0, 2), (1, 0), (2, 0), (3, 0), (4, 0)),
         tokens,
     )
     qkv_whole, so_whole, cq_whole, cc_whole, co_whole, gu_whole, down_whole = weights
-    so_whole, cq_whole, co_whole = so_whole[0], cq_whole[0], co_whole[0]
     down_whole = down_whole[0]
-    cc_whole = cc_whole[0].reshape(8, 2, cc_depth, -1)
-    cc_whole = jnp.moveaxis(cc_whole, 1, 0).reshape(2, 8 * cc_depth, -1)
     normed_one, qkv, mixed_one, stream, normed_two, cross_rows, cond_rows = kept[:7]
-    mixed_two, stream_half, rows_three, sequence, cot, grad_branch, row_keep, conds = kept[7:]
-    row_keep = row_keep[:, :1]
-    keep_half = own_half(row_keep)
-    context_valid = jnp.ones((tokens,), dtype=jnp.bool_)
-    cond = take(conds, z // 2, 0)[0].reshape(-1, 8, 2, cc_depth)[:tokens, :, 0]
-    cond = cond.reshape(tokens, -1)
-    cond_rows = cond_rows[:, :tokens]
-    stream_half = stream_half.reshape(half_rows, model_width)
+    mixed_two, after, rows_three, sequence, cot, grad_branch, row_keep, conds = kept[7:]
     rows_three = rows_three.reshape(-1, model_width)
     grad_branch = grad_branch.reshape(-1, model_width)
-    cot = cot.reshape(padded, model_width).astype(F32)
-    _, scaled_one, inverse_one = norm_rows(
-        sequence.reshape(padded, model_width).astype(F32), norm_gains[0]
-    )
-    _, scaled_two, inverse_two = norm_rows(stream, norm_gains[1])
-    _, scaled_three, inverse_three = norm_rows(stream_half, norm_gains[2])
     gate_rows = jnp.einsum("td,kde->kte", rows_three, gu_whole, preferred_element_type=F32)
     sigmoid_gate = jax.nn.sigmoid(gate_rows[0])
     hidden = (gate_rows[0] * sigmoid_gate * gate_rows[1]).astype(BF)
 
-    grad_stream = row_keep * cot
     grad_hidden = jnp.einsum("td,df->tf", grad_branch, down_whole, preferred_element_type=F32)
     grad_gate = (
         grad_hidden * gate_rows[1] * sigmoid_gate * (1.0 + gate_rows[0] * (1.0 - sigmoid_gate))
@@ -1743,66 +1997,48 @@
     grad_upper = grad_hidden * gate_rows[0] * sigmoid_gate
     grad_expand = jnp.stack([grad_gate, grad_upper]).astype(BF)
     partial_value = jnp.einsum("ktf,kdf->td", grad_expand, gu_whole, preferred_element_type=F32)
-    grad_down = jnp.einsum("td,tf->df", grad_branch, hidden, preferred_element_type=F32)
-    grad_gates = jnp.einsum("td,ktf->kdf", rows_three, grad_expand, preferred_element_type=F32)
     sums, wide_grads = third_moves(
         partial_value.astype(BF).reshape(4, 2, -1, model_width),
-        [grad_gates.astype(BF), grad_down.astype(BF)[None]],
-    )
-    grad_norm, gain_rows = norm_back(
-        sums.reshape(half_rows, model_width), scaled_three, inverse_three, norm_gains[2]
-    )
-    gain_three = jnp.sum(gain_rows, axis=0)
+        rows_three,
+        grad_expand,
+        grad_branch,
+        hidden,
+    )
     wide_grads = lax.psum_scatter(wide_grads, "tensor", scatter_dimension=0, tiled=False)
-    branch = jnp.einsum("tf,df->td", hidden, down_whole, preferred_element_type=F32)
-    stream_half = stream_half + keep_half * plane_sums(branch)
-    output = (keep_half * stream_half).astype(BF)
-
-    grad_stream = grad_stream + both_halves(grad_norm, swap(grad_norm.astype(BF), CORE).astype(F32))
-    grad_branch = (row_keep * grad_stream).astype(BF)
-    grad_mixed = jnp.einsum("td,de->te", grad_branch, co_whole, preferred_element_type=F32).astype(BF)
-    scores = masked_scores(split_heads(cross_rows), split_heads(cond_rows[0]), context_valid)
-    log_sums = jax.nn.logsumexp(scores, axis=-1)
-    grad_query, grad_key, grad_value = attend_backward(
-        (cross_rows, cond_rows[0], cond_rows[1], log_sums, grad_mixed, context_valid)
-    )
-    partial_value = jnp.einsum("te,de->td", grad_query, cq_whole, preferred_element_type=F32)
-    grad_norm, gain_rows = norm_back(
-        pair_sum(partial_value), scaled_two, inverse_two, norm_gains[1]
-    )
-    gain_two = 0.5 * jnp.sum(gain_rows, axis=0)
-    grad_merge = jnp.einsum("td,te->de", grad_branch, mixed_two, preferred_element_type=F32)
-    grad_cross = jnp.einsum("td,te->de", normed_two, grad_query, preferred_element_type=F32)
-    grad_pairs = jnp.stack([grad_key, grad_value])
-    grad_cc = jnp.einsum("sd,kse->kde", cond, grad_pairs, preferred_element_type=F32)
-    grad_cc = jnp.moveaxis(grad_cc.reshape(2, 8, cc_depth, -1), 0, 1).reshape(model_width, -1)
-    context_part = jnp.einsum("kse,kde->sd", grad_pairs, cc_whole, preferred_element_type=F32)
-    context_part = jnp.pad(pair_sum(context_part).astype(BF), ((0, room), (0, 0)))
-
-    grad_stream = grad_stream + grad_norm
-    grad_branch = (row_keep * grad_stream).astype(BF)
-    grad_mixed = jnp.einsum("td,de->te", grad_branch, so_whole, preferred_element_type=F32).astype(BF)
-    grad_after = jnp.einsum("td,te->de", grad_branch, mixed_one, preferred_element_type=F32)
-    gains = jnp.stack([jnp.zeros_like(gain_two), gain_two, gain_three])
+    branch = jnp.einsum("tf,df->td", hidden, down_whole, preferred_element_type=F32).astype(BF)
+
+    grads, grad_mixed, moved, scaled_one, inverse_one, output, gains, conds_grad = cross_moves(
+        sums,
+        branch.reshape(4, 2, -1, model_width),
+        after,
+        stream,
+        cot,
+        row_keep,
+        jnp.pad(norm_gains, ((0, 5), (0, 0))),
+        normed_two,
+        cross_rows,
+        cond_rows,
+        mixed_two,
+        mixed_one,
+        sequence,
+        conds,
+        [co_whole, cq_whole, cc_whole, so_whole],
+        tokens,
+    )
     shares, back, gains, conds = share_moves(
-        [
-            grad_merge.astype(BF)[None],
-            grad_cross.astype(BF)[None],
-            grad_cc.astype(BF)[None],
-            grad_after.astype(BF)[None],
-        ],
+        grads,
         qkv,
         grad_mixed,
-        jnp.broadcast_to(row_keep, (padded, 128)),
-        normed_one.T.reshape(8, -1, padded),
+        row_keep,
+        normed_one,
         qkv_whole,
-        own_half(grad_stream).reshape(2, -1, model_width),
-        own_half(scaled_one).reshape(2, -1, model_width),
-        jnp.broadcast_to(own_half(inverse_one), (half_rows, 128)).reshape(2, -1, 128),
+        moved,
+        scaled_one,
+        inverse_one,
         jnp.broadcast_to(norm_gains[0], (8, model_width)),
-        output.reshape(2, -1, model_width),
-        jnp.pad(gains, ((0, 5), (0, 0))),
-        context_part,
+        output,
+        gains,
+        conds_grad,
     )
     gains = lax.dynamic_slice_in_dim(gains[:3], dp * depth, depth, 1)
     shares = shares.astype(F32)

time: 750 us -> 645 us (0.86)
  Pallas kernels: 462 us -> 523 us
  matrix products: 106 us -> 55.3 us
  local copies, waits for them, and re-layouts: 64.8 us -> 18.9 us
  other arithmetic: 56.3 us -> 12.8 us
  waiting for transfers between devices: 29.6 us -> 11.9 us
    dot_general x15 -> x0, matrix products: 58 us -> none  [the longest x1 17.9 us: chip_shards(): jnp.einsum('td,ktf->kdf', rows_three, grad_expand, preferred_element_type...]
    pallas_call x1 -> x2, Pallas kernels: 33.6 us -> 89.7 us  [the longest x1 49.5 us: cross_moves(): pl.pallas_call(functools.partial(cross_kernel, tokens=tokens), out_shape=...]
    ppermute x7 -> x0, waiting for transfers between devices: 14.9 us -> none  [swap(): return lax.ppermute(value, 'dp', [(i, i ^ bit) for i in range(count)])]
    reduce_sum x9 -> x0, other arithmetic: 13.3 us -> none  [the longest x3 4.16 us: norm_rows(): centred = stream - jnp.mean(stream, axis=-1, keepdims=True)]
    convert_element_type x7 -> x0, other arithmetic: 12.4 us -> none  [the longest x1 3.64 us: chip_shards(): cot = cot.reshape(padded, model_width).astype(F32)]
    another operation x8 -> x0, local copies, waits for them, and re-layouts: 9.1 us -> none  [the longest x2 3.07 us: chip_shards(): jnp.stack([jnp.concatenate([apart, none], 2), jnp.concatenate([none, apar...]
  transfers between devices with their start and end apart: 9 -> 2, of which waited for: 3 -> 1; matrix products, arithmetic and copies ran while one was open for 16% -> 4% of each run, Pallas kernels for 25% -> 38%
where the time goes in v4:
time: 645 us; the launch traced here: 641 us
  Pallas kernels  523 us (81%)
  matrix products  55.3 us (9%)
  local copies, waits for them, and re-layouts  18.9 us (3%)
  between operations  14.6 us (2%)
  other arithmetic  12.8 us (2%)
  waiting for transfers between devices  11.9 us (2%)
    pallas_call x1, Pallas kernels, weights_moves(): pl.pallas_call(functools.partial(weights_kernel, groups=groups, wides=wid...  243 us
    pallas_call x1, Pallas kernels, share_moves(): pl.pallas_call(functools.partial(share_kernel, arrays=arrays), out_shape=...  191 us
    pallas_call x1, Pallas kernels, cross_moves(): pl.pallas_call(functools.partial(cross_kernel, tokens=tokens), out_shape=...  49.5 us
    pallas_call x1, Pallas kernels, third_moves(): pl.pallas_call(third_kernel, out_shape=[jax.ShapeDtypeStruct((2, height,...  40.2 us
    dot_general x1, matrix products, chip_shards(): jnp.einsum('td,kde->kte', rows_three, gu_whole, preferred_element_type=F32)  17.2 us
    dot_general x1, matrix products, chip_shards(): jnp.einsum('ktf,kdf->td', grad_expand, gu_whole, preferred_element_type=F32)  14.4 us
  transfers between devices with their start and end apart: 2, of which 1 were waited for; matrix products, arithmetic and copies ran while one was open for 4% of the time, Pallas kernels for 38%

profile of v4, /device:TPU:0, one launch (start us, length us, event | category | flops | bytes accessed | tf_op | source)
XLA Modules:
  0.0 640.5 jit_solution(1926255292166848466)
XLA Ops:
  7.2 0.0 copy-start
  7.2 0.0 reduce-scatter.2.cloned.1.call-start
  7.3 0.9 copy-done
  8.2 0.4 constant_dynamic-slice_fusion.1
  8.6 0.0 copy-start.5
  8.6 1.3 dynamic_slice.11
  10.0 1.8 convert.45
  11.8 0.0 copy-start.7
  11.8 0.1 copy.43
  11.9 0.0 copy-done.5
  11.9 0.0 copy-start.11
  11.9 0.1 convert_bitcast_fusion.1
  12.0 0.1 concatenate.15
  12.2 0.0 copy-start.8
  12.2 0.1 copy.31
  12.2 0.0 copy-start.9
  12.3 0.0 copy-start.10
  12.3 1.3 convert_dynamic-update-slice_fusion
  13.6 0.0 copy-done.7
  13.6 0.7 pad.9.cond_ref
  14.3 0.0 copy-done.11
  14.3 0.6 pad.10.gain_ref.refs_6_
  14.9 1.4 maximum_bitcast_fusion.units_ref
  16.3 0.0 copy-done.8
  16.4 0.0 copy-done.9
  16.4 0.0 copy-done.10
  16.5 0.0 copy-start.4
  16.5 1.3 broadcast_in_dim.22.size_ref
  17.8 0.0 copy-done.4
  17.8 243.1 %weights_moves.1 = (bf16[3,4,2,192,768]{4,3,2,1,0:T(8,128)(2,1)}, bf16[1,4,2,192,768]{4,3,2,1,0:T(8,128)(2,1)}, bf16[1,4,2,192,768]{4,3,2,1,0:T(8,128)(2,1)}, bf...) custom-call(bf16[7,192,384]{2,1,0:T(8,128)(2,1)} %copy-done.4, ...), custom_call_target="tpu_custom_call" | custom-call | tf_op jit(solution)/shard_map/weights_moves/pallas_call | solution.py:971
  260.9 0.0 copy-start.3
  260.9 0.0 copy-start.13
  260.9 17.2 %convolution_bitcast_fusion = f32[2,1088,1536]{2,1,0:T(8,128)} fusion(bf16[1088,1536,1]{1,0,2:T(8,128)(2,1)} %bitcast.132, bf16[2,1536,1536]{2,1,0:T(8,128)(2,1)} %bitcast.148), kind=kOutput, calls=%fused_computation | convolution fusion | flops 10267656192 | bytes 26148864 | tf_op jit(solution)/shard_map/td,kde->kte/dot_general | solution.py:1989
  278.1 0.0 copy-done.3
  278.1 0.0 copy-done.13
  278.1 12.1 %fusion.14 = (bf16[1,1088,1536]{2,1,0:T(8,128)(2,1)S(1)}, bf16[1,1088,1536]{2,1,0:T(8,128)(2,1)S(1)}, bf16[1088,1536]{1,0:T(8,128)(2,1)}) fusion(f32[2,1088,1536]{2,1,0:T(8,128)} %convolution_bitcast_fusion, bf16[1088,1536]{1,0:T(8,128)(2,1)S(1)} %bitcast.135, bf16[1536,1536]{1,0:T(8,128)(2,1)S(1)} %bitcast.151), kind=kOutput, calls=%fused_computation.25 | convolution fusion | flops 5160566784 | bytes 31457280 | tf_op jit(solution)/shard_map/td,df->tf/dot_general | solution.py:1993
  290.2 3.3 pad_maximum_fusion.right_ref
  293.5 14.4 %fusion = bf16[1088,1536]{1,0:T(8,128)(2,1)} fusion(bf16[2,1536,1536]{2,1,0:T(8,128)(2,1)} %bitcast.149, bf16[1,1088,1536]{2,1,0:T(8,128)(2,1)S(1)} %get-tuple-element.121, bf16[1,1088,1536]{2,1,0:T(8,128)(2,1)S(1)} %get-tuple-element.120), kind=kOutput, calls=%fused_computation.2 | convolution fusion | flops 10272669696 | bytes 19464192 | tf_op jit(solution)/shard_map/ktf,kdf->td/dot_general | solution.py:1999
  307.9 40.2 %third_moves.1 = (f32[2,136,1536]{2,1,0:T(8,128)}, bf16[4,3,4,192,384]{4,3,2,1,0:T(8,128)(2,1)}) custom-call(bf16[4,2,136,1536]{3,2,1,0:T(8,128)(2,1)} %bitcast.137, bf16[1088,1536]{1,0:T(8,128)(2,1)} %bitcast.133, bf16[2,1088,1536]{2,1,0:T(8,128)(2,1)} %pad_maximum_fusion.right_ref, bf16[1088,1536]{1,0:T(8,128)(2,1)} %bitcast.134, ...), custom_call_target="tpu_custom_call" | custom-call | tf_op jit(solution)/shard_map/third_moves/pallas_call | solution.py:1155
  348.1 0.0 reduce-scatter.2.cloned.1.call-update
  348.1 11.6 %convolution_convert_fusion = bf16[1088,1536]{1,0:T(8,128)(2,1)} fusion(bf16[1536,1536]{1,0:T(8,128)(2,1)} %bitcast.150, f32[2,1088,1536]{2,1,0:T(8,128)} %convolution_bitcast_fusion), kind=kOutput, calls=%fused_computation.3 | convolution fusion | flops 5145526272 | bytes 21430272 | tf_op jit(solution)/shard_map/tf,df->td/dot_general | solution.py:2008
  359.7 49.5 %cross_moves.1 = (bf16[4,2,2,2,192,768]{5,4,3,2,1,0:T(8,128)(2,1)}, bf16[544,768]{1,0:T(8,128)(2,1)}, f32[2,136,1536]{2,1,0:T(8,128)}, f32[2,136,1536]{2,1,0:T(8...) custom-call(f32[2,136,1536]{2,1,0:T(8,128)} %get-tuple-element.54.re, ...), custom_call_target="tpu_custom_call" | custom-call | tf_op jit(solution)/shard_map/cross_moves/pallas_call | solution.py:1413
  409.3 0.6 broadcast_in_dim.23.refs_9_
  409.9 190.7 %share_moves.1 = (bf16[7,192,384]{2,1,0:T(8,128)(2,1)}, bf16[2,2,136,1536]{3,2,1,0:T(8,128)(2,1)}, f32[8,1536]{1,0:T(8,128)}, bf16[2,144,768]{2,1,0:T(8,128)(2,1)}) custom-call(bf16[4,2,2,2,192,768]{5,4,3,2,1,0:T(8,128)(2,1)} %get-tuple-element.70.refs_0_, bf16[3,544,768]{2,1,0:T(8,128)(2,1)} %get-tuple-element.71.refs_1_, ...), custom_call_target="tpu_custom_call" | custom-call | tf_op jit(solution)/shard_map/share_moves/pallas_call | solution.py:1872
  600.6 0.0 reduce-scatter.2.cloned.1.call-done
  600.6 0.0 copy-start.2
  600.6 3.0 copy.33
  603.6 3.6 all-to-all-start
  607.2 1.4 convert_element_type.49
  608.6 1.0 slice.67
  609.6 0.7 slice.70
  610.4 0.1 slice_convert_fusion
  610.4 1.3 copy.36
  611.7 0.7 constant_dynamic-slice_fusion
  612.4 2.1 slice_bitcast_fusion.2
  614.5 3.0 bitcast_convert_fusion
  617.5 11.8 %all-to-all-done = bf16[3,4,192,384]{3,2,0,1:T(8,128)(2,1)S(1)} async-done(((bf16[3,4,192,384]{3,2,0,1:T(8,128)(2,1)}), bf16[3,4,192,384]{3,2,0,1:T(8,128)(2,1)S(1)}, u32[]{:S(2)}, u32[]{:S(2)}) %all-to-all-start) | async-done | bytes 1769504 | tf_op jit(solution)/shard_map/all_to_all | solution.py:2046
  629.3 0.3 convert_bitcast_fusion
  629.6 0.2 slice_bitcast_fusion
  629.8 0.1 slice.73
  629.9 0.0 copy-start.1
  629.9 1.7 copy.39
  631.6 0.8 copy.35
  632.4 1.1 copy.40
  (14 shorter events, 0.2 us)
Async XLA Ops:
  7.2 1.0 copy-start
  7.2 593.4 %reduce-scatter.2.cloned.1.call-start = ((), (), s32[]{:S(2)}) async-start(), calls=%async_computation.2 | async-start | bytes 8847360 | tf_op jit(solution)/shard_map/reduce_scatter | solution.py:2007
  8.6 3.3 copy-start.5
  11.8 1.8 copy-start.7
  11.9 2.4 copy-start.11
  12.2 4.2 copy-start.8
  12.2 4.1 copy-start.9
  12.3 4.2 copy-start.10
  16.5 1.3 copy-start.4
  260.9 17.2 %copy-start.3 = (bf16[4,2,136,1536]{3,2,1,0:T(8,128)(2,1)S(1)}, bf16[4,2,136,1536]{3,2,1,0:T(8,128)(2,1)}, u32[]{:S(2)}) copy-start(bf16[4,2,136,1536]{3,2,1,0:T(8,128)(2,1)} %get-tuple-element.49) | copy-start | bytes 10027012
  260.9 17.2 %copy-start.13 = (bf16[1,4,2,192,1536]{4,3,2,1,0:T(8,128)(2,1)S(1)}, bf16[1,4,2,192,1536]{4,3,2,1,0:T(8,128)(2,1)}, u32[]{:S(2)}) copy-start(bf16[1,4,2,192,1536]{4,3,2,1,0:T(8,128)(2,1)} %get-tuple-element.50) | copy-start | bytes 14155780
  600.6 6.6 %copy-start.2 = (bf16[7,192,384]{2,1,0:T(8,128)(2,1)S(1)}, bf16[7,192,384]{2,1,0:T(8,128)(2,1)}, u32[]{:S(2)}) copy-start(bf16[7,192,384]{2,1,0:T(8,128)(2,1)} %get-tuple-element.84) | copy-start | bytes 3096580
  603.6 25.7 %all-to-all-start = ((bf16[3,4,192,384]{3,2,0,1:T(8,128)(2,1)}), bf16[3,4,192,384]{3,2,0,1:T(8,128)(2,1)S(1)}, u32[]{:S(2)}, u32[]{:S(2)}) async-start(bf16[3,4,192,384]{3,2,0,1:T(8,128)(2,1)} %copy.33), calls=%async_computation.1 | async-start | bytes 3538944 | tf_op jit(solution)/shard_map/all_to_all | solution.py:2046
  607.2 3.2 copy-start.6
  608.6 3.1 copy-start.12
  629.9 3.6 copy-start.1
Sparse Core Ops, SparseCore 0:
  348.2 151.5 reduce-scatter.1
